TPU v7x, 512 devices: a whole 4x4x16 slice. The times are simulated.
512 devices in a mesh: beam: 64 (over z, x), trans: 8 (over y, core).
Axes of the slice: x: 4, y: 4, z: 16, core: 2. Of those that a mesh axis runs over, the one named last changes fastest.
Arguments:
- packets: float32 [2, 64, 4096, 128], P(None, 'trans', 'beam'), may hold values from -60 to 60
- kinetic_x: float32 [64, 64], replicated, as said below
- kinetic_y: float32 [64, 64], replicated, as said below
- element_kinetic: float32 [65, 65], replicated, as said below
- potential: float32 [64, 4096, 128], P('trans', 'beam'), may hold values from -0.4 to 0.4, as said below
Outputs:
- basis: float32 [10, 64, 4096, 128], P(None, 'trans', 'beam')
- rfactor: float32 [2, 10, 10], replicated
Inputs may be any that keep to these rules, and one draw needn't show every extreme that they name: kinetic_x is symmetric. kinetic_y is symmetric. element_kinetic is symmetric. `potential`: the absorbing part (the last 64 entries of each row) is not negative.
All inputs are finite; a program needn't handle non-finite values.
Results may differ from a plain program's by a relative error of at most 0.00075.
Values sent between devices are 32-bit elements; how exact they have to be, the bound alone decides.
No kernel may reach another device: no remote copies, remote signals or barrier semaphores. Data moves between devices by JAX's collectives and lax.ppermute only.
A program may use at most 64 MiB of HBM per device.

v0:
```python
import functools

import jax
import jax.numpy as jnp
from jax import lax
from jax.experimental import pallas as pl
from jax.experimental.pallas import tpu as pltpu
from jax.sharding import PartitionSpec as P

POWERS = 4
F32 = jnp.float32
BF16 = jnp.bfloat16
LIMIT = 48 * 1024 * 1024


def split(v):
    high = v.astype(BF16)
    return high, (v - high.astype(F32)).astype(BF16)


def passed(x, by):
    peers = lax.axis_size("beam")
    return lax.ppermute(x, "beam", [(i, i + by) for i in range(peers) if 0 <= i + by < peers])


def step_body(fix, with_prev, last, nx, nz, width, chip, scal, *refs):
    refs = list(refs)
    cur_ref = refs.pop(0)
    if fix:
        pin_ref, bin_ref = refs.pop(0), refs.pop(0)
    prev_ref = refs.pop(0) if with_prev else None
    pot_ref, kz_ref, kx_ref, wy_ref, rcol_ref, wvec_ref = refs[:6]
    refs = refs[6:]
    out_ref = refs.pop(0)
    if not last:
        first_ref, bridge_ref = refs.pop(0), refs.pop(0)
    if fix:
        rows_ref, col_ref = refs.pop(0), refs.pop(0)
    else:
        col_ref = cur_ref
    half = width // 2
    scale = 2.0 if with_prev else 1.0
    left = lax.broadcasted_iota(jnp.int32, (nz, width), 1) < half
    x_start = scal[0] if last else 0

    def fixed(x):
        at = pl.ds(pl.multiple_of(x * nz, nz), nz)
        u = cur_ref[at, :]
        if fix:
            u = u + rcol_ref[...] * pin_ref[pl.ds(x, 1), :]
            head = u[0:8] + jnp.where(
                lax.broadcasted_iota(jnp.int32, (8, width), 0) == 0, bin_ref[pl.ds(x, 1), :], 0.0
            )
            u = jnp.concatenate([head, u[8:]], axis=0)
            col_ref[at, :] = u
        return u

    def local_pair(x0):
        us = []
        for q in range(2):
            if last:
                us.append(col_ref[pl.ds(pl.multiple_of((x_start + x0 + q) * nz, nz), nz), :])
            else:
                us.append(fixed(x0 + q))
        parts = [split(u) for u in us]
        highs = jnp.concatenate([p[0] for p in parts], axis=1)
        lows = jnp.concatenate([p[1] for p in parts], axis=1)
        along_z = jnp.dot(
            kz_ref[...],
            jnp.concatenate([highs, lows, highs], axis=0),
            preferred_element_type=F32,
        )
        along_y = jnp.dot(
            jnp.concatenate([jnp.concatenate(p, axis=1) for p in parts], axis=0),
            wy_ref[...],
            preferred_element_type=F32,
        )
        for q in range(2):
            u = us[q]
            x = x0 + q
            at = pl.ds(pl.multiple_of((x_start + x) * nz, nz), nz)
            to = pl.ds(pl.multiple_of(x * nz, nz), nz)
            pv = pot_ref[at, :]
            pr = pltpu.roll(pv, half, 1)
            optical = jnp.where(left, pv, pr) * u + jnp.where(left, pr, -pv) * pltpu.roll(u, half, 1)
            ay = along_y[q * nz : (q + 1) * nz]
            new = (
                along_z[:, q * width : (q + 1) * width]
                + ay[:, :width]
                + ay[:, width:]
                + scale * optical
            )
            if with_prev:
                new = new - prev_ref[at, :]
            out_ref[to, :] = new

    if last:

        def fix_some(i, carry):
            for q in range(8):
                fixed(i * 8 + q)
            return carry

        lax.fori_loop(0, nx // 8, fix_some, 0)
    out_x = chip if last else nx
    pairs = 4

    def local_some(i, carry):
        for q in range(pairs):
            local_pair((i * pairs + q) * 2)
        return carry

    lax.fori_loop(0, out_x // (2 * pairs), local_some, 0)
    if fix:
        rows_ref[...] = col_ref[pl.ds(pl.multiple_of(scal[0] * nz, nz), chip * nz), :]

    def across_pair(z0, bridge):
        us = [col_ref[pl.ds(z0 + q, nx, stride=nz), :] for q in range(2)]
        parts = [split(u) for u in us]
        highs = jnp.concatenate([p[0] for p in parts], axis=1)
        lows = jnp.concatenate([p[1] for p in parts], axis=1)
        along_x = jnp.dot(
            kx_ref[...],
            jnp.concatenate([highs, lows, highs], axis=0),
            preferred_element_type=F32,
        )
        for q in range(2):
            at = pl.ds(z0 + q, out_x, stride=nz)
            new = out_ref[at, :] + along_x[:, q * width : (q + 1) * width]
            out_ref[at, :] = new
            if not last:
                bridge = bridge + wvec_ref[pl.ds(z0 + q, 1), :] * new
        return bridge

    def across_some(i, bridge):
        for q in range(pairs):
            bridge = across_pair((i * pairs + q) * 2, bridge)
        return bridge

    bridge = jnp.zeros((out_x, width), F32)
    bridge = lax.fori_loop(0, nz // (2 * pairs), across_some, bridge)
    if not last:
        bridge_ref[...] = bridge
        first_ref[...] = out_ref[pl.ds(0, nx, stride=nz), :]


def vm():
    return pl.BlockSpec(memory_space=pltpu.VMEM)


def in_vmem(*shape):
    return pltpu.VMEM(shape, F32)


def step(scal, cur, halo, prev, pot, kz, kx, wy, rcol, wvec, nx, nz, chip, last):
    fix, with_prev = halo is not None, prev is not None
    width = cur.shape[-1]
    ins = [cur] + (list(halo) if fix else []) + ([prev] if with_prev else [])
    ins += [pot, kz, kx, wy, rcol, wvec]
    outs = [in_vmem((chip if last else nx) * nz, width)]
    if not last:
        outs += [in_vmem(nx, width), in_vmem(nx, width)]
    if fix:
        outs += [in_vmem(chip * nz, width)]
    scratch = []
    if fix:
        if last:
            scratch = [pltpu.VMEM((nx * nz, width), F32)]
        else:
            outs += [in_vmem(nx * nz, width)]
    body = functools.partial(step_body, fix, with_prev, last, nx, nz, width, chip)
    return pl.pallas_call(
        body,
        out_shape=outs,
        in_specs=[pl.BlockSpec(memory_space=pltpu.SMEM)] + [vm()] * len(ins),
        out_specs=[vm()] * len(outs),
        scratch_shapes=scratch,
        compiler_params=pltpu.CompilerParams(vmem_limit_bytes=LIMIT),
        cost_estimate=pl.CostEstimate(flops=4 * 10**9, bytes_accessed=8 * 10**6, transcendentals=0),
        name="step",
    )(scal, *ins)


def finish_body(nz, rows, scal, last_ref, pin_ref, bin_ref, rcol_ref, *refs):
    cols = refs[: POWERS - 1]
    keep_ref, send_ref = refs[POWERS - 1 :]
    core = scal[1]
    size = rows * nz
    width = last_ref.shape[-1]
    top = lax.broadcasted_iota(jnp.int32, (8, width), 0) == 0
    for ref, where in ((keep_ref, core), (send_ref, 1 - core)):
        at = pl.ds(pl.multiple_of(where * size, size), size)
        for k in range(POWERS - 1):
            ref[k] = cols[k][at, :]
        for r in range(rows):
            x = where * rows + r
            u = last_ref[pl.ds(pl.multiple_of(x * nz, nz), nz), :]
            u = u + rcol_ref[...] * pin_ref[pl.ds(x, 1), :]
            head = u[0:8] + jnp.where(top, bin_ref[pl.ds(x, 1), :], 0.0)
            ref[POWERS - 1, r * nz : (r + 1) * nz, :] = jnp.concatenate([head, u[8:]], axis=0)


def gram_body(scal, packets_ref, keep_ref, recv_ref, cols_ref, gram_ref, acc_ref):
    core = scal[1]
    ncol, size, width = cols_ref.shape
    npow = ncol // 2
    half = width // 2
    cols_ref[0] = packets_ref[0]
    cols_ref[npow] = packets_ref[1]
    for k in range(npow - 1):
        cols_ref[core * npow + 1 + k] = keep_ref[k]
        cols_ref[(1 - core) * npow + 1 + k] = recv_ref[k]
    acc_ref[...] = jnp.zeros_like(acc_ref)
    sign = jnp.where(lax.broadcasted_iota(jnp.int32, (8, width), 1) < half, 1.0, -1.0)
    first, second = list(range(npow)), list(range(npow, ncol))
    groups = [
        [(a, b) for a in first for b in first if a <= b],
        [(a, b) for a in second for b in second if a <= b],
        [(a, b) for a in first for b in second[:3]],
        [(a, b) for a in first for b in second[3:]],
    ]
    for pairs in groups:
        used = sorted({c for pair in pairs for c in pair})
        turned = sorted({b for a, b in pairs if a != b})

        def chunk(i, sums, pairs=pairs, used=used, turned=turned):
            sums = list(sums)
            at = pl.ds(pl.multiple_of(i * 8, 8), 8)
            v = {c: cols_ref[c, at, :] for c in used}
            t = {c: pltpu.roll(v[c], half, 1) for c in turned}
            n = 0
            for a, b in pairs:
                sums[n] = sums[n] + v[a] * v[b]
                n += 1
                if a != b:
                    sums[n] = sums[n] + v[a] * t[b]
                    n += 1
            return tuple(sums)

        count = sum(1 if a == b else 2 for a, b in pairs)
        sums = lax.fori_loop(
            0, size // 8, chunk, tuple(jnp.zeros((8, width), F32) for _ in range(count)), unroll=2
        )
        n = 0
        for a, b in pairs:
            acc_ref[a * ncol + b : a * ncol + b + 1, :] = jnp.sum(sums[n], axis=0, keepdims=True)
            n += 1
            if a != b:
                acc_ref[b * ncol + a : b * ncol + a + 1, :] = jnp.sum(
                    sums[n] * sign, axis=0, keepdims=True
                )
                n += 1
    row = jnp.sum(acc_ref[...].T, axis=0, keepdims=True)
    gram_ref[...] = jnp.broadcast_to(row[None], gram_ref.shape)


def basis_body(cells, gram_ref, cols_ref, basis_ref, factor_ref, coef_ref):
    ncol, _, size, width = cols_ref.shape
    half = width // 2

    @pl.when(pl.program_id(0) == 0)
    def _():
        row = jnp.sum(gram_ref[...], axis=0) * (1.0 / cells)
        r = lax.broadcasted_iota(jnp.int32, (16, width), 0)
        c = lax.broadcasted_iota(jnp.int32, (16, width), 1)
        packed = jnp.zeros((16, width), F32)
        for j in range(ncol):
            moved = row if j == 0 else pltpu.roll(row, width - ncol * j, 1)
            packed = jnp.where(r == j, moved, packed)
        turned = jnp.concatenate([packed, jnp.zeros((width - 16, width), F32)], axis=0).T[:16]
        inside = (r < ncol) & (c < ncol)
        re = jnp.where(inside, jnp.where(r <= c, packed, turned), 0.0)
        im = jnp.where(inside & (r != c), jnp.where(r < c, turned, -packed), 0.0)
        re = jnp.where(c == r + 16, 1.0, re)
        up_re = jnp.zeros((16, width), F32)
        up_im = jnp.zeros((16, width), F32)
        for j in range(ncol):
            pivot = jnp.sqrt(re[j : j + 1, j : j + 1])
            inverse = 1.0 / pivot
            row_re = re[j : j + 1, :] * inverse
            row_im = im[j : j + 1, :] * inverse
            col_re = re[:, j : j + 1] * inverse
            col_im = im[:, j : j + 1] * inverse
            up_re = jnp.where(r == j, row_re, up_re)
            up_im = jnp.where(r == j, row_im, up_im)
            below = r > j
            re = re - jnp.where(below, col_re * row_re - col_im * row_im, 0.0)
            im = im - jnp.where(below, col_re * row_im + col_im * row_re, 0.0)
        keep = (c >= r) & (c < ncol)
        factor_ref[0] = jnp.where(keep, up_re, 0.0)
        factor_ref[1] = jnp.where(keep & (c > r), up_im, 0.0)
        sign = jnp.where(lax.broadcasted_iota(jnp.int32, (8, width), 1) < half, 1.0, -1.0)
        for k in range(ncol):
            for i in range(k + 1):
                coef_ref[0, k * ncol + i] = jnp.broadcast_to(up_re[k : k + 1, 16 + i : 17 + i], (8, width))
                coef_ref[1, k * ncol + i] = (
                    jnp.broadcast_to(up_im[k : k + 1, 16 + i : 17 + i], (8, width)) * sign
                )

    group = 4
    for start in range(0, size, 8 * group):
        slots = [slice(start + 8 * g, start + 8 * g + 8) for g in range(group)]
        v = [[cols_ref[i, 0, s, :] for s in slots] for i in range(ncol)]
        t = [[pltpu.roll(x, half, 1) for x in xs] for xs in v]
        for k in range(ncol):
            total = [None] * group
            for i in range(k + 1):
                re = coef_ref[0, k * ncol + i]
                im = coef_ref[1, k * ncol + i]
                for g in range(group):
                    term = re * v[i][g]
                    if i < k:
                        term = term + im * t[i][g]
                    total[g] = term if total[g] is None else total[g] + term
            for g in range(group):
                basis_ref[k, 0, slots[g], :] = total[g]


def shards(packets, kinetic_x, kinetic_y, element_kinetic, potential):
    npack, rows, nz, width = packets.shape
    trans = lax.axis_size("trans")
    nx = rows * trans
    ncol = npack * (POWERS + 1)
    me = lax.axis_index("trans")
    core = me % 2
    chip = 2 * rows
    scal = jnp.stack([(me // 2) * chip, core]).astype(jnp.int32)

    pot = lax.all_gather(potential, "trans", axis=0, tiled=True).reshape(nx * nz, width)
    sent = jnp.broadcast_to(packets[None], (trans // 2,) + packets.shape)
    sent = sent.reshape((trans, rows, nz, width))
    cur = lax.all_to_all(sent, "trans", 0, 0, tiled=True).reshape(nx * nz, width)

    corner = element_kinetic[nz, nz] * (lax.axis_index("beam") > 0).astype(F32)
    kz = element_kinetic[:nz, :nz].at[0, 0].add(corner)
    wrow = element_kinetic[nz, :nz]
    rcol = element_kinetic[:nz, nz]

    def parts_of(k):
        high = lax.reduce_precision(k, 8, 7)
        return high.astype(BF16), (k - high).astype(BF16)

    def left_weights(k):
        high, low = parts_of(k)
        return jnp.concatenate([high, high, low], axis=1)

    ky_high, ky_low = parts_of(jnp.kron(jnp.eye(2, dtype=F32), kinetic_y).T)
    wy = jnp.concatenate(
        [
            jnp.concatenate([ky_high, ky_low], axis=1),
            jnp.concatenate([ky_high, jnp.zeros_like(ky_low)], axis=1),
        ],
        axis=0,
    )
    kz1, kx1 = left_weights(kz), left_weights(kinetic_x)
    kz2, kx2, wy2 = kz1 * 2, kx1 * 2, wy * 2
    kx_last = lax.dynamic_slice_in_dim(kx2, scal[0], chip, 0)
    rcol1 = jnp.broadcast_to(rcol[:, None], (nz, width))
    rcol2 = rcol1 * 2.0
    wvec = jnp.broadcast_to(wrow[:, None], (nz, width))

    def halo(first, bridge, pin, bin_, scale):
        if pin is not None:
            bridge = bridge + (scale * jnp.dot(wrow, rcol, precision="highest")) * pin
            bridge = bridge + (scale * wrow[0]) * bin_
            first = first + (scale * rcol[0]) * pin + scale * bin_
        return passed(first, -1), passed(bridge, 1)

    whole = cur.reshape(nx, nz, width)
    halos = [halo(whole[:, 0], jnp.sum(whole * wvec, axis=1), None, None, 1.0)]
    columns = []
    prev = None
    local, first, bridge = step(
        scal, cur, None, None, pot, kz1, kx1, wy, rcol1, wvec, nx, nz, chip, False
    )
    prev = cur
    for k in range(1, POWERS):
        scale = 1.0 if k == 1 else 2.0
        pin, bin_ = halos[-1]
        fresh = halo(first, bridge, pin, bin_, scale)
        last = k == POWERS - 1
        got = step(
            scal,
            local,
            (pin, scale * bin_),
            prev,
            pot,
            kz2,
            kx_last if last else kx2,
            wy2,
            rcol1 if k == 1 else rcol2,
            wvec,
            nx,
            nz,
            chip,
            last,
        )
        if last:
            local, col_rows = got
        else:
            prev_next = got[4]
            local, first, bridge, col_rows = got[:4]
            prev = prev_next
        columns.append(col_rows)
        halos.append(fresh)
    pin, bin_ = halos[-1]
    pin = lax.dynamic_slice_in_dim(pin, scal[0], chip, 0)
    bin_ = lax.dynamic_slice_in_dim(2.0 * bin_, scal[0], chip, 0)
    size = rows * nz
    keep, send = pl.pallas_call(
        functools.partial(finish_body, nz, rows),
        out_shape=[in_vmem(POWERS, size, width)] * 2,
        in_specs=[pl.BlockSpec(memory_space=pltpu.SMEM)] + [vm()] * (4 + POWERS - 1),
        out_specs=[vm()] * 2,
        compiler_params=pltpu.CompilerParams(vmem_limit_bytes=LIMIT),
        name="finish",
    )(scal, local, pin, bin_, rcol2, *columns)
    recv = lax.ppermute(send, "trans", [(i, i ^ 1) for i in range(trans)])
    cols, gram = pl.pallas_call(
        gram_body,
        out_shape=[in_vmem(ncol, size, width), in_vmem(trans, 1, width)],
        in_specs=[pl.BlockSpec(memory_space=pltpu.SMEM)] + [vm()] * 3,
        out_specs=[vm()] * 2,
        scratch_shapes=[pltpu.VMEM((128, width), F32)],
        compiler_params=pltpu.CompilerParams(vmem_limit_bytes=LIMIT),
        name="gram",
    )(scal, packets.reshape(npack, size, width), keep, recv)
    beam = lax.axis_size("beam")
    gram = jnp.sum(lax.all_to_all(gram, "trans", 0, 0, tiled=True), axis=0, keepdims=True)
    gram = lax.all_to_all(jnp.broadcast_to(gram, (beam, 1, width)), "beam", 0, 0, tiled=True)
    cells = float(nx * (width // 2) * nz * beam)
    basis, factor = pl.pallas_call(
        functools.partial(basis_body, cells),
        grid=(rows,),
        out_shape=[
            jax.ShapeDtypeStruct((ncol, rows, nz, width), F32),
            jax.ShapeDtypeStruct((2, 16, width), F32),
        ],
        in_specs=[
            pl.BlockSpec((beam, 1, width), lambda i: (0, 0, 0)),
            pl.BlockSpec((ncol, 1, nz, width), lambda i: (0, i, 0, 0)),
        ],
        out_specs=[
            pl.BlockSpec((ncol, 1, nz, width), lambda i: (0, i, 0, 0)),
            pl.BlockSpec((2, 16, width), lambda i: (0, 0, 0)),
        ],
        scratch_shapes=[pltpu.VMEM((2, ncol * ncol, 8, width), F32)],
        compiler_params=pltpu.CompilerParams(vmem_limit_bytes=LIMIT),
        name="basis",
    )(gram, cols.reshape(ncol, rows, nz, width))
    return basis, factor[:, :ncol, :ncol]


def solution(mesh):
    in_specs = (P(None, "trans", "beam", None), P(), P(), P(), P("trans", "beam", None))
    out_specs = (P(None, "trans", "beam", None), P())
    return jax.shard_map(shards, mesh=mesh, in_specs=in_specs, out_specs=out_specs, check_vma=False)
```

profile of v0, /device:TPU:1, one launch (start us, length us, event | category | flops | bytes accessed | tf_op | source)
XLA Modules:
  0.0 192.8 jit_solution(9094282579736152562)
XLA Ops:
  7.9 1.4 copy.15
  9.2 1.5 broadcast_in_dim.18
  10.7 10.5 %all-to-all-start = ((f32[8,8,64,128]{3,1,2,0:T(8,128)}), f32[8,8,64,128]{3,1,2,0:T(8,128)S(1)}, u32[]{:S(2)}, u32[]{:S(2)}) async-start(f32[8,8,64,128]{3,1,2,0:T(8,128)} %bitcast.32), calls=%async_computation | async-start | bytes 4194304 | tf_op jit(solution)/shard_map/all_to_all | solution.py:332
  26.5 29.5 %all-to-all-done = f32[8,8,64,128]{3,1,2,0:T(8,128)S(1)} async-done(((f32[8,8,64,128]{3,1,2,0:T(8,128)}), f32[8,8,64,128]{3,1,2,0:T(8,128)S(1)}, u32[]{:S(2)}, u32[]{:S(2)}) %all-to-all-start) | async-done | bytes 2097184 | tf_op jit(solution)/shard_map/all_to_all | solution.py:332
  57.8 1.3 collective-permute-start
  59.1 2.0 %copy.16 = f32[8,8,64,128]{3,2,1,0:T(8,128)S(1)} copy(f32[8,8,64,128]{3,1,2,0:T(8,128)} %copy-done.5) | data formatting | bytes 4194304 | tf_op jit(solution)/shard_map/all_to_all | solution.py:332
  61.3 8.5 %step.4 = (f32[4096,128]{1,0:T(8,128)S(1)}, f32[64,128]{1,0:T(8,128)S(1)}, f32[64,128]{1,0:T(8,128)S(1)}) custom-call(s32[2]{0:T(128)S(1)} %pad_add_fusion.scal, f32[4096,128]{1,0:T(8,128)S(1)} %bitcast.28, f32[4096,128]{1,0:T(8,128)} %bitcast.35, bf16[64,192]{1,0:T(8,128)(2,1)S(1)} %get-tuple-element.88.refs_2_, ...), custom_call_target="tpu_custom_call" | custom-call | flops 4000000000 | bytes 8000000 | tf_op jit(solution)/shard_map/step/pallas_call | solution.py:172
  69.8 1.3 copy-done.4
  71.1 1.9 multiply_add_fusion.2
  73.0 1.3 collective-permute-start.2
  74.3 4.6 %collective-permute-start.3 = (f32[64,128]{1,0:T(8,128)S(1)}, f32[64,128]{1,0:T(8,128)S(1)}, u32[]{:S(2)}, u32[]{:S(2)}) collective-permute-start(f32[64,128]{1,0:T(8,128)S(1)} %get-tuple-element.66), channel_id=1, source_target_pairs={{0,8},{8,16},{16,24},{24,32},{32,40},{40,48},{48,56},{56,64},{64,7... | collective-permute-start | bytes 98312 | tf_op jit(solution)/shard_map/ppermute | solution.py:23
  78.9 9.2 %step.5 = (f32[4096,128]{1,0:T(8,128)S(1)}, f32[64,128]{1,0:T(8,128)S(1)}, f32[64,128]{1,0:T(8,128)S(1)}, f32[1024,128]{1,0:T(8,128)S(1)}, f32[4096,128]{1,0:T(8,128)S(1)}) custom-call(s32[2]{0:T(128)S(1)} %pad_add_fusion.scal, f32[4096,128]{1,0:T(8,128)} %copy-done.4, f32[64,128]{1,0:T(8,128)S(1)} %collective-permute-done.refs_1_, ...), custom_call_target="tpu_custom_call" | custom-call | flops 4000000000 | bytes 8000000 | tf_op jit(solution)/shard_map/step/pallas_call | solution.py:172
  88.2 1.3 copy-done.2
  89.5 1.3 copy-done.3
  92.1 4.0 %collective-permute-start.5 = (f32[64,128]{1,0:T(8,128)S(1)}, f32[64,128]{1,0:T(8,128)S(1)}, u32[]{:S(2)}, u32[]{:S(2)}) collective-permute-start(f32[64,128]{1,0:T(8,128)S(1)} %get-tuple-element.64), channel_id=1, source_target_pairs={{0,8},{8,16},{16,24},{24,32},{32,40},{40,48},{48,56},{56,64},{64,7... | collective-permute-start | bytes 98312 | tf_op jit(solution)/shard_map/ppermute | solution.py:23
  96.2 9.2 %step.6 = (f32[4096,128]{1,0:T(8,128)S(1)}, f32[64,128]{1,0:T(8,128)S(1)}, f32[64,128]{1,0:T(8,128)S(1)}, f32[1024,128]{1,0:T(8,128)S(1)}, f32[4096,128]{1,0:T(8,128)S(1)}) custom-call(s32[2]{0:T(128)S(1)} %pad_add_fusion.scal, f32[4096,128]{1,0:T(8,128)} %copy-done.2, f32[64,128]{1,0:T(8,128)S(1)} %collective-permute-done.2.refs_1_, ...), custom_call_target="tpu_custom_call" | custom-call | flops 4000000000 | bytes 8000000 | tf_op jit(solution)/shard_map/step/pallas_call | solution.py:172
  106.7 4.0 %collective-permute-start.7 = (f32[64,128]{1,0:T(8,128)S(1)}, f32[64,128]{1,0:T(8,128)S(1)}, u32[]{:S(2)}, u32[]{:S(2)}) collective-permute-start(f32[64,128]{1,0:T(8,128)S(1)} %get-tuple-element.62), channel_id=1, source_target_pairs={{0,8},{8,16},{16,24},{24,32},{32,40},{40,48},{48,56},{56,64},{64,7... | collective-permute-start | bytes 98312 | tf_op jit(solution)/shard_map/ppermute | solution.py:23
  110.7 4.8 %step.7 = (f32[1024,128]{1,0:T(8,128)S(1)}, f32[1024,128]{1,0:T(8,128)S(1)}) custom-call(s32[2]{0:T(128)S(1)} %pad_add_fusion.scal, f32[4096,128]{1,0:T(8,128)S(1)} %get-tuple-element.40.refs_0_, f32[64,128]{1,0:T(8,128)S(1)} %collective-permute-done.4.refs_1_, f32[64,128]{1,0:T(8,128)S(1)} %get-tuple-element.76.refs_2_, ...), custom_call_target="tpu_custom_call" | custom-call | flops 4000000000 | bytes 8000000 | tf_op jit(solution)/shard_map/step/pallas_call | solution.py:172
  116.3 4.5 %collective-permute-start.8 = (f32[4,512,128]{2,1,0:T(8,128)S(1)}, f32[4,512,128]{2,1,0:T(8,128)S(1)}, u32[]{:S(2)}, u32[]{:S(2)}) collective-permute-start(f32[4,512,128]{2,1,0:T(8,128)S(1)} %get-tuple-element.51), channel_id=1, source_target_pairs={{0,1},{1,0},{2,3},{3,2},{4,5},{5,4},{6,7},{7,6},{8,9},{9,8},{10,11... | collective-permute-start | bytes 3145736 | tf_op jit(solution)/shard_map/ppermute | solution.py:418
  120.8 2.3 %collective-permute-done.8.recv_ref = f32[4,512,128]{2,1,0:T(8,128)S(1)} collective-permute-done((f32[4,512,128]{2,1,0:T(8,128)S(1)}, f32[4,512,128]{2,1,0:T(8,128)S(1)}, u32[]{:S(2)}, u32[]{:S(2)}) %collective-permute-start.8) | collective-permute-done | bytes 1048608 | tf_op jit(solution)/shard_map/ppermute | solution.py:418
  123.1 11.2 %gram.1 = (f32[10,512,128]{2,1,0:T(8,128)S(1)}, f32[8,1,128]{2,1,0:T(1,128)S(1)}) custom-call(s32[2]{0:T(128)S(1)} %pad_add_fusion.scal, f32[2,512,128]{2,1,0:T(8,128)S(1)} %bitcast.30, f32[4,512,128]{2,1,0:T(8,128)S(1)} %get-tuple-element.50.keep_ref, f32[4,512,128]{2,1,0:T(8,128)S(1)} %collective-permute-done.8.recv_ref), custom_call_target="tpu_custom_call" | custom-call | tf_op jit(solution)/shard_map/gram/pallas_call | solution.py:419
  134.2 7.3 %all_to_all.15 = f32[8,1,128]{2,1,0:T(1,128)S(1)} all-to-all(f32[8,1,128]{2,1,0:T(1,128)S(1)} %get-tuple-element.52), channel_id=1, replica_groups=mesh['beam'=64,'trans'=8] {'trans'}, dimensions={0} | all-to-all | bytes 8192 | tf_op jit(solution)/shard_map/all_to_all | solution.py:429
  141.6 38.1 %all_to_all.16.gram_ref = f32[64,1,128]{2,1,0:T(1,128)S(1)} all-to-all(f32[64,1,128]{2,1,0:T(1,128)S(1)} %broadcast_in_dim.39), channel_id=1, replica_groups=mesh['beam'=64,'trans'=8] {'beam'}, dimensions={0} | all-to-all | bytes 65536 | tf_op jit(solution)/shard_map/all_to_all | solution.py:430
  179.7 5.7 %basis.1 = (f32[10,8,64,128]{3,2,1,0:T(8,128)}, f32[2,16,128]{2,1,0:T(8,128)S(1)}) custom-call(f32[64,1,128]{2,1,0:T(1,128)S(1)} %all_to_all.16.gram_ref, f32[10,8,64,128]{3,2,1,0:T(8,128)S(1)} %bitcast.27), custom_call_target="tpu_custom_call" | custom-call | tf_op jit(solution)/shard_map/basis/pallas_call | solution.py:432
  (60 shorter events, 8.9 us)
Async XLA Ops:
  7.2 54.0 %all-gather.2.cloned.1.call-start = ((), (), s32[]{:S(2)}) async-start(), calls=%async_computation.3 | async-start | bytes 2359296 | tf_op jit(solution)/shard_map/all_gather | solution.py:329
  10.7 10.5 %copy-start.7 = (f32[64,64]{1,0:T(8,128)S(1)}, f32[64,64]{1,0:T(8,128)}, u32[]{:S(2)}) copy-start(f32[64,64]{1,0:T(8,128)} %param.9) | copy-start | bytes 49156
  10.7 10.7 %copy-start.6 = (f32[65,65]{1,0:T(8,128)S(1)}, f32[65,65]{1,0:T(8,128)}, u32[]{:S(2)}) copy-start(f32[65,65]{1,0:T(8,128)} %param.10) | copy-start | bytes 50704
  10.7 15.6 %copy-start.8 = (f32[64,64]{1,0:T(8,128)S(1)}, f32[64,64]{1,0:T(8,128)}, u32[]{:S(2)}) copy-start(f32[64,64]{1,0:T(8,128)} %param.8) | copy-start | bytes 49156
  10.7 45.3 %all-to-all-start = ((f32[8,8,64,128]{3,1,2,0:T(8,128)}), f32[8,8,64,128]{3,1,2,0:T(8,128)S(1)}, u32[]{:S(2)}, u32[]{:S(2)}) async-start(f32[8,8,64,128]{3,1,2,0:T(8,128)} %bitcast.32), calls=%async_computation | async-start | bytes 4194304 | tf_op jit(solution)/shard_map/all_to_all | solution.py:332
  56.0 1.8 copy-start.5
  56.2 14.9 %collective-permute-start.1 = (f32[64,128]{1,0:T(8,128)S(1)}, f32[64,128]{1,0:T(8,128)S(1)}, u32[]{:S(2)}, u32[]{:S(2)}) collective-permute-start(f32[64,128]{1,0:T(8,128)S(1)} %bitcast.34), channel_id=1, source_target_pairs={{0,8},{8,16},{16,24},{24,32},{32,40},{40,48},{48,56},{56,64},{64,7... | collective-permute-start | bytes 98312 | tf_op jit(solution)/shard_map/ppermute | solution.py:23
  57.8 13.3 %collective-permute-start = (f32[64,128]{1,0:T(8,128)S(1)}, f32[64,128]{1,0:T(8,128)S(1)}, u32[]{:S(2)}, u32[]{:S(2)}) collective-permute-start(f32[64,128]{1,0:T(8,128)S(1)} %slice_bitcast_fusion), channel_id=1, source_target_pairs={{8,0},{16,8},{24,16},{32,24},{40,32},{48,40},{56,48},{64,56},{72,6... | collective-permute-start | bytes 98312 | tf_op jit(solution)/shard_map/ppermute | solution.py:23
  61.1 8.7 %copy-start = (f32[8,8,64,128]{3,2,1,0:T(8,128)}, f32[8,8,64,128]{3,2,1,0:T(8,128)S(1)}, u32[]{:S(2)}) copy-start(f32[8,8,64,128]{3,2,1,0:T(8,128)S(1)} %copy.16) | copy-start | bytes 6291460
  69.8 1.3 copy-start.4
  73.0 17.8 %collective-permute-start.2 = (f32[64,128]{1,0:T(8,128)S(1)}, f32[64,128]{1,0:T(8,128)S(1)}, u32[]{:S(2)}, u32[]{:S(2)}) collective-permute-start(f32[64,128]{1,0:T(8,128)S(1)} %get-tuple-element.67), channel_id=1, source_target_pairs={{8,0},{16,8},{24,16},{32,24},{40,32},{48,40},{56,48},{64,56},{72,6... | collective-permute-start | bytes 98312 | tf_op jit(solution)/shard_map/ppermute | solution.py:23
  74.3 16.5 %collective-permute-start.3 = (f32[64,128]{1,0:T(8,128)S(1)}, f32[64,128]{1,0:T(8,128)S(1)}, u32[]{:S(2)}, u32[]{:S(2)}) collective-permute-start(f32[64,128]{1,0:T(8,128)S(1)} %get-tuple-element.66), channel_id=1, source_target_pairs={{0,8},{8,16},{16,24},{24,32},{32,40},{40,48},{48,56},{56,64},{64,7... | collective-permute-start | bytes 98312 | tf_op jit(solution)/shard_map/ppermute | solution.py:23
  88.1 1.3 copy-start.2
  89.5 1.3 copy-start.3
  90.8 14.6 %collective-permute-start.4 = (f32[64,128]{1,0:T(8,128)S(1)}, f32[64,128]{1,0:T(8,128)S(1)}, u32[]{:S(2)}, u32[]{:S(2)}) collective-permute-start(f32[64,128]{1,0:T(8,128)S(1)} %get-tuple-element.65), channel_id=1, source_target_pairs={{8,0},{16,8},{24,16},{32,24},{40,32},{48,40},{56,48},{64,56},{72,6... | collective-permute-start | bytes 98312 | tf_op jit(solution)/shard_map/ppermute | solution.py:23
  92.1 13.3 %collective-permute-start.5 = (f32[64,128]{1,0:T(8,128)S(1)}, f32[64,128]{1,0:T(8,128)S(1)}, u32[]{:S(2)}, u32[]{:S(2)}) collective-permute-start(f32[64,128]{1,0:T(8,128)S(1)} %get-tuple-element.64), channel_id=1, source_target_pairs={{0,8},{8,16},{16,24},{24,32},{32,40},{40,48},{48,56},{56,64},{64,7... | collective-permute-start | bytes 98312 | tf_op jit(solution)/shard_map/ppermute | solution.py:23
  105.4 10.2 %collective-permute-start.6 = (f32[64,128]{1,0:T(8,128)S(1)}, f32[64,128]{1,0:T(8,128)S(1)}, u32[]{:S(2)}, u32[]{:S(2)}) collective-permute-start(f32[64,128]{1,0:T(8,128)S(1)} %get-tuple-element.63), channel_id=1, source_target_pairs={{8,0},{16,8},{24,16},{32,24},{40,32},{48,40},{56,48},{64,56},{72,6... | collective-permute-start | bytes 98312 | tf_op jit(solution)/shard_map/ppermute | solution.py:23
  106.7 8.9 %collective-permute-start.7 = (f32[64,128]{1,0:T(8,128)S(1)}, f32[64,128]{1,0:T(8,128)S(1)}, u32[]{:S(2)}, u32[]{:S(2)}) collective-permute-start(f32[64,128]{1,0:T(8,128)S(1)} %get-tuple-element.62), channel_id=1, source_target_pairs={{0,8},{8,16},{16,24},{24,32},{32,40},{40,48},{48,56},{56,64},{64,7... | collective-permute-start | bytes 98312 | tf_op jit(solution)/shard_map/ppermute | solution.py:23
  115.6 7.5 %copy-start.1 = (f32[2,8,64,128]{3,2,1,0:T(8,128)S(1)}, f32[2,8,64,128]{3,2,1,0:T(8,128)}, u32[]{:S(2)}) copy-start(f32[2,8,64,128]{3,2,1,0:T(8,128)} %param.7) | copy-start | bytes 1572868
  116.3 6.7 %collective-permute-start.8 = (f32[4,512,128]{2,1,0:T(8,128)S(1)}, f32[4,512,128]{2,1,0:T(8,128)S(1)}, u32[]{:S(2)}, u32[]{:S(2)}) collective-permute-start(f32[4,512,128]{2,1,0:T(8,128)S(1)} %get-tuple-element.51), channel_id=1, source_target_pairs={{0,1},{1,0},{2,3},{3,2},{4,5},{5,4},{6,7},{7,6},{8,9},{9,8},{10,11... | collective-permute-start | bytes 3145736 | tf_op jit(solution)/shard_map/ppermute | solution.py:418
Sparse Core Ops, SparseCore 0:
  10.1 45.0 all-gather.1
where the time goes:
time: 194 us; the launch traced here: 193 us
  Pallas kernels  49.3 us (25%)
  blocking collectives  45.4 us (23%)
  starting transfers between devices  34.1 us (18%)
  waiting for transfers between devices  32.5 us (17%)
  between operations  17.5 us (9%)
  local copies, waits for them, and re-layouts  11 us (6%)
  other arithmetic  3.12 us (2%)
    all_to_all x1, blocking collectives, shards(): lax.all_to_all(jnp.broadcast_to(gram, (beam, 1, width)), 'beam', 0, 0, ti...  38.1 us
    pallas_call x4, Pallas kernels, step(): pl.pallas_call(body, out_shape=outs, in_specs=[pl.BlockSpec(memory_space=...  31.8 us
    all_to_all x1, waiting for transfers between devices, shards(): lax.all_to_all(sent, 'trans', 0, 0, tiled=True).reshape(nx * nz, width)  29.5 us
    ppermute x8, starting transfers between devices, passed(): lax.ppermute(x, 'beam', [(i, i + by) for i in range(peers) if 0 <= i + by...  19.1 us
    pallas_call x1, Pallas kernels, shards(): pl.pallas_call(gram_body, out_shape=[in_vmem(ncol, size, width), in_vmem(...  11.2 us
    all_to_all x1, starting transfers between devices, shards(): lax.all_to_all(sent, 'trans', 0, 0, tiled=True).reshape(nx * nz, width)  10.5 us
    all_to_all x1, blocking collectives, shards(): lax.all_to_all(gram, 'trans', 0, 0, tiled=True)  7.3 us
    unnamed x21, local copies, waits for them, and re-layouts  5.99 us
  transfers between devices with their start and end apart: 11, of which 2 were waited for; matrix products, arithmetic and copies ran while one was open for 4% of the time, Pallas kernels for 16%

commit v1 on v0

v1 whole, which is shorter than its diff:
```python
import functools

import jax
import jax.numpy as jnp
from jax import lax
from jax.experimental import pallas as pl
from jax.experimental.pallas import tpu as pltpu
from jax.sharding import PartitionSpec as P

POWERS = 4
F32 = jnp.float32
BF16 = jnp.bfloat16
LIMIT = 16 * 1024 * 1024


def split(v):
    high = v.astype(BF16)
    return high, (v - high.astype(F32)).astype(BF16)


def passed(x, by):
    peers = lax.axis_size("beam")
    return lax.ppermute(x, "beam", [(i, i + by) for i in range(peers) if 0 <= i + by < peers])


PAD = 8


def step_body(fix, with_prev, last, nx, nz, width, chip, strides, scal, *refs):
    refs = list(refs)
    cur_ref = refs.pop(0)
    if fix:
        pin_ref, bin_ref = refs.pop(0), refs.pop(0)
    prev_ref = refs.pop(0) if with_prev else None
    pot_ref, kz_ref, kx_ref, wy_ref, rcol_ref, wvec_ref = refs[:6]
    refs = refs[6:]
    out_ref = refs.pop(0)
    if not last:
        first_ref, bridge_ref = refs.pop(0), refs.pop(0)
    rows_ref = refs.pop(0) if fix else None
    col_ref = refs.pop(0)
    cur_stride, prev_stride = strides
    stride = nz + PAD
    half = width // 2
    scale = 2.0 if with_prev else 1.0
    left = lax.broadcasted_iota(jnp.int32, (nz, width), 1) < half
    top = lax.broadcasted_iota(jnp.int32, (8, width), 0) == 0
    x_start = scal[0] if last else 0
    out_x = chip if last else nx

    def rows_of(x, step):
        return pl.ds(pl.multiple_of(x * step, 8), nz)

    def fixed(x):
        u = cur_ref[rows_of(x, cur_stride), :]
        if fix:
            u = u + rcol_ref[...] * pin_ref[pl.ds(x, 1), :]
            head = u[0:8] + jnp.where(top, bin_ref[pl.ds(x, 1), :], 0.0)
            u = jnp.concatenate([head, u[8:]], axis=0)
        col_ref[rows_of(x, stride), :] = u
        return u

    def product(k_ref, us):
        parts = [split(u) for u in us]
        rows = []
        for p, q in (parts[0:2], parts[2:4]):
            rows += [jnp.concatenate([p[0], q[0]], axis=1), jnp.concatenate([p[1], q[1]], axis=1)]
        got = jnp.dot(k_ref[...], jnp.concatenate(rows, axis=0), preferred_element_type=F32)
        m = got.shape[0] // 4
        outs = []
        for i in range(2):
            both = got[2 * i * m : (2 * i + 1) * m] + got[(2 * i + 1) * m : (2 * i + 2) * m]
            outs += [both[:, :width], both[:, width:]]
        return outs, parts

    def local_four(x0):
        us = []
        for q in range(4):
            if last:
                us.append(col_ref[rows_of(x_start + x0 + q, stride), :])
            else:
                us.append(fixed(x0 + q))
        along_z, parts = product(kz_ref, us)
        along_y = jnp.dot(
            jnp.concatenate([jnp.concatenate(p, axis=1) for p in parts], axis=0),
            wy_ref[...],
            preferred_element_type=F32,
        )
        for q in range(4):
            u = us[q]
            x = x_start + x0 + q
            pv = pot_ref[rows_of(x, nz), :]
            pr = pltpu.roll(pv, half, 1)
            optical = jnp.where(left, pv, pr) * u + jnp.where(left, pr, -pv) * pltpu.roll(u, half, 1)
            ay = along_y[q * nz : (q + 1) * nz]
            new = along_z[q] + ay[:, :width] + ay[:, width:] + scale * optical
            if with_prev:
                new = new - prev_ref[rows_of(x, prev_stride), :]
            out_ref[rows_of(x0 + q, stride), :] = new

    def repeat(count, unroll, body, carry):
        unroll = min(unroll, count)

        def some(i, carry):
            for q in range(unroll):
                carry = body(i * unroll + q, carry)
            return carry

        return lax.fori_loop(0, count // unroll, some, carry)

    def only(body):
        def with_carry(i, carry):
            body(i)
            return carry

        return with_carry

    if last:
        repeat(nx, 16, only(fixed), 0)
    repeat(out_x // 4, 8, only(lambda i: local_four(i * 4)), 0)
    if fix:
        for q in range(chip):
            rows_ref[q * nz : (q + 1) * nz, :] = col_ref[rows_of(scal[0] + q, stride), :]

    def across_four(i, bridge):
        z0 = i * 4
        us = [col_ref[pl.ds(z0 + q, nx, stride=stride), :] for q in range(4)]
        along_x, _ = product(kx_ref, us)
        for q in range(4):
            at = pl.ds(z0 + q, out_x, stride=stride)
            new = out_ref[at, :] + along_x[q]
            out_ref[at, :] = new
            if not last:
                bridge = bridge + wvec_ref[pl.ds(z0 + q, 1), :] * new
        return bridge

    bridge = repeat(nz // 4, 8, across_four, jnp.zeros((out_x, width), F32))
    if not last:
        bridge_ref[...] = bridge
        first_ref[...] = out_ref[pl.ds(0, nx, stride=stride), :]


def vm():
    return pl.BlockSpec(memory_space=pltpu.VMEM)


def in_vmem(*shape):
    return pltpu.VMEM(shape, F32)


def step(scal, cur, halo, prev, pot, kz, kx, wy, rcol, wvec, nx, nz, chip, last):
    fix, with_prev = halo is not None, prev is not None
    width = cur.shape[-1]
    stride = nz + PAD
    ins = [cur] + (list(halo) if fix else []) + ([prev] if with_prev else [])
    ins += [pot, kz, kx, wy, rcol, wvec]
    outs = [in_vmem((chip if last else nx) * stride, width)]
    if not last:
        outs += [in_vmem(nx, width), in_vmem(nx, width)]
    if fix:
        outs += [in_vmem(chip * nz, width)]
    scratch = []
    if fix and not last:
        outs += [in_vmem(nx * stride, width)]
    else:
        scratch = [pltpu.VMEM((nx * stride, width), F32)]
    strides = (cur.shape[0] // nx, prev.shape[0] // nx if with_prev else 0)
    body = functools.partial(step_body, fix, with_prev, last, nx, nz, width, chip, strides)
    return pl.pallas_call(
        body,
        out_shape=outs,
        in_specs=[pl.BlockSpec(memory_space=pltpu.SMEM)] + [vm()] * len(ins),
        out_specs=[vm()] * len(outs),
        scratch_shapes=scratch,
        compiler_params=pltpu.CompilerParams(vmem_limit_bytes=LIMIT),
        cost_estimate=pl.CostEstimate(flops=4 * 10**9, bytes_accessed=8 * 10**6, transcendentals=0),
        name="step",
    )(scal, *ins)


def finish_body(nz, rows, scal, last_ref, pin_ref, bin_ref, rcol_ref, *refs):
    cols = refs[: POWERS - 1]
    keep_ref, send_ref = refs[POWERS - 1 :]
    core = scal[1]
    size = rows * nz
    width = last_ref.shape[-1]
    top = lax.broadcasted_iota(jnp.int32, (8, width), 0) == 0
    for ref, where in ((keep_ref, core), (send_ref, 1 - core)):
        at = pl.ds(pl.multiple_of(where * size, size), size)
        for k in range(POWERS - 1):
            ref[k] = cols[k][at, :]
        for r in range(rows):
            x = where * rows + r
            u = last_ref[pl.ds(pl.multiple_of(x * (nz + PAD), 8), nz), :]
            u = u + rcol_ref[...] * pin_ref[pl.ds(x, 1), :]
            head = u[0:8] + jnp.where(top, bin_ref[pl.ds(x, 1), :], 0.0)
            ref[POWERS - 1, r * nz : (r + 1) * nz, :] = jnp.concatenate([head, u[8:]], axis=0)


def gram_body(scal, packets_ref, keep_ref, recv_ref, cols_ref, gram_ref, acc_ref):
    core = scal[1]
    ncol, size, width = cols_ref.shape
    npow = ncol // 2
    half = width // 2
    cols_ref[0] = packets_ref[0]
    cols_ref[npow] = packets_ref[1]
    for k in range(npow - 1):
        cols_ref[core * npow + 1 + k] = keep_ref[k]
        cols_ref[(1 - core) * npow + 1 + k] = recv_ref[k]
    acc_ref[...] = jnp.zeros_like(acc_ref)
    sign = jnp.where(lax.broadcasted_iota(jnp.int32, (8, width), 1) < half, 1.0, -1.0)
    first, second = list(range(npow)), list(range(npow, ncol))
    groups = [
        [(a, b) for a in first for b in first if a <= b],
        [(a, b) for a in second for b in second if a <= b],
        [(a, b) for a in first for b in second[:3]],
        [(a, b) for a in first for b in second[3:]],
    ]
    unroll = 16
    for pairs in groups:
        used = sorted({c for pair in pairs for c in pair})
        turned = sorted({b for a, b in pairs if a != b})

        def chunk(i, sums, pairs=pairs, used=used, turned=turned):
            sums = list(sums)
            for q in range(unroll):
                at = pl.ds(pl.multiple_of((i * unroll + q) * 8, 8), 8)
                v = {c: cols_ref[c, at, :] for c in used}
                t = {c: pltpu.roll(v[c], half, 1) for c in turned}
                n = 0
                for a, b in pairs:
                    sums[n] = sums[n] + v[a] * v[b]
                    n += 1
                    if a != b:
                        sums[n] = sums[n] + v[a] * t[b]
                        n += 1
            return tuple(sums)

        count = sum(1 if a == b else 2 for a, b in pairs)
        sums = lax.fori_loop(
            0, size // (8 * unroll), chunk, tuple(jnp.zeros((8, width), F32) for _ in range(count))
        )
        n = 0
        for a, b in pairs:
            acc_ref[a * ncol + b : a * ncol + b + 1, :] = jnp.sum(sums[n], axis=0, keepdims=True)
            n += 1
            if a != b:
                acc_ref[b * ncol + a : b * ncol + a + 1, :] = jnp.sum(
                    sums[n] * sign, axis=0, keepdims=True
                )
                n += 1
    row = jnp.sum(acc_ref[...].T, axis=0, keepdims=True)
    gram_ref[...] = jnp.broadcast_to(row[None], gram_ref.shape)


def basis_body(cells, rows, gram_ref, cols_ref, basis_ref, factor_ref, coef_ref, out_ref, sems):
    ncol, size, width = cols_ref.shape
    half = width // 2
    row = jnp.sum(gram_ref[...], axis=0) * (1.0 / cells)
    r = lax.broadcasted_iota(jnp.int32, (16, width), 0)
    c = lax.broadcasted_iota(jnp.int32, (16, width), 1)
    packed = jnp.zeros((16, width), F32)
    for j in range(ncol):
        moved = row if j == 0 else pltpu.roll(row, width - ncol * j, 1)
        packed = jnp.where(r == j, moved, packed)
    turned = jnp.concatenate([packed, jnp.zeros((width - 16, width), F32)], axis=0).T[:16]
    inside = (r < ncol) & (c < ncol)
    re = jnp.where(inside, jnp.where(r <= c, packed, turned), 0.0)
    im = jnp.where(inside & (r != c), jnp.where(r < c, turned, -packed), 0.0)
    re = jnp.where(c == r + 16, 1.0, re)
    up_re = jnp.zeros((16, width), F32)
    up_im = jnp.zeros((16, width), F32)
    for j in range(ncol):
        pivot = jnp.sqrt(re[j : j + 1, j : j + 1])
        inverse = 1.0 / pivot
        row_re = re[j : j + 1, :] * inverse
        row_im = im[j : j + 1, :] * inverse
        col_re = re[:, j : j + 1] * inverse
        col_im = im[:, j : j + 1] * inverse
        up_re = jnp.where(r == j, row_re, up_re)
        up_im = jnp.where(r == j, row_im, up_im)
        below = r > j
        re = re - jnp.where(below, col_re * row_re - col_im * row_im, 0.0)
        im = im - jnp.where(below, col_re * row_im + col_im * row_re, 0.0)
    keep = (c >= r) & (c < ncol)
    factor_ref[0] = jnp.where(keep, up_re, 0.0)
    factor_ref[1] = jnp.where(keep & (c > r), up_im, 0.0)
    sign = jnp.where(lax.broadcasted_iota(jnp.int32, (8, width), 1) < half, 1.0, -1.0)
    for k in range(ncol):
        for i in range(k + 1):
            coef_ref[0, k * ncol + i] = jnp.broadcast_to(up_re[k : k + 1, 16 + i : 17 + i], (8, width))
            coef_ref[1, k * ncol + i] = (
                jnp.broadcast_to(up_im[k : k + 1, 16 + i : 17 + i], (8, width)) * sign
            )
    group = 4
    each = size // rows
    copies = []
    for r in range(rows):
        for start in range(r * each, (r + 1) * each, 8 * group):
            slots = [slice(start + 8 * g, start + 8 * g + 8) for g in range(group)]
            v = [[cols_ref[i, s, :] for s in slots] for i in range(ncol)]
            t = [[pltpu.roll(x, half, 1) for x in xs] for xs in v]
            for k in range(ncol):
                total = [None] * group
                for i in range(k + 1):
                    re = coef_ref[0, k * ncol + i]
                    im = coef_ref[1, k * ncol + i]
                    for g in range(group):
                        term = re * v[i][g]
                        if i < k:
                            term = term + im * t[i][g]
                        total[g] = term if total[g] is None else total[g] + term
                for g in range(group):
                    out_ref[k, slots[g], :] = total[g]
        part = pl.ds(r * each, each)
        copy = pltpu.make_async_copy(out_ref.at[:, part, :], basis_ref.at[:, part, :], sems.at[r])
        copy.start()
        copies.append(copy)
    for copy in copies:
        copy.wait()


def shards(packets, kinetic_x, kinetic_y, element_kinetic, potential):
    npack, rows, nz, width = packets.shape
    trans = lax.axis_size("trans")
    nx = rows * trans
    ncol = npack * (POWERS + 1)
    me = lax.axis_index("trans")
    core = me % 2
    chip = 2 * rows
    scal = jnp.stack([(me // 2) * chip, core]).astype(jnp.int32)

    pot = lax.all_gather(potential.reshape(rows * nz, width), "trans", axis=0, tiled=True)
    sent = packets.reshape(npack, rows * nz, width)
    sent = jnp.concatenate([sent] * (trans // npack), axis=0)
    cur = lax.all_to_all(sent, "trans", 0, 0, tiled=True).reshape(nx * nz, width)

    corner = element_kinetic[nz, nz] * (lax.axis_index("beam") > 0).astype(F32)
    kz = element_kinetic[:nz, :nz].at[0, 0].add(corner)
    wrow = element_kinetic[nz, :nz]
    rcol = element_kinetic[:nz, nz]

    def parts_of(k):
        high = lax.reduce_precision(k, 8, 7)
        return high.astype(BF16), (k - high).astype(BF16)

    def left_weights(k):
        high, low = parts_of(k)
        none = jnp.zeros_like(high)
        block = jnp.concatenate(
            [jnp.concatenate([high, high], axis=1), jnp.concatenate([low, none], axis=1)], axis=0
        )
        none = jnp.zeros_like(block)
        return jnp.concatenate(
            [jnp.concatenate([block, none], axis=1), jnp.concatenate([none, block], axis=1)], axis=0
        )

    ky_high, ky_low = parts_of(jnp.kron(jnp.eye(2, dtype=F32), kinetic_y).T)
    wy = jnp.concatenate(
        [
            jnp.concatenate([ky_high, ky_low], axis=1),
            jnp.concatenate([ky_high, jnp.zeros_like(ky_low)], axis=1),
        ],
        axis=0,
    )
    kz1, kx1 = left_weights(kz), left_weights(kinetic_x)
    kz2, kx2, wy2 = kz1 * 2, kx1 * 2, wy * 2
    kx_last = left_weights(2.0 * lax.dynamic_slice_in_dim(kinetic_x, scal[0], chip, 0))
    rcol1 = jnp.broadcast_to(rcol[:, None], (nz, width))
    rcol2 = rcol1 * 2.0
    wvec = jnp.broadcast_to(wrow[:, None], (nz, width))

    def halo(first, bridge, pin, bin_, scale):
        if pin is not None:
            bridge = bridge + (scale * jnp.dot(wrow, rcol, precision="highest")) * pin
            bridge = bridge + (scale * wrow[0]) * bin_
            first = first + (scale * rcol[0]) * pin + scale * bin_
        return passed(first, -1), passed(bridge, 1)

    whole = cur.reshape(nx, nz, width)
    halos = [halo(whole[:, 0], jnp.sum(whole * wvec, axis=1), None, None, 1.0)]
    columns = []
    prev = None
    local, first, bridge = step(
        scal, cur, None, None, pot, kz1, kx1, wy, rcol1, wvec, nx, nz, chip, False
    )
    prev = cur
    for k in range(1, POWERS):
        scale = 1.0 if k == 1 else 2.0
        pin, bin_ = halos[-1]
        fresh = halo(first, bridge, pin, bin_, scale)
        last = k == POWERS - 1
        got = step(
            scal,
            local,
            (pin, scale * bin_),
            prev,
            pot,
            kz2,
            kx_last if last else kx2,
            wy2,
            rcol1 if k == 1 else rcol2,
            wvec,
            nx,
            nz,
            chip,
            last,
        )
        if last:
            local, col_rows = got
        else:
            prev_next = got[4]
            local, first, bridge, col_rows = got[:4]
            prev = prev_next
        columns.append(col_rows)
        halos.append(fresh)
    pin, bin_ = halos[-1]
    pin = lax.dynamic_slice_in_dim(pin, scal[0], chip, 0)
    bin_ = lax.dynamic_slice_in_dim(2.0 * bin_, scal[0], chip, 0)
    size = rows * nz
    keep, send = pl.pallas_call(
        functools.partial(finish_body, nz, rows),
        out_shape=[in_vmem(POWERS, size, width)] * 2,
        in_specs=[pl.BlockSpec(memory_space=pltpu.SMEM)] + [vm()] * (4 + POWERS - 1),
        out_specs=[vm()] * 2,
        compiler_params=pltpu.CompilerParams(vmem_limit_bytes=LIMIT),
        name="finish",
    )(scal, local, pin, bin_, rcol2, *columns)
    recv = lax.ppermute(send, "trans", [(i, i ^ 1) for i in range(trans)])
    cols, gram = pl.pallas_call(
        gram_body,
        out_shape=[in_vmem(ncol, size, width), in_vmem(trans, 1, width)],
        in_specs=[pl.BlockSpec(memory_space=pltpu.SMEM)] + [vm()] * 3,
        out_specs=[vm()] * 2,
        scratch_shapes=[pltpu.VMEM((128, width), F32)],
        compiler_params=pltpu.CompilerParams(vmem_limit_bytes=LIMIT),
        name="gram",
    )(scal, packets.reshape(npack, size, width), keep, recv)
    beam = lax.axis_size("beam")
    gram = jnp.sum(lax.all_to_all(gram, "trans", 0, 0, tiled=True), axis=0, keepdims=True)
    gram = lax.all_to_all(jnp.broadcast_to(gram, (beam, 1, width)), "beam", 0, 0, tiled=True)
    cells = float(nx * (width // 2) * nz * beam)
    basis, factor = pl.pallas_call(
        functools.partial(basis_body, cells, rows),
        out_shape=[
            jax.ShapeDtypeStruct((ncol, size, width), F32),
            jax.ShapeDtypeStruct((2, 16, width), F32),
        ],
        in_specs=[vm(), vm()],
        out_specs=[pl.BlockSpec(memory_space=pl.ANY), vm()],
        scratch_shapes=[
            pltpu.VMEM((2, ncol * ncol, 8, width), F32),
            pltpu.VMEM((ncol, size, width), F32),
            pltpu.SemaphoreType.DMA((rows,)),
        ],
        compiler_params=pltpu.CompilerParams(vmem_limit_bytes=LIMIT),
        name="basis",
    )(gram, cols)
    return basis.reshape(ncol, rows, nz, width), factor[:, :ncol, :ncol]


def solution(mesh):
    in_specs = (P(None, "trans", "beam", None), P(), P(), P(), P("trans", "beam", None))
    out_specs = (P(None, "trans", "beam", None), P())
    return jax.shard_map(shards, mesh=mesh, in_specs=in_specs, out_specs=out_specs, check_vma=False)
```

time: 194 us -> 167 us (0.86)
  Pallas kernels: 49.3 us -> 21.9 us
  local copies, waits for them, and re-layouts: 11 us -> 3.58 us
  blocking collectives: 45.4 us -> 49.9 us
  other arithmetic: 3.12 us -> 7.02 us
    pallas_call x4, Pallas kernels: 31.8 us -> 12.9 us  [step(): pl.pallas_call(body, out_shape=outs, in_specs=[pl.BlockSpec(memory_space=...]
    pallas_call x1, Pallas kernels: 11.2 us -> 3.03 us  [shards(): pl.pallas_call(gram_body, out_shape=[in_vmem(ncol, size, width), in_vmem(...]
    all_to_all x1, blocking collectives: 38.1 us -> 42.6 us  [shards(): lax.all_to_all(jnp.broadcast_to(gram, (beam, 1, width)), 'beam', 0, 0, ti...]
    concatenate x0 -> x5, other arithmetic: none -> 3.73 us  [the longest x1 3.47 us: shards(): sent = jnp.concatenate([sent] * (trans // npack), axis=0)]
    unnamed x21 -> x12, local copies, waits for them, and re-layouts: 5.99 us -> 2.3 us
    all_to_all x2 -> x0, local copies, waits for them, and re-layouts: 2.23 us -> none  [shards(): lax.all_to_all(sent, 'trans', 0, 0, tiled=True).reshape(nx * nz, width)]
  transfers between devices with their start and end apart: 11 -> 11, of which waited for: 2 -> 2; matrix products, arithmetic and copies ran while one was open for 4% -> 4% of each run, Pallas kernels for 16% -> 8%
where the time goes in v1:
time: 167 us; the launch traced here: 166 us
  blocking collectives  49.9 us (30%)
  starting transfers between devices  34.1 us (20%)
  waiting for transfers between devices  32.3 us (19%)
  Pallas kernels  21.9 us (13%)
  between operations  17.4 us (10%)
  other arithmetic  7.02 us (4%)
  local copies, waits for them, and re-layouts  3.58 us (2%)
    all_to_all x1, blocking collectives, shards(): lax.all_to_all(jnp.broadcast_to(gram, (beam, 1, width)), 'beam', 0, 0, ti...  42.6 us
    all_to_all x1, waiting for transfers between devices, shards(): lax.all_to_all(sent, 'trans', 0, 0, tiled=True).reshape(nx * nz, width)  29.3 us
    ppermute x8, starting transfers between devices, passed(): lax.ppermute(x, 'beam', [(i, i + by) for i in range(peers) if 0 <= i + by...  19 us
    pallas_call x4, Pallas kernels, step(): pl.pallas_call(body, out_shape=outs, in_specs=[pl.BlockSpec(memory_space=...  12.9 us
    all_to_all x1, starting transfers between devices, shards(): lax.all_to_all(sent, 'trans', 0, 0, tiled=True).reshape(nx * nz, width)  10.5 us
    all_to_all x1, blocking collectives, shards(): lax.all_to_all(gram, 'trans', 0, 0, tiled=True)  7.3 us
    pallas_call x1, Pallas kernels, shards(): pl.pallas_call(functools.partial(basis_body, cells, rows), out_shape=[jax...  5.32 us
    ppermute x1, starting transfers between devices, shards(): recv = lax.ppermute(send, 'trans', [(i, i ^ 1) for i in range(trans)])  4.45 us
  transfers between devices with their start and end apart: 11, of which 2 were waited for; matrix products, arithmetic and copies ran while one was open for 4% of the time, Pallas kernels for 8%

profile of v1, /device:TPU:1, one launch (start us, length us, event | category | flops | bytes accessed | tf_op | source)
XLA Modules:
  0.0 166.3 jit_solution(9813110856511715726)
XLA Ops:
  7.9 3.5 %pad_maximum_fusion = f32[8,512,128]{2,1,0:T(8,128)} fusion(f32[2,512,128]{2,1,0:T(8,128)} %bitcast.28), kind=kLoop, calls=%fused_computation | loop fusion | flops 1572864 | bytes 2621440 | tf_op jit(solution)/shard_map/concatenate | solution.py:335
  11.4 10.5 %all-to-all-start = ((f32[8,512,128]{2,1,0:T(8,128)}), f32[8,512,128]{2,1,0:T(8,128)S(1)}, u32[]{:S(2)}, u32[]{:S(2)}) async-start(f32[8,512,128]{2,1,0:T(8,128)} %pad_maximum_fusion), calls=%async_computation | async-start | bytes 4194304 | tf_op jit(solution)/shard_map/all_to_all | solution.py:336
  27.3 29.3 %all-to-all-done = f32[8,512,128]{2,1,0:T(8,128)S(1)} async-done(((f32[8,512,128]{2,1,0:T(8,128)}), f32[8,512,128]{2,1,0:T(8,128)S(1)}, u32[]{:S(2)}, u32[]{:S(2)}) %all-to-all-start) | async-done | bytes 2097184 | tf_op jit(solution)/shard_map/all_to_all | solution.py:336
  57.1 1.3 collective-permute-start.1
  58.4 1.3 collective-permute-start
  59.9 1.6 copy-done.1
  61.5 3.3 %step.4 = (f32[4608,128]{1,0:T(8,128)S(1)}, f32[64,128]{1,0:T(8,128)S(1)}, f32[64,128]{1,0:T(8,128)S(1)}) custom-call(s32[2]{0:T(128)S(1)} %pad_add_fusion.scal, f32[4096,128]{1,0:T(8,128)S(1)} %bitcast.26, f32[4096,128]{1,0:T(8,128)S(1)} %copy-done.1, bf16[256,256]{1,0:T(8,128)(2,1)S(1)} %get-tuple-element.81.refs_2_, ...), custom_call_target="tpu_custom_call" | custom-call | flops 4000000000 | bytes 8000000 | tf_op jit(solution)/shard_map/step/pallas_call | solution.py:169
  64.8 1.9 %multiply_add_fusion.2 = (f32[64,128]{1,0:T(8,128)S(1)}, f32[64,128]{1,0:T(8,128)S(1)}) fusion(f32[64,128]{1,0:T(8,128)S(1)} %collective-permute-done.1.refs_2_, f32[64,128]{1,0:T(8,128)S(1)} %get-tuple-element.38, f32[64,128]{1,0:T(8,128)S(1)} %collective-permute-done.refs_1_, f32[]{:T(128)} %bitcast.12, f32[]{:T(128)} %get-tuple-element.87, ...), kind=kLoop, calls=%fused_computation.39 | loop fusion | flops 57344 | bytes 196620 | tf_op jit(solution)/shard_map/add | solution.py:376
  66.7 1.3 collective-permute-start.2
  68.0 4.6 %collective-permute-start.3 = (f32[64,128]{1,0:T(8,128)S(1)}, f32[64,128]{1,0:T(8,128)S(1)}, u32[]{:S(2)}, u32[]{:S(2)}) collective-permute-start(f32[64,128]{1,0:T(8,128)S(1)} %get-tuple-element.64), channel_id=1, source_target_pairs={{0,8},{8,16},{16,24},{24,32},{32,40},{40,48},{48,56},{56,64},{64,7... | collective-permute-start | bytes 98312 | tf_op jit(solution)/shard_map/ppermute | solution.py:23
  72.6 3.8 %step.5 = (f32[4608,128]{1,0:T(8,128)S(1)}, f32[64,128]{1,0:T(8,128)S(1)}, f32[64,128]{1,0:T(8,128)S(1)}, f32[1024,128]{1,0:T(8,128)S(1)}, f32[4608,128]{1,0:T(8,128)S(1)}) custom-call(s32[2]{0:T(128)S(1)} %pad_add_fusion.scal, f32[4608,128]{1,0:T(8,128)S(1)} %get-tuple-element.35.refs_0_, f32[64,128]{1,0:T(8,128)S(1)} %collective-permute-done.refs_1_, ...), custom_call_target="tpu_custom_call" | custom-call | flops 4000000000 | bytes 8000000 | tf_op jit(solution)/shard_map/step/pallas_call | solution.py:169
  76.5 1.3 collective-permute-start.4
  77.8 4.0 %collective-permute-start.5 = (f32[64,128]{1,0:T(8,128)S(1)}, f32[64,128]{1,0:T(8,128)S(1)}, u32[]{:S(2)}, u32[]{:S(2)}) collective-permute-start(f32[64,128]{1,0:T(8,128)S(1)} %get-tuple-element.62), channel_id=1, source_target_pairs={{0,8},{8,16},{16,24},{24,32},{32,40},{40,48},{48,56},{56,64},{64,7... | collective-permute-start | bytes 98312 | tf_op jit(solution)/shard_map/ppermute | solution.py:23
  81.9 3.9 %step.6 = (f32[4608,128]{1,0:T(8,128)S(1)}, f32[64,128]{1,0:T(8,128)S(1)}, f32[64,128]{1,0:T(8,128)S(1)}, f32[1024,128]{1,0:T(8,128)S(1)}, f32[4608,128]{1,0:T(8,128)S(1)}) custom-call(s32[2]{0:T(128)S(1)} %pad_add_fusion.scal, f32[4608,128]{1,0:T(8,128)S(1)} %get-tuple-element.36.refs_0_, f32[64,128]{1,0:T(8,128)S(1)} %collective-permute-done.2.refs_1_, ...), custom_call_target="tpu_custom_call" | custom-call | flops 4000000000 | bytes 8000000 | tf_op jit(solution)/shard_map/step/pallas_call | solution.py:169
  85.8 1.3 collective-permute-start.6
  87.1 4.0 %collective-permute-start.7 = (f32[64,128]{1,0:T(8,128)S(1)}, f32[64,128]{1,0:T(8,128)S(1)}, u32[]{:S(2)}, u32[]{:S(2)}) collective-permute-start(f32[64,128]{1,0:T(8,128)S(1)} %get-tuple-element.60), channel_id=1, source_target_pairs={{0,8},{8,16},{16,24},{24,32},{32,40},{40,48},{48,56},{56,64},{64,7... | collective-permute-start | bytes 98312 | tf_op jit(solution)/shard_map/ppermute | solution.py:23
  91.1 1.9 %step.7 = (f32[1152,128]{1,0:T(8,128)S(1)}, f32[1024,128]{1,0:T(8,128)S(1)}) custom-call(s32[2]{0:T(128)S(1)} %pad_add_fusion.scal, f32[4608,128]{1,0:T(8,128)S(1)} %get-tuple-element.40.refs_0_, f32[64,128]{1,0:T(8,128)S(1)} %collective-permute-done.4.refs_1_, f32[64,128]{1,0:T(8,128)S(1)} %get-tuple-element.74.refs_2_, ...), custom_call_target="tpu_custom_call" | custom-call | flops 4000000000 | bytes 8000000 | tf_op jit(solution)/shard_map/step/pallas_call | solution.py:169
  93.0 0.7 finish.1
  93.7 4.5 %collective-permute-start.8 = (f32[4,512,128]{2,1,0:T(8,128)S(1)}, f32[4,512,128]{2,1,0:T(8,128)S(1)}, u32[]{:S(2)}, u32[]{:S(2)}) collective-permute-start(f32[4,512,128]{2,1,0:T(8,128)S(1)} %get-tuple-element.51), channel_id=1, source_target_pairs={{0,1},{1,0},{2,3},{3,2},{4,5},{5,4},{6,7},{7,6},{8,9},{9,8},{10,11... | collective-permute-start | bytes 3145736 | tf_op jit(solution)/shard_map/ppermute | solution.py:429
  98.2 2.3 %collective-permute-done.8.recv_ref = f32[4,512,128]{2,1,0:T(8,128)S(1)} collective-permute-done((f32[4,512,128]{2,1,0:T(8,128)S(1)}, f32[4,512,128]{2,1,0:T(8,128)S(1)}, u32[]{:S(2)}, u32[]{:S(2)}) %collective-permute-start.8) | collective-permute-done | bytes 1048608 | tf_op jit(solution)/shard_map/ppermute | solution.py:429
  100.5 3.0 %gram.1 = (f32[10,512,128]{2,1,0:T(8,128)S(1)}, f32[8,1,128]{2,1,0:T(1,128)S(1)}) custom-call(s32[2]{0:T(128)S(1)} %pad_add_fusion.scal, f32[2,512,128]{2,1,0:T(8,128)S(1)} %bitcast.29, f32[4,512,128]{2,1,0:T(8,128)S(1)} %get-tuple-element.50.keep_ref, f32[4,512,128]{2,1,0:T(8,128)S(1)} %collective-permute-done.8.recv_ref), custom_call_target="tpu_custom_call" | custom-call | tf_op jit(solution)/shard_map/gram/pallas_call | solution.py:430
  103.5 7.3 %all_to_all.15 = f32[8,1,128]{2,1,0:T(1,128)S(1)} all-to-all(f32[8,1,128]{2,1,0:T(1,128)S(1)} %get-tuple-element.52), channel_id=1, replica_groups=mesh['beam'=64,'trans'=8] {'trans'}, dimensions={0} | all-to-all | bytes 8192 | tf_op jit(solution)/shard_map/all_to_all | solution.py:440
  110.9 42.6 %all_to_all.16.gram_ref = f32[64,1,128]{2,1,0:T(1,128)S(1)} all-to-all(f32[64,1,128]{2,1,0:T(1,128)S(1)} %broadcast_in_dim.33), channel_id=1, replica_groups=mesh['beam'=64,'trans'=8] {'beam'}, dimensions={0} | all-to-all | bytes 65536 | tf_op jit(solution)/shard_map/all_to_all | solution.py:441
  153.5 5.3 %basis.1 = (f32[10,512,128]{2,1,0:T(8,128)}, f32[2,16,128]{2,1,0:T(8,128)S(1)}) custom-call(f32[64,1,128]{2,1,0:T(1,128)S(1)} %all_to_all.16.gram_ref, f32[10,512,128]{2,1,0:T(8,128)S(1)} %get-tuple-element.53.cols_ref), custom_call_target="tpu_custom_call" | custom-call | tf_op jit(solution)/shard_map/basis/pallas_call | solution.py:443
  (53 shorter events, 4.4 us)
Async XLA Ops:
  7.2 52.6 %all-gather.2.cloned.1.call-start = ((), (), s32[]{:S(2)}) async-start(), calls=%async_computation.3 | async-start | bytes 2359296 | tf_op jit(solution)/shard_map/all_gather | solution.py:333
  11.4 10.5 %copy-start.4 = (f32[64,64]{1,0:T(8,128)S(1)}, f32[64,64]{1,0:T(8,128)}, u32[]{:S(2)}) copy-start(f32[64,64]{1,0:T(8,128)} %param.9) | copy-start | bytes 49156
  11.4 10.6 %copy-start.2 = (f32[65,65]{1,0:T(8,128)S(1)}, f32[65,65]{1,0:T(8,128)}, u32[]{:S(2)}) copy-start(f32[65,65]{1,0:T(8,128)} %param.10) | copy-start | bytes 50704
  11.4 15.6 %copy-start.3 = (f32[64,64]{1,0:T(8,128)S(1)}, f32[64,64]{1,0:T(8,128)}, u32[]{:S(2)}) copy-start(f32[64,64]{1,0:T(8,128)} %param.8) | copy-start | bytes 49156
  11.4 45.3 %all-to-all-start = ((f32[8,512,128]{2,1,0:T(8,128)}), f32[8,512,128]{2,1,0:T(8,128)S(1)}, u32[]{:S(2)}, u32[]{:S(2)}) async-start(f32[8,512,128]{2,1,0:T(8,128)} %pad_maximum_fusion), calls=%async_computation | async-start | bytes 4194304 | tf_op jit(solution)/shard_map/all_to_all | solution.py:336
  57.1 7.7 %collective-permute-start.1 = (f32[64,128]{1,0:T(8,128)S(1)}, f32[64,128]{1,0:T(8,128)S(1)}, u32[]{:S(2)}, u32[]{:S(2)}) collective-permute-start(f32[64,128]{1,0:T(8,128)S(1)} %multiply_reduce_fusion), channel_id=1, source_target_pairs={{0,8},{8,16},{16,24},{24,32},{32,40},{40,48},{48,56},{56,64},{64,7... | collective-permute-start | bytes 98312 | tf_op jit(solution)/shard_map/ppermute | solution.py:23
  58.4 6.4 %collective-permute-start = (f32[64,128]{1,0:T(8,128)S(1)}, f32[64,128]{1,0:T(8,128)S(1)}, u32[]{:S(2)}, u32[]{:S(2)}) collective-permute-start(f32[64,128]{1,0:T(8,128)S(1)} %bitcast.32), channel_id=1, source_target_pairs={{8,0},{16,8},{24,16},{32,24},{40,32},{48,40},{56,48},{64,56},{72,6... | collective-permute-start | bytes 98312 | tf_op jit(solution)/shard_map/ppermute | solution.py:23
  59.9 1.6 copy-start.1
  66.7 9.7 %collective-permute-start.2 = (f32[64,128]{1,0:T(8,128)S(1)}, f32[64,128]{1,0:T(8,128)S(1)}, u32[]{:S(2)}, u32[]{:S(2)}) collective-permute-start(f32[64,128]{1,0:T(8,128)S(1)} %get-tuple-element.65), channel_id=1, source_target_pairs={{8,0},{16,8},{24,16},{32,24},{40,32},{48,40},{56,48},{64,56},{72,6... | collective-permute-start | bytes 98312 | tf_op jit(solution)/shard_map/ppermute | solution.py:23
  68.0 8.4 %collective-permute-start.3 = (f32[64,128]{1,0:T(8,128)S(1)}, f32[64,128]{1,0:T(8,128)S(1)}, u32[]{:S(2)}, u32[]{:S(2)}) collective-permute-start(f32[64,128]{1,0:T(8,128)S(1)} %get-tuple-element.64), channel_id=1, source_target_pairs={{0,8},{8,16},{16,24},{24,32},{32,40},{40,48},{48,56},{56,64},{64,7... | collective-permute-start | bytes 98312 | tf_op jit(solution)/shard_map/ppermute | solution.py:23
  76.5 9.3 %collective-permute-start.4 = (f32[64,128]{1,0:T(8,128)S(1)}, f32[64,128]{1,0:T(8,128)S(1)}, u32[]{:S(2)}, u32[]{:S(2)}) collective-permute-start(f32[64,128]{1,0:T(8,128)S(1)} %get-tuple-element.63), channel_id=1, source_target_pairs={{8,0},{16,8},{24,16},{32,24},{40,32},{48,40},{56,48},{64,56},{72,6... | collective-permute-start | bytes 98312 | tf_op jit(solution)/shard_map/ppermute | solution.py:23
  77.8 8.0 %collective-permute-start.5 = (f32[64,128]{1,0:T(8,128)S(1)}, f32[64,128]{1,0:T(8,128)S(1)}, u32[]{:S(2)}, u32[]{:S(2)}) collective-permute-start(f32[64,128]{1,0:T(8,128)S(1)} %get-tuple-element.62), channel_id=1, source_target_pairs={{0,8},{8,16},{16,24},{24,32},{32,40},{40,48},{48,56},{56,64},{64,7... | collective-permute-start | bytes 98312 | tf_op jit(solution)/shard_map/ppermute | solution.py:23
  85.8 7.2 %collective-permute-start.6 = (f32[64,128]{1,0:T(8,128)S(1)}, f32[64,128]{1,0:T(8,128)S(1)}, u32[]{:S(2)}, u32[]{:S(2)}) collective-permute-start(f32[64,128]{1,0:T(8,128)S(1)} %get-tuple-element.61), channel_id=1, source_target_pairs={{8,0},{16,8},{24,16},{32,24},{40,32},{48,40},{56,48},{64,56},{72,6... | collective-permute-start | bytes 98312 | tf_op jit(solution)/shard_map/ppermute | solution.py:23
  87.1 5.9 %collective-permute-start.7 = (f32[64,128]{1,0:T(8,128)S(1)}, f32[64,128]{1,0:T(8,128)S(1)}, u32[]{:S(2)}, u32[]{:S(2)}) collective-permute-start(f32[64,128]{1,0:T(8,128)S(1)} %get-tuple-element.60), channel_id=1, source_target_pairs={{0,8},{8,16},{16,24},{24,32},{32,40},{40,48},{48,56},{56,64},{64,7... | collective-permute-start | bytes 98312 | tf_op jit(solution)/shard_map/ppermute | solution.py:23
  93.0 7.5 %copy-start = (f32[2,8,64,128]{3,2,1,0:T(8,128)S(1)}, f32[2,8,64,128]{3,2,1,0:T(8,128)}, u32[]{:S(2)}) copy-start(f32[2,8,64,128]{3,2,1,0:T(8,128)} %param.7) | copy-start | bytes 1572868
  93.7 6.7 %collective-permute-start.8 = (f32[4,512,128]{2,1,0:T(8,128)S(1)}, f32[4,512,128]{2,1,0:T(8,128)S(1)}, u32[]{:S(2)}, u32[]{:S(2)}) collective-permute-start(f32[4,512,128]{2,1,0:T(8,128)S(1)} %get-tuple-element.51), channel_id=1, source_target_pairs={{0,1},{1,0},{2,3},{3,2},{4,5},{5,4},{6,7},{7,6},{8,9},{9,8},{10,11... | collective-permute-start | bytes 3145736 | tf_op jit(solution)/shard_map/ppermute | solution.py:429
Sparse Core Ops, SparseCore 0:
  10.1 45.0 all-gather.1

commit v2 on v1

--- a/solution.py
+++ b/solution.py
@@ -26,39 +26,13 @@
 PAD = 8
 
 
-def step_body(fix, with_prev, last, nx, nz, width, chip, strides, scal, *refs):
-    refs = list(refs)
-    cur_ref = refs.pop(0)
-    if fix:
-        pin_ref, bin_ref = refs.pop(0), refs.pop(0)
-    prev_ref = refs.pop(0) if with_prev else None
-    pot_ref, kz_ref, kx_ref, wy_ref, rcol_ref, wvec_ref = refs[:6]
-    refs = refs[6:]
-    out_ref = refs.pop(0)
-    if not last:
-        first_ref, bridge_ref = refs.pop(0), refs.pop(0)
-    rows_ref = refs.pop(0) if fix else None
-    col_ref = refs.pop(0)
-    cur_stride, prev_stride = strides
-    stride = nz + PAD
+def apply_local(nx, nz, width, refs, col, load, prev, halo, scale, out, bridge_ref):
+    pot_ref, kz_ref, kx_ref, wy_ref, wvec_ref = refs
+    col_ref, stride = col
+    out_ref, x_start, out_x = out
+    out_stride = nz + PAD
     half = width // 2
-    scale = 2.0 if with_prev else 1.0
     left = lax.broadcasted_iota(jnp.int32, (nz, width), 1) < half
-    top = lax.broadcasted_iota(jnp.int32, (8, width), 0) == 0
-    x_start = scal[0] if last else 0
-    out_x = chip if last else nx
-
-    def rows_of(x, step):
-        return pl.ds(pl.multiple_of(x * step, 8), nz)
-
-    def fixed(x):
-        u = cur_ref[rows_of(x, cur_stride), :]
-        if fix:
-            u = u + rcol_ref[...] * pin_ref[pl.ds(x, 1), :]
-            head = u[0:8] + jnp.where(top, bin_ref[pl.ds(x, 1), :], 0.0)
-            u = jnp.concatenate([head, u[8:]], axis=0)
-        col_ref[rows_of(x, stride), :] = u
-        return u
 
     def product(k_ref, us):
         parts = [split(u) for u in us]
@@ -74,12 +48,7 @@
         return outs, parts
 
     def local_four(x0):
-        us = []
-        for q in range(4):
-            if last:
-                us.append(col_ref[rows_of(x_start + x0 + q, stride), :])
-            else:
-                us.append(fixed(x0 + q))
+        us = [load(x_start + x0 + q) for q in range(4)]
         along_z, parts = product(kz_ref, us)
         along_y = jnp.dot(
             jnp.concatenate([jnp.concatenate(p, axis=1) for p in parts], axis=0),
@@ -87,57 +56,157 @@
             preferred_element_type=F32,
         )
         for q in range(4):
-            u = us[q]
             x = x_start + x0 + q
-            pv = pot_ref[rows_of(x, nz), :]
-            pr = pltpu.roll(pv, half, 1)
-            optical = jnp.where(left, pv, pr) * u + jnp.where(left, pr, -pv) * pltpu.roll(u, half, 1)
             ay = along_y[q * nz : (q + 1) * nz]
-            new = along_z[q] + ay[:, :width] + ay[:, width:] + scale * optical
-            if with_prev:
-                new = new - prev_ref[rows_of(x, prev_stride), :]
-            out_ref[rows_of(x0 + q, stride), :] = new
-
-    def repeat(count, unroll, body, carry):
-        unroll = min(unroll, count)
-
-        def some(i, carry):
-            for q in range(unroll):
-                carry = body(i * unroll + q, carry)
-            return carry
-
-        return lax.fori_loop(0, count // unroll, some, carry)
-
-    def only(body):
-        def with_carry(i, carry):
-            body(i)
-            return carry
-
-        return with_carry
-
-    if last:
-        repeat(nx, 16, only(fixed), 0)
+            new = along_z[q] + ay[:, :width] + ay[:, width:]
+            new = new + scale * optical(us[q], pot_ref[rows_of(x, nz, nz), :], left)
+            if prev is not None:
+                new = new - prev[0][rows_of(x, prev[1], nz), :]
+            if halo is not None:
+                new = with_halo(new, halo, x)
+            out_ref[rows_of(x0 + q, out_stride, nz), :] = new
+
     repeat(out_x // 4, 8, only(lambda i: local_four(i * 4)), 0)
-    if fix:
-        for q in range(chip):
-            rows_ref[q * nz : (q + 1) * nz, :] = col_ref[rows_of(scal[0] + q, stride), :]
 
     def across_four(i, bridge):
         z0 = i * 4
         us = [col_ref[pl.ds(z0 + q, nx, stride=stride), :] for q in range(4)]
         along_x, _ = product(kx_ref, us)
         for q in range(4):
-            at = pl.ds(z0 + q, out_x, stride=stride)
+            at = pl.ds(z0 + q, out_x, stride=out_stride)
             new = out_ref[at, :] + along_x[q]
             out_ref[at, :] = new
-            if not last:
+            if bridge_ref is not None:
                 bridge = bridge + wvec_ref[pl.ds(z0 + q, 1), :] * new
         return bridge
 
     bridge = repeat(nz // 4, 8, across_four, jnp.zeros((out_x, width), F32))
-    if not last:
+    if bridge_ref is not None:
         bridge_ref[...] = bridge
-        first_ref[...] = out_ref[pl.ds(0, nx, stride=stride), :]
+
+
+def rows_of(x, stride, nz):
+    return pl.ds(pl.multiple_of(x * stride, 8), nz)
+
+
+def optical(u, pot, left):
+    half = u.shape[-1] // 2
+    turned = pltpu.roll(pot, half, 1)
+    return jnp.where(left, pot, turned) * u + jnp.where(left, turned, -pot) * pltpu.roll(u, half, 1)
+
+
+def with_halo(u, halo, x):
+    column_ref, plane_ref, sum_ref = halo
+    top = lax.broadcasted_iota(jnp.int32, (8, u.shape[-1]), 0) == 0
+    u = u + column_ref[...] * plane_ref[pl.ds(x, 1), :]
+    head = u[0:8] + jnp.where(top, sum_ref[pl.ds(x, 1), :], 0.0)
+    return jnp.concatenate([head, u[8:]], axis=0)
+
+
+def repeat(count, unroll, body, carry):
+    unroll = min(unroll, count)
+
+    def some(i, carry):
+        for q in range(unroll):
+            carry = body(i * unroll + q, carry)
+        return carry
+
+    return lax.fori_loop(0, count // unroll, some, carry)
+
+
+def only(body):
+    def with_carry(i, carry):
+        body(i)
+        return carry
+
+    return with_carry
+
+
+def copies_body(packets_ref, sent_ref, sems):
+    npack = packets_ref.shape[0]
+    copies = [
+        pltpu.make_async_copy(packets_ref, sent_ref.at[pl.ds(i * npack, npack)], sems.at[i])
+        for i in range(sent_ref.shape[0] // npack)
+    ]
+    for copy in copies:
+        copy.start()
+    for copy in copies:
+        copy.wait()
+
+
+def planes_body(nz, packets_ref, pot_ref, wvec_ref, kvec_ref, mvec_ref, first_ref, bridge_ref, zrest_ref, brest_ref):
+    npack, size, width = packets_ref.shape
+    rows = size // nz
+    left = lax.broadcasted_iota(jnp.int32, (nz, width), 1) < width // 2
+    for p in range(npack):
+        for x in range(rows):
+            u = packets_ref[p, x * nz : (x + 1) * nz, :]
+            v = optical(u, pot_ref[x * nz : (x + 1) * nz, :], left)
+            at = slice(p * rows + x, p * rows + x + 1)
+            first_ref[at, :] = u[0:1]
+            bridge_ref[at, :] = jnp.sum(wvec_ref[...] * u, axis=0, keepdims=True)
+            zrest_ref[at, :] = v[0:1] + jnp.sum(kvec_ref[...] * u, axis=0, keepdims=True)
+            brest_ref[at, :] = jnp.sum(wvec_ref[...] * v + mvec_ref[...] * u, axis=0, keepdims=True)
+
+
+def pair_body(nx, nz, width, chip, scal, cur_ref, planes_ref, pot_ref, *refs):
+    kz1, kx1, wy1, kz2, kx2, wy2, kx_ref, ky_ref, rcol1, rcol2, wvec = refs[:11]
+    one_ref, two_ref, first_ref, bridge_ref, rows1_ref, rows2_ref, col_ref, halo_ref = refs[11:]
+    stride = nz + PAD
+
+    def packed(x):
+        u = cur_ref[rows_of(x, nz, nz), :]
+        col_ref[rows_of(x, stride, nz), :] = u
+        return u
+
+    precise = lax.Precision.HIGHEST
+    for q in range(2):
+        plane = planes_ref[q]
+        moved = jnp.dot(kx_ref[...], plane, precision=precise, preferred_element_type=F32)
+        moved = moved + jnp.dot(plane, ky_ref[...], precision=precise, preferred_element_type=F32)
+        moved = moved + planes_ref[2 + q]
+        halo_ref[q] = moved if q == 0 else 2.0 * moved
+    apply_local(
+        nx, nz, width, (pot_ref, kz1, kx1, wy1, wvec), (col_ref, stride), packed, None,
+        (rcol1, planes_ref.at[0], planes_ref.at[1]), 1.0, (one_ref, 0, nx), None,
+    )
+    apply_local(
+        nx, nz, width, (pot_ref, kz2, kx2, wy2, wvec), (one_ref, stride),
+        lambda x: one_ref[rows_of(x, stride, nz), :], (cur_ref, nz),
+        (rcol2, halo_ref.at[0], halo_ref.at[1]), 2.0, (two_ref, 0, nx), bridge_ref,
+    )
+    first_ref[...] = two_ref[pl.ds(0, nx, stride=stride), :]
+    for ref, rows_ref in ((one_ref, rows1_ref), (two_ref, rows2_ref)):
+        for q in range(chip):
+            rows_ref[q * nz : (q + 1) * nz, :] = ref[rows_of(scal[0] + q, stride, nz), :]
+
+
+def third_body(nx, nz, width, cur_ref, prev_ref, pot_ref, kz, kx, wy, wvec, out_ref, first_ref, bridge_ref):
+    stride = nz + PAD
+    apply_local(
+        nx, nz, width, (pot_ref, kz, kx, wy, wvec), (cur_ref, stride),
+        lambda x: cur_ref[rows_of(x, stride, nz), :], (prev_ref, stride), None, 2.0,
+        (out_ref, 0, nx), bridge_ref,
+    )
+    first_ref[...] = out_ref[pl.ds(0, nx, stride=stride), :]
+
+
+def fourth_body(nx, nz, width, chip, scal, cur_ref, pin_ref, bin_ref, prev_ref, pot_ref, *refs):
+    kz, kx, wy, wvec, rcol, out_ref, rows_ref, col_ref = refs
+    stride = nz + PAD
+
+    def complete(x):
+        u = with_halo(cur_ref[rows_of(x, stride, nz), :], (rcol, pin_ref, bin_ref), x)
+        col_ref[rows_of(x, stride, nz), :] = u
+
+    repeat(nx, 16, only(complete), 0)
+    for q in range(chip):
+        rows_ref[q * nz : (q + 1) * nz, :] = col_ref[rows_of(scal[0] + q, stride, nz), :]
+    apply_local(
+        nx, nz, width, (pot_ref, kz, kx, wy, wvec), (col_ref, stride),
+        lambda x: col_ref[rows_of(x, stride, nz), :], (prev_ref, stride), None, 2.0,
+        (out_ref, scal[0], chip), None,
+    )
 
 
 def vm():
@@ -148,34 +217,23 @@
     return pltpu.VMEM(shape, F32)
 
 
-def step(scal, cur, halo, prev, pot, kz, kx, wy, rcol, wvec, nx, nz, chip, last):
-    fix, with_prev = halo is not None, prev is not None
-    width = cur.shape[-1]
-    stride = nz + PAD
-    ins = [cur] + (list(halo) if fix else []) + ([prev] if with_prev else [])
-    ins += [pot, kz, kx, wy, rcol, wvec]
-    outs = [in_vmem((chip if last else nx) * stride, width)]
-    if not last:
-        outs += [in_vmem(nx, width), in_vmem(nx, width)]
-    if fix:
-        outs += [in_vmem(chip * nz, width)]
-    scratch = []
-    if fix and not last:
-        outs += [in_vmem(nx * stride, width)]
-    else:
-        scratch = [pltpu.VMEM((nx * stride, width), F32)]
-    strides = (cur.shape[0] // nx, prev.shape[0] // nx if with_prev else 0)
-    body = functools.partial(step_body, fix, with_prev, last, nx, nz, width, chip, strides)
+def call(name, body, outs, *ins, scal=None, scratch=(), cost=4):
+    specs = [vm()] * len(ins)
+    if scal is not None:
+        specs = [pl.BlockSpec(memory_space=pltpu.SMEM)] + specs
+        ins = (scal,) + ins
     return pl.pallas_call(
         body,
         out_shape=outs,
-        in_specs=[pl.BlockSpec(memory_space=pltpu.SMEM)] + [vm()] * len(ins),
+        in_specs=specs,
         out_specs=[vm()] * len(outs),
-        scratch_shapes=scratch,
+        scratch_shapes=list(scratch),
         compiler_params=pltpu.CompilerParams(vmem_limit_bytes=LIMIT),
-        cost_estimate=pl.CostEstimate(flops=4 * 10**9, bytes_accessed=8 * 10**6, transcendentals=0),
-        name="step",
-    )(scal, *ins)
+        cost_estimate=pl.CostEstimate(
+            flops=cost * 10**9, bytes_accessed=2 * cost * 10**6, transcendentals=0
+        ),
+        name=name,
+    )(*ins)
 
 
 def finish_body(nz, rows, scal, last_ref, pin_ref, bin_ref, rcol_ref, *refs):
@@ -330,15 +388,28 @@
     chip = 2 * rows
     scal = jnp.stack([(me // 2) * chip, core]).astype(jnp.int32)
 
-    pot = lax.all_gather(potential.reshape(rows * nz, width), "trans", axis=0, tiled=True)
-    sent = packets.reshape(npack, rows * nz, width)
-    sent = jnp.concatenate([sent] * (trans // npack), axis=0)
+    size = rows * nz
+    flat = packets.reshape(npack, size, width)
+    mine = potential.reshape(size, width)
+    pot = lax.all_gather(mine, "trans", axis=0, tiled=True)
+    sent = pl.pallas_call(
+        copies_body,
+        out_shape=jax.ShapeDtypeStruct((trans, size, width), F32),
+        in_specs=[vm()],
+        out_specs=pl.BlockSpec(memory_space=pl.ANY),
+        scratch_shapes=[pltpu.SemaphoreType.DMA((trans // npack,))],
+        compiler_params=pltpu.CompilerParams(vmem_limit_bytes=LIMIT),
+        name="copies",
+    )(flat)
     cur = lax.all_to_all(sent, "trans", 0, 0, tiled=True).reshape(nx * nz, width)
+    sent, flat_late, mine_late = lax.optimization_barrier((sent, flat, mine))
 
     corner = element_kinetic[nz, nz] * (lax.axis_index("beam") > 0).astype(F32)
     kz = element_kinetic[:nz, :nz].at[0, 0].add(corner)
     wrow = element_kinetic[nz, :nz]
     rcol = element_kinetic[:nz, nz]
+    mrow = jnp.sum(wrow[:, None] * kz, axis=0)
+    wr = jnp.sum(wrow * rcol)
 
     def parts_of(k):
         high = lax.reduce_precision(k, 8, 7)
@@ -355,7 +426,12 @@
             [jnp.concatenate([block, none], axis=1), jnp.concatenate([none, block], axis=1)], axis=0
         )
 
-    ky_high, ky_low = parts_of(jnp.kron(jnp.eye(2, dtype=F32), kinetic_y).T)
+    none = jnp.zeros_like(kinetic_y)
+    ky = jnp.concatenate(
+        [jnp.concatenate([kinetic_y.T, none], axis=1), jnp.concatenate([none, kinetic_y.T], axis=1)],
+        axis=0,
+    )
+    ky_high, ky_low = parts_of(ky)
     wy = jnp.concatenate(
         [
             jnp.concatenate([ky_high, ky_low], axis=1),
@@ -366,58 +442,50 @@
     kz1, kx1 = left_weights(kz), left_weights(kinetic_x)
     kz2, kx2, wy2 = kz1 * 2, kx1 * 2, wy * 2
     kx_last = left_weights(2.0 * lax.dynamic_slice_in_dim(kinetic_x, scal[0], chip, 0))
-    rcol1 = jnp.broadcast_to(rcol[:, None], (nz, width))
+
+    def wide(column):
+        return jnp.broadcast_to(column[:, None], (nz, width))
+
+    rcol1, wvec = wide(rcol), wide(wrow)
     rcol2 = rcol1 * 2.0
-    wvec = jnp.broadcast_to(wrow[:, None], (nz, width))
-
-    def halo(first, bridge, pin, bin_, scale):
-        if pin is not None:
-            bridge = bridge + (scale * jnp.dot(wrow, rcol, precision="highest")) * pin
-            bridge = bridge + (scale * wrow[0]) * bin_
-            first = first + (scale * rcol[0]) * pin + scale * bin_
-        return passed(first, -1), passed(bridge, 1)
-
-    whole = cur.reshape(nx, nz, width)
-    halos = [halo(whole[:, 0], jnp.sum(whole * wvec, axis=1), None, None, 1.0)]
-    columns = []
-    prev = None
-    local, first, bridge = step(
-        scal, cur, None, None, pot, kz1, kx1, wy, rcol1, wvec, nx, nz, chip, False
-    )
-    prev = cur
-    for k in range(1, POWERS):
-        scale = 1.0 if k == 1 else 2.0
-        pin, bin_ = halos[-1]
-        fresh = halo(first, bridge, pin, bin_, scale)
-        last = k == POWERS - 1
-        got = step(
-            scal,
-            local,
-            (pin, scale * bin_),
-            prev,
-            pot,
-            kz2,
-            kx_last if last else kx2,
-            wy2,
-            rcol1 if k == 1 else rcol2,
-            wvec,
-            nx,
-            nz,
-            chip,
-            last,
-        )
-        if last:
-            local, col_rows = got
-        else:
-            prev_next = got[4]
-            local, first, bridge, col_rows = got[:4]
-            prev = prev_next
-        columns.append(col_rows)
-        halos.append(fresh)
-    pin, bin_ = halos[-1]
-    pin = lax.dynamic_slice_in_dim(pin, scal[0], chip, 0)
-    bin_ = lax.dynamic_slice_in_dim(2.0 * bin_, scal[0], chip, 0)
-    size = rows * nz
+
+    plane = in_vmem(npack * rows, width)
+    first, bridge, zrest, brest = call(
+        "planes", functools.partial(planes_body, nz), [plane] * 4,
+        flat_late, mine_late, wvec, wide(kz[0]), wide(mrow), cost=1,
+    )
+    pin, bin_ = passed(first, -1), passed(bridge, 1)
+    pnext = passed(zrest + rcol[0] * pin + bin_, -1)
+    bnext = passed(brest + wr * pin + wrow[0] * bin_, 1)
+    planes = jnp.stack([pin, bin_, pnext, bnext])
+    planes = lax.all_gather(planes, "trans").reshape(trans, 4, npack, rows, width)
+    planes = lax.dynamic_index_in_dim(planes, core, 2, keepdims=False)
+    planes = planes.transpose(1, 0, 2, 3).reshape(4, nx, width)
+
+    full, edge = in_vmem(nx * (nz + PAD), width), in_vmem(nx, width)
+    here = in_vmem(chip * nz, width)
+    col1, col2, first, bridge, rows1, rows2 = call(
+        "pair", functools.partial(pair_body, nx, nz, width, chip), [full, full, edge, edge, here, here],
+        cur, planes, pot, kz1, kx1, wy, kz2, kx2, wy2, kinetic_x, ky, rcol1, rcol2, wvec,
+        scal=scal, scratch=[full, in_vmem(2, nx, width)], cost=8,
+    )
+    pin, bin_ = passed(first, -1), 2.0 * passed(bridge, 1)
+    col3, first, bridge = call(
+        "third", functools.partial(third_body, nx, nz, width), [full, edge, edge],
+        col2, col1, pot, kz2, kx2, wy2, wvec,
+    )
+    first = first + (2.0 * rcol[0]) * pin + bin_
+    bridge = bridge + (2.0 * wr) * pin + wrow[0] * bin_
+    plast, blast = passed(first, -1), 2.0 * passed(bridge, 1)
+    local, rows3 = call(
+        "fourth", functools.partial(fourth_body, nx, nz, width, chip),
+        [in_vmem(chip * (nz + PAD), width), here],
+        col3, pin, bin_, col2, pot, kz2, kx_last, wy2, wvec, rcol2,
+        scal=scal, scratch=[full], cost=2,
+    )
+    columns = [rows1, rows2, rows3]
+    pin = lax.dynamic_slice_in_dim(plast, scal[0], chip, 0)
+    bin_ = lax.dynamic_slice_in_dim(blast, scal[0], chip, 0)
     keep, send = pl.pallas_call(
         functools.partial(finish_body, nz, rows),
         out_shape=[in_vmem(POWERS, size, width)] * 2,

time: 167 us -> 160 us (0.958)
  waiting for transfers between devices: 32.3 us -> 2.97 us
  blocking collectives: 49.9 us -> 63.2 us
  local copies, waits for them, and re-layouts: 3.58 us -> 11.3 us
    all_to_all x1, waiting for transfers between devices: 29.3 us -> 0.01 us  [shards(): lax.all_to_all(sent, 'trans', 0, 0, tiled=True).reshape(nx * nz, width)]
    all_gather x0 -> x1, blocking collectives: none -> 19.6 us  [shards(): lax.all_gather(planes, 'trans').reshape(trans, 4, npack, rows, width)]
    all_to_all x1, blocking collectives: 42.6 us -> 35.5 us  [shards(): lax.all_to_all(jnp.broadcast_to(gram, (beam, 1, width)), 'beam', 0, 0, ti...]
    unnamed x12 -> x36, local copies, waits for them, and re-layouts: 2.3 us -> 9.32 us
    concatenate x1, other arithmetic: 3.47 us -> 0.72 us  [shards(): jnp.concatenate([jnp.concatenate([kinetic_y.T, none], axis=1), jnp.concat...]
    ppermute x8, starting transfers between devices: 19 us -> 21.1 us  [passed(): lax.ppermute(x, 'beam', [(i, i + by) for i in range(peers) if 0 <= i + by...]
    pallas_call x4 -> x5, Pallas kernels: 12.9 us -> 13.9 us  [the longest x4 12.5 us: call(): pl.pallas_call(body, out_shape=outs, in_specs=specs, out_specs=[vm()] * l...]
  transfers between devices with their start and end apart: 11 -> 11, of which waited for: 2 -> 1; matrix products, arithmetic and copies ran while one was open for 4% -> 5% of each run, Pallas kernels for 8% -> 4%
where the time goes in v2:
time: 160 us; the launch traced here: 159 us
  blocking collectives  63.2 us (40%)
  starting transfers between devices  34.9 us (22%)
  Pallas kernels  22.9 us (14%)
  between operations  17.7 us (11%)
  local copies, waits for them, and re-layouts  11.3 us (7%)
  other arithmetic  6.43 us (4%)
  waiting for transfers between devices  2.97 us (2%)
    all_to_all x1, blocking collectives, shards(): lax.all_to_all(jnp.broadcast_to(gram, (beam, 1, width)), 'beam', 0, 0, ti...  35.5 us
    ppermute x8, starting transfers between devices, passed(): lax.ppermute(x, 'beam', [(i, i + by) for i in range(peers) if 0 <= i + by...  21.1 us
    all_gather x1, blocking collectives, shards(): lax.all_gather(planes, 'trans').reshape(trans, 4, npack, rows, width)  19.6 us
    pallas_call x4, Pallas kernels, call(): pl.pallas_call(body, out_shape=outs, in_specs=specs, out_specs=[vm()] * l...  12.5 us
    all_to_all x1, starting transfers between devices, shards(): lax.all_to_all(sent, 'trans', 0, 0, tiled=True).reshape(nx * nz, width)  10.5 us
    unnamed x36, local copies, waits for them, and re-layouts  9.32 us
    all_to_all x1, blocking collectives, shards(): lax.all_to_all(gram, 'trans', 0, 0, tiled=True)  8.08 us
    pallas_call x1, Pallas kernels, shards(): pl.pallas_call(functools.partial(basis_body, cells, rows), out_shape=[jax...  5.32 us
  transfers between devices with their start and end apart: 11, of which 1 were waited for; matrix products, arithmetic and copies ran while one was open for 5% of the time, Pallas kernels for 4%

profile of v2, /device:TPU:1, one launch (start us, length us, event | category | flops | bytes accessed | tf_op | source)
XLA Modules:
  0.0 159.4 jit_solution(11183494972856629122)
XLA Ops:
  7.9 1.0 copy-done
  8.9 1.3 copies.1
  10.3 10.5 %all-to-all-start = ((f32[8,512,128]{2,1,0:T(8,128)}), f32[8,512,128]{2,1,0:T(8,128)S(1)}, u32[]{:S(2)}, u32[]{:S(2)}) async-start(f32[8,512,128]{2,1,0:T(8,128)} %copies.1), calls=%async_computation | async-start | bytes 4194304 | tf_op jit(solution)/shard_map/all_to_all | solution.py:404
  23.7 1.3 collective-permute-start
  25.0 4.0 %collective-permute-start.1 = (f32[16,128]{1,0:T(8,128)S(1)}, f32[16,128]{1,0:T(8,128)S(1)}, u32[]{:S(2)}, u32[]{:S(2)}) collective-permute-start(f32[16,128]{1,0:T(8,128)S(1)} %get-tuple-element.40), channel_id=1, source_target_pairs={{0,8},{8,16},{16,24},{24,32},{32,40},{40,48},{48,56},{56,64},{64,7... | collective-permute-start | bytes 24584 | tf_op jit(solution)/shard_map/ppermute | solution.py:23
  31.7 1.3 broadcast_multiply_fusion.4
  33.6 1.9 %add_add_fusion.1 = (f32[16,128]{1,0:T(8,128)S(1)}, f32[16,128]{1,0:T(8,128)S(1)}) fusion(f32[16,128]{1,0:T(8,128)S(1)} %collective-permute-done.1, f32[16,128]{1,0:T(8,128)S(1)} %get-tuple-element.41, f32[16,128]{1,0:T(8,128)S(1)} %collective-permute-done, f32[]{:T(128)} %bitcast.11, f32[]{:T(128)} %bitcast.13, f32[16,128]{1,0:T(8,128)S(1)} %get-tuple-element.42, ...), kind=kLoop, calls=%fused_computation.50 | loop fusion | flops 14336 | bytes 49164 | tf_op jit(solution)/shard_map/add | solution.py:458
  35.5 1.3 collective-permute-start.2
  36.8 4.0 %collective-permute-start.3 = (f32[16,128]{1,0:T(8,128)S(1)}, f32[16,128]{1,0:T(8,128)S(1)}, u32[]{:S(2)}, u32[]{:S(2)}) collective-permute-start(f32[16,128]{1,0:T(8,128)S(1)} %get-tuple-element.90), channel_id=1, source_target_pairs={{0,8},{8,16},{16,24},{24,32},{32,40},{40,48},{48,56},{56,64},{64,7... | collective-permute-start | bytes 24584 | tf_op jit(solution)/shard_map/ppermute | solution.py:23
  42.8 19.6 %all-gather = f32[32,16,128]{2,1,0:T(8,128)S(1)} all-gather(f32[4,16,128]{2,1,0:T(8,128)S(1)} %pad_maximum_fusion), channel_id=2, replica_groups=mesh['beam'=64,'trans'=8] {'trans'}, dimensions={0}, use_global_device_ids=true | all-gather | bytes 294912 | tf_op jit(solution)/shard_map/all_gather | solution.py:461
  69.3 1.6 copy-done.14
  70.8 7.2 %pair.1 = (f32[4608,128]{1,0:T(8,128)S(1)}, f32[4608,128]{1,0:T(8,128)S(1)}, f32[64,128]{1,0:T(8,128)S(1)}, f32[64,128]{1,0:T(8,128)S(1)}, f32[1024,128]{1,0:T(8,128)S(1)}, /*index=5*/f32[1024,128]{1,0:T(8,128)S(1)}) custom-call(s32[2]{0:T(128)S(1)} %pad_add_fusion.scal, f32[4096,128]{1,0:T(8,128)S(1)} %bitcast.29, f32[4,64,128]{2,1,0:T(8,128)S(1)} %copy-done.7, ...), custom_call_target="tpu_custom_call" | custom-call | flops 8000000000 | bytes 16000000 | tf_op jit(solution)/shard_map/pair/pallas_call | solution.py:225
  78.0 1.3 collective-permute-start.4
  79.3 4.0 %collective-permute-start.5 = (f32[64,128]{1,0:T(8,128)S(1)}, f32[64,128]{1,0:T(8,128)S(1)}, u32[]{:S(2)}, u32[]{:S(2)}) collective-permute-start(f32[64,128]{1,0:T(8,128)S(1)} %get-tuple-element.47), channel_id=1, source_target_pairs={{0,8},{8,16},{16,24},{24,32},{32,40},{40,48},{48,56},{56,64},{64,7... | collective-permute-start | bytes 98312 | tf_op jit(solution)/shard_map/ppermute | solution.py:23
  83.4 3.1 %third.1 = (f32[4608,128]{1,0:T(8,128)S(1)}, f32[64,128]{1,0:T(8,128)S(1)}, f32[64,128]{1,0:T(8,128)S(1)}) custom-call(f32[4608,128]{1,0:T(8,128)S(1)} %get-tuple-element.43.cur_ref.prev_ref, f32[4608,128]{1,0:T(8,128)S(1)} %get-tuple-element.44.prev_ref, f32[4096,128]{1,0:T(8,128)S(1)} %copy-done.14, bf16[256,256]{1,0:T(8,128)(2,1)S(1)} %copy-done.5, ...), custom_call_target="tpu_custom_call" | custom-call | flops 4000000000 | bytes 8000000 | tf_op jit(solution)/shard_map/third/pallas_call | solution.py:225
  86.5 1.3 collective-permute-start.6
  87.8 4.0 %collective-permute-start.7 = (f32[64,128]{1,0:T(8,128)S(1)}, f32[64,128]{1,0:T(8,128)S(1)}, u32[]{:S(2)}, u32[]{:S(2)}) collective-permute-start(f32[64,128]{1,0:T(8,128)S(1)} %get-tuple-element.66), channel_id=1, source_target_pairs={{0,8},{8,16},{16,24},{24,32},{32,40},{40,48},{48,56},{56,64},{64,7... | collective-permute-start | bytes 98312 | tf_op jit(solution)/shard_map/ppermute | solution.py:23
  91.8 1.9 %fourth.1 = (f32[1152,128]{1,0:T(8,128)S(1)}, f32[1024,128]{1,0:T(8,128)S(1)}) custom-call(s32[2]{0:T(128)S(1)} %pad_add_fusion.scal, f32[4608,128]{1,0:T(8,128)S(1)} %get-tuple-element.45.cur_ref, f32[64,128]{1,0:T(8,128)S(1)} %collective-permute-done.4.pin_ref, f32[64,128]{1,0:T(8,128)S(1)} %get-tuple-element.74.bin_ref, ...), custom_call_target="tpu_custom_call" | custom-call | flops 2000000000 | bytes 4000000 | tf_op jit(solution)/shard_map/fourth/pallas_call | solution.py:225
  94.5 3.2 %collective-permute-start.8 = (f32[4,512,128]{2,1,0:T(8,128)S(1)}, f32[4,512,128]{2,1,0:T(8,128)S(1)}, u32[]{:S(2)}, u32[]{:S(2)}) collective-permute-start(f32[4,512,128]{2,1,0:T(8,128)S(1)} %get-tuple-element.55), channel_id=1, source_target_pairs={{0,1},{1,0},{2,3},{3,2},{4,5},{5,4},{6,7},{7,6},{8,9},{9,8},{10,11... | collective-permute-start | bytes 3145736 | tf_op jit(solution)/shard_map/ppermute | solution.py:497
  97.7 2.3 %collective-permute-done.8.recv_ref = f32[4,512,128]{2,1,0:T(8,128)S(1)} collective-permute-done((f32[4,512,128]{2,1,0:T(8,128)S(1)}, f32[4,512,128]{2,1,0:T(8,128)S(1)}, u32[]{:S(2)}, u32[]{:S(2)}) %collective-permute-start.8) | collective-permute-done | bytes 1048608 | tf_op jit(solution)/shard_map/ppermute | solution.py:497
  99.9 3.0 %gram.1 = (f32[10,512,128]{2,1,0:T(8,128)S(1)}, f32[8,1,128]{2,1,0:T(1,128)S(1)}) custom-call(s32[2]{0:T(128)S(1)} %pad_add_fusion.scal, f32[2,512,128]{2,1,0:T(8,128)S(1)} %bitcast.32, f32[4,512,128]{2,1,0:T(8,128)S(1)} %get-tuple-element.54.keep_ref, f32[4,512,128]{2,1,0:T(8,128)S(1)} %collective-permute-done.8.recv_ref), custom_call_target="tpu_custom_call" | custom-call | tf_op jit(solution)/shard_map/gram/pallas_call | solution.py:498
  103.0 8.1 %all_to_all.15 = f32[8,1,128]{2,1,0:T(1,128)S(1)} all-to-all(f32[8,1,128]{2,1,0:T(1,128)S(1)} %get-tuple-element.56), channel_id=1, replica_groups=mesh['beam'=64,'trans'=8] {'trans'}, dimensions={0} | all-to-all | bytes 8192 | tf_op jit(solution)/shard_map/all_to_all | solution.py:508
  111.1 35.5 %all_to_all.16.gram_ref = f32[64,1,128]{2,1,0:T(1,128)S(1)} all-to-all(f32[64,1,128]{2,1,0:T(1,128)S(1)} %broadcast_in_dim.43), channel_id=1, replica_groups=mesh['beam'=64,'trans'=8] {'beam'}, dimensions={0} | all-to-all | bytes 65536 | tf_op jit(solution)/shard_map/all_to_all | solution.py:509
  146.6 5.3 %basis.1 = (f32[10,512,128]{2,1,0:T(8,128)}, f32[2,16,128]{2,1,0:T(8,128)S(1)}) custom-call(f32[64,1,128]{2,1,0:T(1,128)S(1)} %all_to_all.16.gram_ref, f32[10,512,128]{2,1,0:T(8,128)S(1)} %get-tuple-element.57.cols_ref), custom_call_target="tpu_custom_call" | custom-call | tf_op jit(solution)/shard_map/basis/pallas_call | solution.py:511
  (77 shorter events, 13.7 us)
Async XLA Ops:
  7.2 56.0 %all-gather.3.cloned.1.call-start = ((), (), s32[]{:S(2)}) async-start(), calls=%async_computation.3 | async-start | bytes 2359296 | tf_op jit(solution)/shard_map/all_gather | solution.py:394
  7.9 1.0 copy-start
  10.3 10.6 %copy-start.15 = (f32[65,65]{1,0:T(8,128)S(1)}, f32[65,65]{1,0:T(8,128)}, u32[]{:S(2)}) copy-start(f32[65,65]{1,0:T(8,128)} %param.10) | copy-start | bytes 50704
  10.3 13.0 %copy-start.1 = (f32[2,8,64,128]{3,2,1,0:T(8,128)S(1)}, f32[2,8,64,128]{3,2,1,0:T(8,128)}, u32[]{:S(2)}) copy-start(f32[2,8,64,128]{3,2,1,0:T(8,128)} %param.7) | copy-start | bytes 1572868
  10.3 13.0 %copy-start.2 = (f32[8,64,128]{2,1,0:T(8,128)S(1)}, f32[8,64,128]{2,1,0:T(8,128)}, u32[]{:S(2)}) copy-start(f32[8,64,128]{2,1,0:T(8,128)} %param.11) | copy-start | bytes 786436
  10.3 52.8 %all-to-all-start = ((f32[8,512,128]{2,1,0:T(8,128)}), f32[8,512,128]{2,1,0:T(8,128)S(1)}, u32[]{:S(2)}, u32[]{:S(2)}) async-start(f32[8,512,128]{2,1,0:T(8,128)} %copies.1), calls=%async_computation | async-start | bytes 4194304 | tf_op jit(solution)/shard_map/all_to_all | solution.py:404
  20.9 8.2 %copy-start.9 = (f32[64,64]{1,0:T(8,128)S(1)}, f32[64,64]{1,0:T(8,128)}, u32[]{:S(2)}) copy-start(f32[64,64]{1,0:T(8,128)} %refs_6_.1) | copy-start | bytes 49156
  20.9 8.3 %copy-start.16 = (f32[64,64]{1,0:T(8,128)S(1)}, f32[64,64]{1,0:T(8,128)}, u32[]{:S(2)}) copy-start(f32[64,64]{1,0:T(8,128)} %param.9) | copy-start | bytes 49156
  23.3 8.4 %copy-start.12 = (f32[64,128]{1,0:T(8,128)}, f32[64,128]{1,0:T(8,128)S(1)}, u32[]{:S(2)}) copy-start(f32[64,128]{1,0:T(8,128)S(1)} %broadcast_in_dim.17.wvec_ref.refs_10_.wvec.refs_3_) | copy-start | bytes 98308
  23.7 9.9 %collective-permute-start = (f32[16,128]{1,0:T(8,128)S(1)}, f32[16,128]{1,0:T(8,128)S(1)}, u32[]{:S(2)}, u32[]{:S(2)}) collective-permute-start(f32[16,128]{1,0:T(8,128)S(1)} %get-tuple-element.39), channel_id=1, source_target_pairs={{8,0},{16,8},{24,16},{32,24},{40,32},{48,40},{56,48},{64,56},{72,6... | collective-permute-start | bytes 24584 | tf_op jit(solution)/shard_map/ppermute | solution.py:23
  25.0 8.6 %collective-permute-start.1 = (f32[16,128]{1,0:T(8,128)S(1)}, f32[16,128]{1,0:T(8,128)S(1)}, u32[]{:S(2)}, u32[]{:S(2)}) collective-permute-start(f32[16,128]{1,0:T(8,128)S(1)} %get-tuple-element.40), channel_id=1, source_target_pairs={{0,8},{8,16},{16,24},{24,32},{32,40},{40,48},{48,56},{56,64},{64,7... | collective-permute-start | bytes 24584 | tf_op jit(solution)/shard_map/ppermute | solution.py:23
  35.5 7.3 %collective-permute-start.2 = (f32[16,128]{1,0:T(8,128)S(1)}, f32[16,128]{1,0:T(8,128)S(1)}, u32[]{:S(2)}, u32[]{:S(2)}) collective-permute-start(f32[16,128]{1,0:T(8,128)S(1)} %get-tuple-element.89), channel_id=1, source_target_pairs={{8,0},{16,8},{24,16},{32,24},{40,32},{48,40},{56,48},{64,56},{72,6... | collective-permute-start | bytes 24584 | tf_op jit(solution)/shard_map/ppermute | solution.py:23
  36.8 6.0 %collective-permute-start.3 = (f32[16,128]{1,0:T(8,128)S(1)}, f32[16,128]{1,0:T(8,128)S(1)}, u32[]{:S(2)}, u32[]{:S(2)}) collective-permute-start(f32[16,128]{1,0:T(8,128)S(1)} %get-tuple-element.90), channel_id=1, source_target_pairs={{0,8},{8,16},{16,24},{24,32},{32,40},{40,48},{48,56},{56,64},{64,7... | collective-permute-start | bytes 24584 | tf_op jit(solution)/shard_map/ppermute | solution.py:23
  63.3 0.9 copy-start.3
  64.2 0.9 copy-start.4
  65.1 0.9 copy-start.6
  69.2 1.6 copy-start.14
  70.8 12.5 %copy-start.5 = (bf16[256,256]{1,0:T(8,128)(2,1)S(1)}, bf16[256,256]{1,0:T(8,128)(2,1)}, u32[]{:S(2)}) copy-start(bf16[256,256]{1,0:T(8,128)(2,1)} %get-tuple-element.82.refs_3_.kz.refs_0_) | copy-start | bytes 393220
  78.0 8.4 %collective-permute-start.4 = (f32[64,128]{1,0:T(8,128)S(1)}, f32[64,128]{1,0:T(8,128)S(1)}, u32[]{:S(2)}, u32[]{:S(2)}) collective-permute-start(f32[64,128]{1,0:T(8,128)S(1)} %get-tuple-element.46), channel_id=1, source_target_pairs={{8,0},{16,8},{24,16},{32,24},{40,32},{48,40},{56,48},{64,56},{72,6... | collective-permute-start | bytes 98312 | tf_op jit(solution)/shard_map/ppermute | solution.py:23
  79.3 7.1 %collective-permute-start.5 = (f32[64,128]{1,0:T(8,128)S(1)}, f32[64,128]{1,0:T(8,128)S(1)}, u32[]{:S(2)}, u32[]{:S(2)}) collective-permute-start(f32[64,128]{1,0:T(8,128)S(1)} %get-tuple-element.47), channel_id=1, source_target_pairs={{0,8},{8,16},{16,24},{24,32},{32,40},{40,48},{48,56},{56,64},{64,7... | collective-permute-start | bytes 98312 | tf_op jit(solution)/shard_map/ppermute | solution.py:23
  83.3 8.5 %copy-start.11 = (bf16[64,256]{1,0:T(8,128)(2,1)S(1)}, bf16[64,256]{1,0:T(8,128)(2,1)}, u32[]{:S(2)}) copy-start(bf16[64,256]{1,0:T(8,128)(2,1)} %fusion.15.refs_1_) | copy-start | bytes 98308
  86.5 7.2 %collective-permute-start.6 = (f32[64,128]{1,0:T(8,128)S(1)}, f32[64,128]{1,0:T(8,128)S(1)}, u32[]{:S(2)}, u32[]{:S(2)}) collective-permute-start(f32[64,128]{1,0:T(8,128)S(1)} %get-tuple-element.67), channel_id=1, source_target_pairs={{8,0},{16,8},{24,16},{32,24},{40,32},{48,40},{56,48},{64,56},{72,6... | collective-permute-start | bytes 98312 | tf_op jit(solution)/shard_map/ppermute | solution.py:23
  87.8 5.9 %collective-permute-start.7 = (f32[64,128]{1,0:T(8,128)S(1)}, f32[64,128]{1,0:T(8,128)S(1)}, u32[]{:S(2)}, u32[]{:S(2)}) collective-permute-start(f32[64,128]{1,0:T(8,128)S(1)} %get-tuple-element.66), channel_id=1, source_target_pairs={{0,8},{8,16},{16,24},{24,32},{32,40},{40,48},{48,56},{56,64},{64,7... | collective-permute-start | bytes 98312 | tf_op jit(solution)/shard_map/ppermute | solution.py:23
  94.5 5.5 %collective-permute-start.8 = (f32[4,512,128]{2,1,0:T(8,128)S(1)}, f32[4,512,128]{2,1,0:T(8,128)S(1)}, u32[]{:S(2)}, u32[]{:S(2)}) collective-permute-start(f32[4,512,128]{2,1,0:T(8,128)S(1)} %get-tuple-element.55), channel_id=1, source_target_pairs={{0,1},{1,0},{2,3},{3,2},{4,5},{5,4},{6,7},{7,6},{8,9},{9,8},{10,11... | collective-permute-start | bytes 3145736 | tf_op jit(solution)/shard_map/ppermute | solution.py:497
  (4 other events, 3.3 us)
Sparse Core Ops, SparseCore 0:
  10.1 47.3 all-gather.2

commit v3 on v2

--- a/solution.py
+++ b/solution.py
@@ -26,7 +26,7 @@
 PAD = 8
 
 
-def apply_local(nx, nz, width, refs, col, load, prev, halo, scale, out, bridge_ref):
+def apply_local(nx, nz, width, refs, col, load, prev, halo, scale, out, bridge_ref, ready=None):
     pot_ref, kz_ref, kx_ref, wy_ref, wvec_ref = refs
     col_ref, stride = col
     out_ref, x_start, out_x = out
@@ -66,7 +66,12 @@
                 new = with_halo(new, halo, x)
             out_ref[rows_of(x0 + q, out_stride, nz), :] = new
 
-    repeat(out_x // 4, 8, only(lambda i: local_four(i * 4)), 0)
+    if ready is None:
+        repeat(out_x // 4, 8, only(lambda i: local_four(i * 4)), 0)
+    else:
+        for h in range(2):
+            ready(h)
+            repeat(out_x // 8, 8, only(lambda i, h=h: local_four((h * out_x // 8 + i) * 4)), 0)
 
     def across_four(i, bridge):
         z0 = i * 4
@@ -96,10 +101,10 @@
 
 
 def with_halo(u, halo, x):
-    column_ref, plane_ref, sum_ref = halo
+    column_ref, plane_ref, sum_ref, scale = halo
     top = lax.broadcasted_iota(jnp.int32, (8, u.shape[-1]), 0) == 0
-    u = u + column_ref[...] * plane_ref[pl.ds(x, 1), :]
-    head = u[0:8] + jnp.where(top, sum_ref[pl.ds(x, 1), :], 0.0)
+    u = u + column_ref[...] * (scale * plane_ref[pl.ds(x, 1), :])
+    head = u[0:8] + jnp.where(top, scale * sum_ref[pl.ds(x, 1), :], 0.0)
     return jnp.concatenate([head, u[8:]], axis=0)
 
 
@@ -149,31 +154,129 @@
             brest_ref[at, :] = jnp.sum(wvec_ref[...] * v + mvec_ref[...] * u, axis=0, keepdims=True)
 
 
-def pair_body(nx, nz, width, chip, scal, cur_ref, planes_ref, pot_ref, *refs):
-    kz1, kx1, wy1, kz2, kx2, wy2, kx_ref, ky_ref, rcol1, rcol2, wvec = refs[:11]
-    one_ref, two_ref, first_ref, bridge_ref, rows1_ref, rows2_ref, col_ref, halo_ref = refs[11:]
+def element_matrix(scal, ek):
+    nz = ek.shape[0] - 1
+    r = lax.broadcasted_iota(jnp.int32, (nz, nz), 0)
+    c = lax.broadcasted_iota(jnp.int32, (nz, nz), 1)
+    corner = (r == 0) & (c == 0) & (scal[2] > 0)
+    return ek[0:nz, 0:nz] + jnp.where(corner, ek[nz : nz + 1, nz : nz + 1], 0.0)
+
+
+def vectors_body(scal, ek_ref, rcol, kvec, mvec, coef):
+    nz, width = rcol.shape
+    kz = element_matrix(scal, ek_ref)
+    edge_vectors(ek_ref, rcol, coef)
+    kvec[...] = jnp.broadcast_to(kz[:, 0:1], (nz, width))
+    bridge = ek_ref[nz : nz + 1, 0:nz]
+    mvec[...] = jnp.broadcast_to(jnp.sum(kz * bridge, axis=1, keepdims=True), (nz, width))
+
+
+def edge_vectors(ek_ref, rcol, coef):
+    nz, width = rcol.shape
+    rcol[...] = jnp.broadcast_to(ek_ref[0:nz, nz : nz + 1], (nz, width))
+    coef[...] = jnp.zeros_like(coef)
+    coef[0:1, :] = rcol[0:1, :]
+    coef[1:2, :] = jnp.sum(rcol[...] * rcol[...], axis=0, keepdims=True)
+
+
+def matrices(scal, kx_ref, ky_ref, ek_ref, kz1, kx1, wy1, kz2, kx2, wy2, kx4, kyd):
+    chip = kx4.shape[0] // 4
+
+    def split_wide(k):
+        high = k.astype(BF16).astype(F32)
+        return high, k - high
+
+    def left_weights(k):
+        high, low = split_wide(k)
+        none = jnp.zeros_like(high)
+        block = jnp.concatenate(
+            [jnp.concatenate([high, high], axis=1), jnp.concatenate([low, none], axis=1)], axis=0
+        )
+        none = jnp.zeros_like(block)
+        return jnp.concatenate(
+            [jnp.concatenate([block, none], axis=1), jnp.concatenate([none, block], axis=1)], axis=0
+        )
+
+    for one, two, k in ((kz1, kz2, element_matrix(scal, ek_ref)), (kx1, kx2, kx_ref[...])):
+        block = left_weights(k)
+        one[...] = block.astype(BF16)
+        two[...] = (2.0 * block).astype(BF16)
+    kx4[...] = left_weights(2.0 * kx_ref[pl.ds(pl.multiple_of(scal[0], 8), chip), :]).astype(BF16)
+    ky = ky_ref[...]
+    none = jnp.zeros_like(ky)
+    ky = jnp.concatenate(
+        [jnp.concatenate([ky, none], axis=1), jnp.concatenate([none, ky], axis=1)], axis=0
+    )
+    kyd[...] = ky
+    high, low = split_wide(ky)
+    block = jnp.concatenate(
+        [jnp.concatenate([high, low], axis=1), jnp.concatenate([high, jnp.zeros_like(low)], axis=1)],
+        axis=0,
+    )
+    wy1[...] = block.astype(BF16)
+    wy2[...] = (2.0 * block).astype(BF16)
+
+
+def edges_body(scale, first_ref, bridge_ref, pin_ref, bin_ref, coef_ref, out_first, out_bridge):
+    head, square = coef_ref[0:1, :], coef_ref[1:2, :]
+    pin, bin_ = scale * pin_ref[...], scale * bin_ref[...]
+    out_first[...] = first_ref[...] + head * pin + bin_
+    out_bridge[...] = bridge_ref[...] + square * pin + head * bin_
+
+
+def pair_body(nx, nz, width, chip, scal, cur_ref, gathered_ref, pot_hbm, kx_hbm, ky_hbm, ek_hbm, *refs):
+    one_ref, two_ref, first_ref, bridge_ref, rows1_ref, rows2_ref, pot_ref = refs[:7]
+    kz2, kx2, wy2, kx4, rcol, coef = refs[7:13]
+    col_ref, planes_ref, halo_ref, sems, kx_ref, ky_raw, ek_ref, kz1, kx1, wy1, ky_ref = refs[13:]
     stride = nz + PAD
-
-    def packed(x):
-        u = cur_ref[rows_of(x, nz, nz), :]
-        col_ref[rows_of(x, stride, nz), :] = u
-        return u
-
+    small = [
+        pltpu.make_async_copy(src, dst, sems.at[2 + i])
+        for i, (src, dst) in enumerate(((kx_hbm, kx_ref), (ky_hbm, ky_raw), (ek_hbm, ek_ref)))
+    ]
+    for copy in small:
+        copy.start()
+    part = nx * nz // 2
+    copies = [
+        pltpu.make_async_copy(
+            pot_hbm.at[pl.ds(h * part, part), :], pot_ref.at[pl.ds(h * part, part), :], sems.at[h]
+        )
+        for h in range(2)
+    ]
+    for copy in copies:
+        copy.start()
+
+    trans, planes, each, _ = gathered_ref.shape
+    each = each // 2
+    for t in range(trans):
+        for q in range(planes):
+            planes_ref[q, t * each : (t + 1) * each, :] = gathered_ref[
+                t, q, pl.ds(pl.multiple_of(scal[1] * each, 8), each), :
+            ]
+    for copy in small:
+        copy.wait()
+    matrices(scal, kx_ref, ky_raw, ek_ref, kz1, kx1, wy1, kz2, kx2, wy2, kx4, ky_ref)
+    edge_vectors(ek_ref, rcol, coef)
     precise = lax.Precision.HIGHEST
     for q in range(2):
         plane = planes_ref[q]
         moved = jnp.dot(kx_ref[...], plane, precision=precise, preferred_element_type=F32)
         moved = moved + jnp.dot(plane, ky_ref[...], precision=precise, preferred_element_type=F32)
-        moved = moved + planes_ref[2 + q]
-        halo_ref[q] = moved if q == 0 else 2.0 * moved
+        halo_ref[q] = moved + planes_ref[2 + q]
+
+    def packed(x):
+        u = cur_ref[rows_of(x, nz, nz), :]
+        col_ref[rows_of(x, stride, nz), :] = u
+        return u
+
     apply_local(
-        nx, nz, width, (pot_ref, kz1, kx1, wy1, wvec), (col_ref, stride), packed, None,
-        (rcol1, planes_ref.at[0], planes_ref.at[1]), 1.0, (one_ref, 0, nx), None,
+        nx, nz, width, (pot_ref, kz1, kx1, wy1, rcol), (col_ref, stride), packed, None,
+        (rcol, planes_ref.at[0], planes_ref.at[1], 1.0), 1.0, (one_ref, 0, nx), None,
+        ready=lambda h: copies[h].wait(),
     )
     apply_local(
-        nx, nz, width, (pot_ref, kz2, kx2, wy2, wvec), (one_ref, stride),
+        nx, nz, width, (pot_ref, kz2, kx2, wy2, rcol), (one_ref, stride),
         lambda x: one_ref[rows_of(x, stride, nz), :], (cur_ref, nz),
-        (rcol2, halo_ref.at[0], halo_ref.at[1]), 2.0, (two_ref, 0, nx), bridge_ref,
+        (rcol, halo_ref.at[0], halo_ref.at[1], 2.0), 2.0, (two_ref, 0, nx), bridge_ref,
     )
     first_ref[...] = two_ref[pl.ds(0, nx, stride=stride), :]
     for ref, rows_ref in ((one_ref, rows1_ref), (two_ref, rows2_ref)):
@@ -181,10 +284,10 @@
             rows_ref[q * nz : (q + 1) * nz, :] = ref[rows_of(scal[0] + q, stride, nz), :]
 
 
-def third_body(nx, nz, width, cur_ref, prev_ref, pot_ref, kz, kx, wy, wvec, out_ref, first_ref, bridge_ref):
+def third_body(nx, nz, width, cur_ref, prev_ref, pot_ref, kz, kx, wy, rcol, out_ref, first_ref, bridge_ref):
     stride = nz + PAD
     apply_local(
-        nx, nz, width, (pot_ref, kz, kx, wy, wvec), (cur_ref, stride),
+        nx, nz, width, (pot_ref, kz, kx, wy, rcol), (cur_ref, stride),
         lambda x: cur_ref[rows_of(x, stride, nz), :], (prev_ref, stride), None, 2.0,
         (out_ref, 0, nx), bridge_ref,
     )
@@ -192,18 +295,18 @@
 
 
 def fourth_body(nx, nz, width, chip, scal, cur_ref, pin_ref, bin_ref, prev_ref, pot_ref, *refs):
-    kz, kx, wy, wvec, rcol, out_ref, rows_ref, col_ref = refs
+    kz, kx, wy, rcol, out_ref, rows_ref, col_ref = refs
     stride = nz + PAD
 
     def complete(x):
-        u = with_halo(cur_ref[rows_of(x, stride, nz), :], (rcol, pin_ref, bin_ref), x)
+        u = with_halo(cur_ref[rows_of(x, stride, nz), :], (rcol, pin_ref, bin_ref, 2.0), x)
         col_ref[rows_of(x, stride, nz), :] = u
 
     repeat(nx, 16, only(complete), 0)
     for q in range(chip):
         rows_ref[q * nz : (q + 1) * nz, :] = col_ref[rows_of(scal[0] + q, stride, nz), :]
     apply_local(
-        nx, nz, width, (pot_ref, kz, kx, wy, wvec), (col_ref, stride),
+        nx, nz, width, (pot_ref, kz, kx, wy, rcol), (col_ref, stride),
         lambda x: col_ref[rows_of(x, stride, nz), :], (prev_ref, stride), None, 2.0,
         (out_ref, scal[0], chip), None,
     )
@@ -217,8 +320,11 @@
     return pltpu.VMEM(shape, F32)
 
 
-def call(name, body, outs, *ins, scal=None, scratch=(), cost=4):
-    specs = [vm()] * len(ins)
+def call(name, body, outs, *ins, scal=None, scratch=(), cost=4, away=()):
+    specs = [pl.BlockSpec(memory_space=pltpu.HBM) if i in away else vm() for i in range(len(ins))]
+    ins = tuple(
+        pltpu.with_memory_space_constraint(x, pltpu.HBM) if i in away else x for i, x in enumerate(ins)
+    )
     if scal is not None:
         specs = [pl.BlockSpec(memory_space=pltpu.SMEM)] + specs
         ins = (scal,) + ins
@@ -241,18 +347,15 @@
     keep_ref, send_ref = refs[POWERS - 1 :]
     core = scal[1]
     size = rows * nz
-    width = last_ref.shape[-1]
-    top = lax.broadcasted_iota(jnp.int32, (8, width), 0) == 0
+    halo = (rcol_ref, pin_ref, bin_ref, 2.0)
     for ref, where in ((keep_ref, core), (send_ref, 1 - core)):
         at = pl.ds(pl.multiple_of(where * size, size), size)
         for k in range(POWERS - 1):
             ref[k] = cols[k][at, :]
         for r in range(rows):
             x = where * rows + r
-            u = last_ref[pl.ds(pl.multiple_of(x * (nz + PAD), 8), nz), :]
-            u = u + rcol_ref[...] * pin_ref[pl.ds(x, 1), :]
-            head = u[0:8] + jnp.where(top, bin_ref[pl.ds(x, 1), :], 0.0)
-            ref[POWERS - 1, r * nz : (r + 1) * nz, :] = jnp.concatenate([head, u[8:]], axis=0)
+            u = with_halo(last_ref[rows_of(x, nz + PAD, nz), :], halo, scal[0] + x)
+            ref[POWERS - 1, r * nz : (r + 1) * nz, :] = u
 
 
 def gram_body(scal, packets_ref, keep_ref, recv_ref, cols_ref, gram_ref, acc_ref):
@@ -386,7 +489,7 @@
     me = lax.axis_index("trans")
     core = me % 2
     chip = 2 * rows
-    scal = jnp.stack([(me // 2) * chip, core]).astype(jnp.int32)
+    scal = jnp.stack([(me // 2) * chip, core, lax.axis_index("beam")]).astype(jnp.int32)
 
     size = rows * nz
     flat = packets.reshape(npack, size, width)
@@ -402,90 +505,60 @@
         name="copies",
     )(flat)
     cur = lax.all_to_all(sent, "trans", 0, 0, tiled=True).reshape(nx * nz, width)
-    sent, flat_late, mine_late = lax.optimization_barrier((sent, flat, mine))
-
-    corner = element_kinetic[nz, nz] * (lax.axis_index("beam") > 0).astype(F32)
-    kz = element_kinetic[:nz, :nz].at[0, 0].add(corner)
-    wrow = element_kinetic[nz, :nz]
-    rcol = element_kinetic[:nz, nz]
-    mrow = jnp.sum(wrow[:, None] * kz, axis=0)
-    wr = jnp.sum(wrow * rcol)
-
-    def parts_of(k):
-        high = lax.reduce_precision(k, 8, 7)
-        return high.astype(BF16), (k - high).astype(BF16)
-
-    def left_weights(k):
-        high, low = parts_of(k)
-        none = jnp.zeros_like(high)
-        block = jnp.concatenate(
-            [jnp.concatenate([high, high], axis=1), jnp.concatenate([low, none], axis=1)], axis=0
-        )
-        none = jnp.zeros_like(block)
-        return jnp.concatenate(
-            [jnp.concatenate([block, none], axis=1), jnp.concatenate([none, block], axis=1)], axis=0
-        )
-
-    none = jnp.zeros_like(kinetic_y)
-    ky = jnp.concatenate(
-        [jnp.concatenate([kinetic_y.T, none], axis=1), jnp.concatenate([none, kinetic_y.T], axis=1)],
-        axis=0,
-    )
-    ky_high, ky_low = parts_of(ky)
-    wy = jnp.concatenate(
-        [
-            jnp.concatenate([ky_high, ky_low], axis=1),
-            jnp.concatenate([ky_high, jnp.zeros_like(ky_low)], axis=1),
-        ],
-        axis=0,
-    )
-    kz1, kx1 = left_weights(kz), left_weights(kinetic_x)
-    kz2, kx2, wy2 = kz1 * 2, kx1 * 2, wy * 2
-    kx_last = left_weights(2.0 * lax.dynamic_slice_in_dim(kinetic_x, scal[0], chip, 0))
-
-    def wide(column):
-        return jnp.broadcast_to(column[:, None], (nz, width))
-
-    rcol1, wvec = wide(rcol), wide(wrow)
-    rcol2 = rcol1 * 2.0
+    sent, flat_late, mine_late, ek_late = lax.optimization_barrier(
+        (sent, flat, mine, element_kinetic)
+    )
+
+    def half_wide(*shape):
+        return pltpu.VMEM(shape, BF16)
+
+    square, column = half_wide(4 * nz, 4 * nz), in_vmem(nz, width)
+    across = half_wide(4 * nx, 4 * nx)
+    wide = half_wide(2 * width, 2 * width)
+    rcol, kvec, mvec, coef = call(
+        "vectors", vectors_body, [column, column, column, in_vmem(8, width)], ek_late, scal=scal, cost=1
+    )
 
     plane = in_vmem(npack * rows, width)
     first, bridge, zrest, brest = call(
         "planes", functools.partial(planes_body, nz), [plane] * 4,
-        flat_late, mine_late, wvec, wide(kz[0]), wide(mrow), cost=1,
+        flat_late, mine_late, rcol, kvec, mvec, cost=1,
     )
     pin, bin_ = passed(first, -1), passed(bridge, 1)
-    pnext = passed(zrest + rcol[0] * pin + bin_, -1)
-    bnext = passed(brest + wr * pin + wrow[0] * bin_, 1)
-    planes = jnp.stack([pin, bin_, pnext, bnext])
-    planes = lax.all_gather(planes, "trans").reshape(trans, 4, npack, rows, width)
-    planes = lax.dynamic_index_in_dim(planes, core, 2, keepdims=False)
-    planes = planes.transpose(1, 0, 2, 3).reshape(4, nx, width)
+    pnext, bnext = call(
+        "edges", functools.partial(edges_body, 1.0), [plane] * 2, zrest, brest, pin, bin_, coef, cost=1
+    )
+    planes = jnp.stack([pin, bin_, passed(pnext, -1), passed(bnext, 1)])
+    planes = lax.all_gather(planes, "trans")
 
     full, edge = in_vmem(nx * (nz + PAD), width), in_vmem(nx, width)
     here = in_vmem(chip * nz, width)
-    col1, col2, first, bridge, rows1, rows2 = call(
-        "pair", functools.partial(pair_body, nx, nz, width, chip), [full, full, edge, edge, here, here],
-        cur, planes, pot, kz1, kx1, wy, kz2, kx2, wy2, kinetic_x, ky, rcol1, rcol2, wvec,
-        scal=scal, scratch=[full, in_vmem(2, nx, width)], cost=8,
-    )
-    pin, bin_ = passed(first, -1), 2.0 * passed(bridge, 1)
+    col1, col2, first, bridge, rows1, rows2, pot, kz2, kx2, wy2, kx4, rcol, coef = call(
+        "pair", functools.partial(pair_body, nx, nz, width, chip),
+        [full, full, edge, edge, here, here, in_vmem(nx * nz, width),
+         square, across, wide, half_wide(4 * chip, 4 * nx), column, in_vmem(8, width)],
+        cur, planes, pot, kinetic_x, kinetic_y, element_kinetic,
+        scal=scal, cost=8, away=(2, 3, 4, 5),
+        scratch=[full, in_vmem(4, nx, width), in_vmem(2, nx, width), pltpu.SemaphoreType.DMA((5,)),
+                 in_vmem(*kinetic_x.shape), in_vmem(*kinetic_y.shape), in_vmem(*element_kinetic.shape),
+                 square, across, wide, in_vmem(width, width)],
+    )
+    pin, bin_ = passed(first, -1), passed(bridge, 1)
     col3, first, bridge = call(
         "third", functools.partial(third_body, nx, nz, width), [full, edge, edge],
-        col2, col1, pot, kz2, kx2, wy2, wvec,
-    )
-    first = first + (2.0 * rcol[0]) * pin + bin_
-    bridge = bridge + (2.0 * wr) * pin + wrow[0] * bin_
-    plast, blast = passed(first, -1), 2.0 * passed(bridge, 1)
+        col2, col1, pot, kz2, kx2, wy2, rcol,
+    )
+    first, bridge = call(
+        "edges", functools.partial(edges_body, 2.0), [edge] * 2, first, bridge, pin, bin_, coef, cost=1
+    )
+    plast, blast = passed(first, -1), passed(bridge, 1)
     local, rows3 = call(
         "fourth", functools.partial(fourth_body, nx, nz, width, chip),
         [in_vmem(chip * (nz + PAD), width), here],
-        col3, pin, bin_, col2, pot, kz2, kx_last, wy2, wvec, rcol2,
+        col3, pin, bin_, col2, pot, kz2, kx4, wy2, rcol,
         scal=scal, scratch=[full], cost=2,
     )
     columns = [rows1, rows2, rows3]
-    pin = lax.dynamic_slice_in_dim(plast, scal[0], chip, 0)
-    bin_ = lax.dynamic_slice_in_dim(blast, scal[0], chip, 0)
     keep, send = pl.pallas_call(
         functools.partial(finish_body, nz, rows),
         out_shape=[in_vmem(POWERS, size, width)] * 2,
@@ -493,7 +566,7 @@
         out_specs=[vm()] * 2,
         compiler_params=pltpu.CompilerParams(vmem_limit_bytes=LIMIT),
         name="finish",
-    )(scal, local, pin, bin_, rcol2, *columns)
+    )(scal, local, plast, blast, rcol, *columns)
     recv = lax.ppermute(send, "trans", [(i, i ^ 1) for i in range(trans)])
     cols, gram = pl.pallas_call(
         gram_body,

time: 160 us -> 151 us (0.944)
  local copies, waits for them, and re-layouts: 11.3 us -> 1.97 us
  other arithmetic: 6.43 us -> 0.1 us
  blocking collectives: 63.2 us -> 69 us
  between operations: 17.7 us -> 14.2 us
  Pallas kernels: 22.9 us -> 24.9 us
    all_gather x1, blocking collectives: 19.6 us -> 27.4 us  [shards(): planes = lax.all_gather(planes, 'trans')]
    unnamed x36 -> x9, local copies, waits for them, and re-layouts: 9.32 us -> 1.95 us
    mul x4 -> x0, other arithmetic: 2.69 us -> none  [the longest x2 1.41 us: shards(): kz2, kx2, wy2 = (kz1 * 2, kx1 * 2, wy * 2)]
    all_to_all x1, blocking collectives: 35.5 us -> 33.5 us  [shards(): lax.all_to_all(jnp.broadcast_to(gram, (beam, 1, width)), 'beam', 0, 0, ti...]
    pallas_call x4 -> x7, Pallas kernels: 12.5 us -> 14.5 us  [call(): pl.pallas_call(body, out_shape=outs, in_specs=specs, out_specs=[vm()] * l...]
    add x2 -> x0, other arithmetic: 1.93 us -> none  [the longest x1 1.91 us: shards(): pnext = passed(zrest + rcol[0] * pin + bin_, -1)]
  transfers between devices with their start and end apart: 11 -> 11, of which waited for: 1 -> 3; matrix products, arithmetic and copies ran while one was open for 5% -> 0% of each run, Pallas kernels for 4% -> 5%
where the time goes in v3:
time: 151 us; the launch traced here: 150 us
  blocking collectives  69 us (46%)
  starting transfers between devices  35.3 us (23%)
  Pallas kernels  24.9 us (16%)
  between operations  14.2 us (9%)
  waiting for transfers between devices  4.5 us (3%)
  local copies, waits for them, and re-layouts  1.97 us (1%)
    all_to_all x1, blocking collectives, shards(): lax.all_to_all(jnp.broadcast_to(gram, (beam, 1, width)), 'beam', 0, 0, ti...  33.5 us
    all_gather x1, blocking collectives, shards(): planes = lax.all_gather(planes, 'trans')  27.4 us
    ppermute x8, starting transfers between devices, passed(): lax.ppermute(x, 'beam', [(i, i + by) for i in range(peers) if 0 <= i + by...  21.7 us
    pallas_call x7, Pallas kernels, call(): pl.pallas_call(body, out_shape=outs, in_specs=specs, out_specs=[vm()] * l...  14.5 us
    all_to_all x1, starting transfers between devices, shards(): lax.all_to_all(sent, 'trans', 0, 0, tiled=True).reshape(nx * nz, width)  10.4 us
    all_to_all x1, blocking collectives, shards(): lax.all_to_all(gram, 'trans', 0, 0, tiled=True)  8.07 us
    pallas_call x1, Pallas kernels, shards(): pl.pallas_call(functools.partial(basis_body, cells, rows), out_shape=[jax...  5.32 us
    ppermute x1, starting transfers between devices, shards(): recv = lax.ppermute(send, 'trans', [(i, i ^ 1) for i in range(trans)])  3.18 us
  transfers between devices with their start and end apart: 11, of which 3 were waited for; matrix products, arithmetic and copies ran while one was open for 0% of the time, Pallas kernels for 5%

profile of v3, /device:TPU:1, one launch (start us, length us, event | category | flops | bytes accessed | tf_op | source)
XLA Modules:
  0.0 150.0 jit_solution(10142194289759544235)
XLA Ops:
  7.9 1.0 copy-done
  8.9 1.3 copies.1
  10.3 10.4 %all-to-all-start = ((f32[8,512,128]{2,1,0:T(8,128)}), f32[8,512,128]{2,1,0:T(8,128)S(1)}, u32[]{:S(2)}, u32[]{:S(2)}) async-start(f32[8,512,128]{2,1,0:T(8,128)} %copies.1), calls=%async_computation | async-start | bytes 4194304 | tf_op jit(solution)/shard_map/all_to_all | solution.py:507
  20.8 0.7 vectors.1
  22.2 1.3 collective-permute-start
  23.5 4.0 %collective-permute-start.1 = (f32[16,128]{1,0:T(8,128)S(1)}, f32[16,128]{1,0:T(8,128)S(1)}, u32[]{:S(2)}, u32[]{:S(2)}) collective-permute-start(f32[16,128]{1,0:T(8,128)S(1)} %get-tuple-element.48), channel_id=1, source_target_pairs={{0,8},{8,16},{16,24},{24,32},{32,40},{40,48},{48,56},{56,64},{64,7... | collective-permute-start | bytes 24584 | tf_op jit(solution)/shard_map/ppermute | solution.py:23
  27.5 0.8 collective-permute-done.1.bin_ref
  28.3 1.3 collective-permute-start.2
  29.6 4.5 %collective-permute-start.3 = (f32[16,128]{1,0:T(8,128)S(1)}, f32[16,128]{1,0:T(8,128)S(1)}, u32[]{:S(2)}, u32[]{:S(2)}) collective-permute-start(f32[16,128]{1,0:T(8,128)S(1)} %get-tuple-element.53), channel_id=1, source_target_pairs={{0,8},{8,16},{16,24},{24,32},{32,40},{40,48},{48,56},{56,64},{64,7... | collective-permute-start | bytes 24584 | tf_op jit(solution)/shard_map/ppermute | solution.py:23
  34.2 0.8 collective-permute-done.3
  34.9 27.4 %all-gather = f32[32,16,128]{2,1,0:T(8,128)S(1)} all-gather(f32[4,16,128]{2,1,0:T(8,128)S(1)} %pad_maximum_fusion), channel_id=2, replica_groups=mesh['beam'=64,'trans'=8] {'trans'}, dimensions={0}, use_global_device_ids=true | all-gather | bytes 294912 | tf_op jit(solution)/shard_map/all_gather | solution.py:532
  62.3 8.3 %pair.1 = (f32[4608,128]{1,0:T(8,128)S(1)}, f32[4608,128]{1,0:T(8,128)S(1)}, f32[64,128]{1,0:T(8,128)S(1)}, f32[64,128]{1,0:T(8,128)S(1)}, f32[1024,128]{1,0:T(8...) custom-call(s32[3]{0:T(128)S(1)} %pad_add_fusion.scal, ...), custom_call_target="tpu_custom_call" | custom-call | flops 8000000000 | bytes 16000000 | tf_op jit(solution)/shard_map/pair/pallas_call | solution.py:331
  70.6 1.3 collective-permute-start.4
  71.9 4.0 %collective-permute-start.5 = (f32[64,128]{1,0:T(8,128)S(1)}, f32[64,128]{1,0:T(8,128)S(1)}, u32[]{:S(2)}, u32[]{:S(2)}) collective-permute-start(f32[64,128]{1,0:T(8,128)S(1)} %get-tuple-element.63), channel_id=1, source_target_pairs={{0,8},{8,16},{16,24},{24,32},{32,40},{40,48},{48,56},{56,64},{64,7... | collective-permute-start | bytes 98312 | tf_op jit(solution)/shard_map/ppermute | solution.py:23
  75.9 3.1 %third.1 = (f32[4608,128]{1,0:T(8,128)S(1)}, f32[64,128]{1,0:T(8,128)S(1)}, f32[64,128]{1,0:T(8,128)S(1)}) custom-call(f32[4608,128]{1,0:T(8,128)S(1)} %get-tuple-element.54.cur_ref.prev_ref, f32[4608,128]{1,0:T(8,128)S(1)} %get-tuple-element.55.prev_ref, f32[4096,128]{1,0:T(8,128)S(1)} %get-tuple-element.56.pot_ref, ...), custom_call_target="tpu_custom_call" | custom-call | flops 4000000000 | bytes 8000000 | tf_op jit(solution)/shard_map/third/pallas_call | solution.py:331
  79.1 1.3 collective-permute-start.6
  80.4 4.0 %collective-permute-start.7 = (f32[64,128]{1,0:T(8,128)S(1)}, f32[64,128]{1,0:T(8,128)S(1)}, u32[]{:S(2)}, u32[]{:S(2)}) collective-permute-start(f32[64,128]{1,0:T(8,128)S(1)} %get-tuple-element.70), channel_id=1, source_target_pairs={{0,8},{8,16},{16,24},{24,32},{32,40},{40,48},{48,56},{56,64},{64,7... | collective-permute-start | bytes 98312 | tf_op jit(solution)/shard_map/ppermute | solution.py:23
  84.4 2.0 %fourth.1 = (f32[1152,128]{1,0:T(8,128)S(1)}, f32[1024,128]{1,0:T(8,128)S(1)}) custom-call(s32[3]{0:T(128)S(1)} %pad_add_fusion.scal, f32[4608,128]{1,0:T(8,128)S(1)} %get-tuple-element.61.cur_ref, f32[64,128]{1,0:T(8,128)S(1)} %collective-permute-done.4.pin_ref, f32[64,128]{1,0:T(8,128)S(1)} %collective-permute-done.5.bin_ref, ...), custom_call_target="tpu_custom_call" | custom-call | flops 2000000000 | bytes 4000000 | tf_op jit(solution)/shard_map/fourth/pallas_call | solution.py:331
  87.1 3.2 %collective-permute-start.8 = (f32[4,512,128]{2,1,0:T(8,128)S(1)}, f32[4,512,128]{2,1,0:T(8,128)S(1)}, u32[]{:S(2)}, u32[]{:S(2)}) collective-permute-start(f32[4,512,128]{2,1,0:T(8,128)S(1)} %get-tuple-element.75), channel_id=1, source_target_pairs={{0,1},{1,0},{2,3},{3,2},{4,5},{5,4},{6,7},{7,6},{8,9},{9,8},{10,11... | collective-permute-start | bytes 3145736 | tf_op jit(solution)/shard_map/ppermute | solution.py:570
  90.2 2.3 %collective-permute-done.8.recv_ref = f32[4,512,128]{2,1,0:T(8,128)S(1)} collective-permute-done((f32[4,512,128]{2,1,0:T(8,128)S(1)}, f32[4,512,128]{2,1,0:T(8,128)S(1)}, u32[]{:S(2)}, u32[]{:S(2)}) %collective-permute-start.8) | collective-permute-done | bytes 1048608 | tf_op jit(solution)/shard_map/ppermute | solution.py:570
  92.5 3.0 %gram.1 = (f32[10,512,128]{2,1,0:T(8,128)S(1)}, f32[8,1,128]{2,1,0:T(1,128)S(1)}) custom-call(s32[3]{0:T(128)S(1)} %pad_add_fusion.scal, f32[2,512,128]{2,1,0:T(8,128)S(1)} %bitcast.16, f32[4,512,128]{2,1,0:T(8,128)S(1)} %get-tuple-element.74.keep_ref, f32[4,512,128]{2,1,0:T(8,128)S(1)} %collective-permute-done.8.recv_ref), custom_call_target="tpu_custom_call" | custom-call | tf_op jit(solution)/shard_map/gram/pallas_call | solution.py:571
  95.5 8.1 %all_to_all.15 = f32[8,1,128]{2,1,0:T(1,128)S(1)} all-to-all(f32[8,1,128]{2,1,0:T(1,128)S(1)} %get-tuple-element.76), channel_id=1, replica_groups=mesh['beam'=64,'trans'=8] {'trans'}, dimensions={0} | all-to-all | bytes 8192 | tf_op jit(solution)/shard_map/all_to_all | solution.py:581
  103.7 33.5 %all_to_all.16.gram_ref = f32[64,1,128]{2,1,0:T(1,128)S(1)} all-to-all(f32[64,1,128]{2,1,0:T(1,128)S(1)} %broadcast_in_dim.2), channel_id=1, replica_groups=mesh['beam'=64,'trans'=8] {'beam'}, dimensions={0} | all-to-all | bytes 65536 | tf_op jit(solution)/shard_map/all_to_all | solution.py:582
  137.2 5.3 %basis.1 = (f32[10,512,128]{2,1,0:T(8,128)}, f32[2,16,128]{2,1,0:T(8,128)S(1)}) custom-call(f32[64,1,128]{2,1,0:T(1,128)S(1)} %all_to_all.16.gram_ref, f32[10,512,128]{2,1,0:T(8,128)S(1)} %get-tuple-element.77.cols_ref), custom_call_target="tpu_custom_call" | custom-call | tf_op jit(solution)/shard_map/basis/pallas_call | solution.py:584
  (26 shorter events, 2.9 us)
Async XLA Ops:
  7.2 55.1 %all-gather.3.cloned.1.call-start = ((), (), s32[]{:S(2)}) async-start(), calls=%async_computation.3 | async-start | bytes 2359296 | tf_op jit(solution)/shard_map/all_gather | solution.py:497
  7.9 1.0 copy-start
  10.3 10.5 %copy-start.3 = (f32[65,65]{1,0:T(8,128)S(1)}, f32[65,65]{1,0:T(8,128)}, u32[]{:S(2)}) copy-start(f32[65,65]{1,0:T(8,128)} %ek_hbm.1) | copy-start | bytes 50704
  10.3 52.0 %all-to-all-start = ((f32[8,512,128]{2,1,0:T(8,128)}), f32[8,512,128]{2,1,0:T(8,128)S(1)}, u32[]{:S(2)}, u32[]{:S(2)}) async-start(f32[8,512,128]{2,1,0:T(8,128)} %copies.1), calls=%async_computation | async-start | bytes 4194304 | tf_op jit(solution)/shard_map/all_to_all | solution.py:507
  20.7 1.0 copy-start.1
  20.7 1.1 copy-start.2
  22.2 5.3 %collective-permute-start = (f32[16,128]{1,0:T(8,128)S(1)}, f32[16,128]{1,0:T(8,128)S(1)}, u32[]{:S(2)}, u32[]{:S(2)}) collective-permute-start(f32[16,128]{1,0:T(8,128)S(1)} %get-tuple-element.47), channel_id=1, source_target_pairs={{8,0},{16,8},{24,16},{32,24},{40,32},{48,40},{56,48},{64,56},{72,6... | collective-permute-start | bytes 24584 | tf_op jit(solution)/shard_map/ppermute | solution.py:23
  23.5 4.8 %collective-permute-start.1 = (f32[16,128]{1,0:T(8,128)S(1)}, f32[16,128]{1,0:T(8,128)S(1)}, u32[]{:S(2)}, u32[]{:S(2)}) collective-permute-start(f32[16,128]{1,0:T(8,128)S(1)} %get-tuple-element.48), channel_id=1, source_target_pairs={{0,8},{8,16},{16,24},{24,32},{32,40},{40,48},{48,56},{56,64},{64,7... | collective-permute-start | bytes 24584 | tf_op jit(solution)/shard_map/ppermute | solution.py:23
  28.3 5.8 %collective-permute-start.2 = (f32[16,128]{1,0:T(8,128)S(1)}, f32[16,128]{1,0:T(8,128)S(1)}, u32[]{:S(2)}, u32[]{:S(2)}) collective-permute-start(f32[16,128]{1,0:T(8,128)S(1)} %get-tuple-element.52), channel_id=1, source_target_pairs={{8,0},{16,8},{24,16},{32,24},{40,32},{48,40},{56,48},{64,56},{72,6... | collective-permute-start | bytes 24584 | tf_op jit(solution)/shard_map/ppermute | solution.py:23
  29.6 5.3 %collective-permute-start.3 = (f32[16,128]{1,0:T(8,128)S(1)}, f32[16,128]{1,0:T(8,128)S(1)}, u32[]{:S(2)}, u32[]{:S(2)}) collective-permute-start(f32[16,128]{1,0:T(8,128)S(1)} %get-tuple-element.53), channel_id=1, source_target_pairs={{0,8},{8,16},{16,24},{24,32},{32,40},{40,48},{48,56},{56,64},{64,7... | collective-permute-start | bytes 24584 | tf_op jit(solution)/shard_map/ppermute | solution.py:23
  70.6 8.4 %collective-permute-start.4 = (f32[64,128]{1,0:T(8,128)S(1)}, f32[64,128]{1,0:T(8,128)S(1)}, u32[]{:S(2)}, u32[]{:S(2)}) collective-permute-start(f32[64,128]{1,0:T(8,128)S(1)} %get-tuple-element.62), channel_id=1, source_target_pairs={{8,0},{16,8},{24,16},{32,24},{40,32},{48,40},{56,48},{64,56},{72,6... | collective-permute-start | bytes 98312 | tf_op jit(solution)/shard_map/ppermute | solution.py:23
  71.9 7.1 %collective-permute-start.5 = (f32[64,128]{1,0:T(8,128)S(1)}, f32[64,128]{1,0:T(8,128)S(1)}, u32[]{:S(2)}, u32[]{:S(2)}) collective-permute-start(f32[64,128]{1,0:T(8,128)S(1)} %get-tuple-element.63), channel_id=1, source_target_pairs={{0,8},{8,16},{16,24},{24,32},{32,40},{40,48},{48,56},{56,64},{64,7... | collective-permute-start | bytes 98312 | tf_op jit(solution)/shard_map/ppermute | solution.py:23
  79.1 7.3 %collective-permute-start.6 = (f32[64,128]{1,0:T(8,128)S(1)}, f32[64,128]{1,0:T(8,128)S(1)}, u32[]{:S(2)}, u32[]{:S(2)}) collective-permute-start(f32[64,128]{1,0:T(8,128)S(1)} %get-tuple-element.69), channel_id=1, source_target_pairs={{8,0},{16,8},{24,16},{32,24},{40,32},{48,40},{56,48},{64,56},{72,6... | collective-permute-start | bytes 98312 | tf_op jit(solution)/shard_map/ppermute | solution.py:23
  80.4 6.0 %collective-permute-start.7 = (f32[64,128]{1,0:T(8,128)S(1)}, f32[64,128]{1,0:T(8,128)S(1)}, u32[]{:S(2)}, u32[]{:S(2)}) collective-permute-start(f32[64,128]{1,0:T(8,128)S(1)} %get-tuple-element.70), channel_id=1, source_target_pairs={{0,8},{8,16},{16,24},{24,32},{32,40},{40,48},{48,56},{56,64},{64,7... | collective-permute-start | bytes 98312 | tf_op jit(solution)/shard_map/ppermute | solution.py:23
  87.1 5.5 %collective-permute-start.8 = (f32[4,512,128]{2,1,0:T(8,128)S(1)}, f32[4,512,128]{2,1,0:T(8,128)S(1)}, u32[]{:S(2)}, u32[]{:S(2)}) collective-permute-start(f32[4,512,128]{2,1,0:T(8,128)S(1)} %get-tuple-element.75), channel_id=1, source_target_pairs={{0,1},{1,0},{2,3},{3,2},{4,5},{5,4},{6,7},{7,6},{8,9},{9,8},{10,11... | collective-permute-start | bytes 3145736 | tf_op jit(solution)/shard_map/ppermute | solution.py:570
Sparse Core Ops, SparseCore 0:
  10.1 47.1 all-gather.2

commit v4 on v3

--- a/solution.py
+++ b/solution.py
@@ -139,19 +139,26 @@
         copy.wait()
 
 
-def planes_body(nz, packets_ref, pot_ref, wvec_ref, kvec_ref, mvec_ref, first_ref, bridge_ref, zrest_ref, brest_ref):
+def planes_body(nz, packets_ref, pot_ref, wvec_ref, kvec_ref, mvec_ref, left_ref, right_ref, first_ref, bridge_ref):
     npack, size, width = packets_ref.shape
     rows = size // nz
+    count = npack * rows
     left = lax.broadcasted_iota(jnp.int32, (nz, width), 1) < width // 2
     for p in range(npack):
         for x in range(rows):
             u = packets_ref[p, x * nz : (x + 1) * nz, :]
             v = optical(u, pot_ref[x * nz : (x + 1) * nz, :], left)
-            at = slice(p * rows + x, p * rows + x + 1)
-            first_ref[at, :] = u[0:1]
-            bridge_ref[at, :] = jnp.sum(wvec_ref[...] * u, axis=0, keepdims=True)
-            zrest_ref[at, :] = v[0:1] + jnp.sum(kvec_ref[...] * u, axis=0, keepdims=True)
-            brest_ref[at, :] = jnp.sum(wvec_ref[...] * v + mvec_ref[...] * u, axis=0, keepdims=True)
+            n = p * rows + x
+            left_ref[n : n + 1, :] = u[0:1]
+            right_ref[n : n + 1, :] = jnp.sum(wvec_ref[...] * u, axis=0, keepdims=True)
+            left_ref[count + n : count + n + 1, :] = v[0:1] + jnp.sum(
+                kvec_ref[...] * u, axis=0, keepdims=True
+            )
+            right_ref[count + n : count + n + 1, :] = jnp.sum(
+                wvec_ref[...] * v + mvec_ref[...] * u, axis=0, keepdims=True
+            )
+    first_ref[...] = left_ref[0:count, :]
+    bridge_ref[...] = right_ref[0:count, :]
 
 
 def element_matrix(scal, ek):
@@ -165,15 +172,10 @@
 def vectors_body(scal, ek_ref, rcol, kvec, mvec, coef):
     nz, width = rcol.shape
     kz = element_matrix(scal, ek_ref)
-    edge_vectors(ek_ref, rcol, coef)
+    rcol[...] = jnp.broadcast_to(ek_ref[0:nz, nz : nz + 1], (nz, width))
     kvec[...] = jnp.broadcast_to(kz[:, 0:1], (nz, width))
     bridge = ek_ref[nz : nz + 1, 0:nz]
     mvec[...] = jnp.broadcast_to(jnp.sum(kz * bridge, axis=1, keepdims=True), (nz, width))
-
-
-def edge_vectors(ek_ref, rcol, coef):
-    nz, width = rcol.shape
-    rcol[...] = jnp.broadcast_to(ek_ref[0:nz, nz : nz + 1], (nz, width))
     coef[...] = jnp.zeros_like(coef)
     coef[0:1, :] = rcol[0:1, :]
     coef[1:2, :] = jnp.sum(rcol[...] * rcol[...], axis=0, keepdims=True)
@@ -217,17 +219,40 @@
     wy2[...] = (2.0 * block).astype(BF16)
 
 
-def edges_body(scale, first_ref, bridge_ref, pin_ref, bin_ref, coef_ref, out_first, out_bridge):
+def edge_rests(scal, left_ref, right_ref, left2_ref, right2_ref, first_ref, bridge_ref, coef_ref):
+    count = left2_ref.shape[0]
     head, square = coef_ref[0:1, :], coef_ref[1:2, :]
-    pin, bin_ = scale * pin_ref[...], scale * bin_ref[...]
-    out_first[...] = first_ref[...] + head * pin + bin_
-    out_bridge[...] = bridge_ref[...] + square * pin + head * bin_
+    has_right = jnp.where(scal[2] < scal[3] - 1, 1.0, 0.0)
+    has_left = jnp.where(scal[2] > 0, 1.0, 0.0)
+    plane = left_ref[count : 2 * count, :] + head * left2_ref[...] + has_right * bridge_ref[...]
+    bridge = (
+        right_ref[count : 2 * count, :] + head * right2_ref[...] + (has_left * square) * first_ref[...]
+    )
+    return plane, bridge
+
+
+def edges_body(scal, left_ref, right_ref, left2_ref, right2_ref, first_ref, bridge_ref, coef_ref, out_ref):
+    count = left2_ref.shape[0]
+    plane, bridge = edge_rests(
+        scal, left_ref, right_ref, left2_ref, right2_ref, first_ref, bridge_ref, coef_ref
+    )
+    out_ref[0] = left_ref[0:count, :]
+    out_ref[1] = right_ref[0:count, :]
+    out_ref[2] = plane
+    out_ref[3] = bridge
+
+
+def transverse(kx_ref, ky_ref, plane):
+    precise = lax.Precision.HIGHEST
+    moved = jnp.dot(kx_ref[...], plane, precision=precise, preferred_element_type=F32)
+    return moved + jnp.dot(plane, ky_ref[...], precision=precise, preferred_element_type=F32)
 
 
 def pair_body(nx, nz, width, chip, scal, cur_ref, gathered_ref, pot_hbm, kx_hbm, ky_hbm, ek_hbm, *refs):
-    one_ref, two_ref, first_ref, bridge_ref, rows1_ref, rows2_ref, pot_ref = refs[:7]
-    kz2, kx2, wy2, kx4, rcol, coef = refs[7:13]
-    col_ref, planes_ref, halo_ref, sems, kx_ref, ky_raw, ek_ref, kz1, kx1, wy1, ky_ref = refs[13:]
+    one_ref, two_ref, left_ref, right_ref, first_ref, bridge_ref, rows1_ref, rows2_ref = refs[:8]
+    pot_ref, kz2, kx2, wy2, kx4, kx_ref, ky_ref, halo_ref = refs[8:16]
+    rcol, kvec, mvec, coef = refs[16:20]
+    col_ref, planes_ref, sems, ky_raw, ek_ref, kz1, kx1, wy1 = refs[20:]
     stride = nz + PAD
     small = [
         pltpu.make_async_copy(src, dst, sems.at[2 + i])
@@ -255,13 +280,9 @@
     for copy in small:
         copy.wait()
     matrices(scal, kx_ref, ky_raw, ek_ref, kz1, kx1, wy1, kz2, kx2, wy2, kx4, ky_ref)
-    edge_vectors(ek_ref, rcol, coef)
-    precise = lax.Precision.HIGHEST
+    vectors_body(scal, ek_ref, rcol, kvec, mvec, coef)
     for q in range(2):
-        plane = planes_ref[q]
-        moved = jnp.dot(kx_ref[...], plane, precision=precise, preferred_element_type=F32)
-        moved = moved + jnp.dot(plane, ky_ref[...], precision=precise, preferred_element_type=F32)
-        halo_ref[q] = moved + planes_ref[2 + q]
+        halo_ref[q] = transverse(kx_ref, ky_ref, planes_ref[q]) + planes_ref[2 + q]
 
     def packed(x):
         u = cur_ref[rows_of(x, nz, nz), :]
@@ -278,38 +299,71 @@
         lambda x: one_ref[rows_of(x, stride, nz), :], (cur_ref, nz),
         (rcol, halo_ref.at[0], halo_ref.at[1], 2.0), 2.0, (two_ref, 0, nx), bridge_ref,
     )
-    first_ref[...] = two_ref[pl.ds(0, nx, stride=stride), :]
+    first = two_ref[pl.ds(0, nx, stride=stride), :]
+    first_ref[...] = first
+    left_ref[0:nx, :] = first
+    right_ref[0:nx, :] = bridge_ref[...]
+    left = lax.broadcasted_iota(jnp.int32, (nz, width), 1) < width // 2
+
+    def fold(v):
+        while v.shape[0] > 8:
+            half = v.shape[0] // 2
+            v = v[:half] + v[half:]
+        return jnp.sum(v, axis=0, keepdims=True)
+
+    def rests(x):
+        u = two_ref[rows_of(x, stride, nz), :]
+        v = optical(u, pot_ref[rows_of(x, nz, nz), :], left)
+        left_ref[pl.ds(nx + x, 1), :] = v[0:1] + fold(kvec[...] * u)
+        right_ref[pl.ds(nx + x, 1), :] = fold(rcol[...] * v + mvec[...] * u)
+
+    repeat(nx, 16, only(rests), 0)
     for ref, rows_ref in ((one_ref, rows1_ref), (two_ref, rows2_ref)):
         for q in range(chip):
             rows_ref[q * nz : (q + 1) * nz, :] = ref[rows_of(scal[0] + q, stride, nz), :]
 
 
-def third_body(nx, nz, width, cur_ref, prev_ref, pot_ref, kz, kx, wy, rcol, out_ref, first_ref, bridge_ref):
+def third_body(nx, nz, width, cur_ref, prev_ref, pot_ref, kz, kx, wy, rcol, out_ref):
     stride = nz + PAD
     apply_local(
         nx, nz, width, (pot_ref, kz, kx, wy, rcol), (cur_ref, stride),
         lambda x: cur_ref[rows_of(x, stride, nz), :], (prev_ref, stride), None, 2.0,
-        (out_ref, 0, nx), bridge_ref,
-    )
-    first_ref[...] = out_ref[pl.ds(0, nx, stride=stride), :]
-
-
-def fourth_body(nx, nz, width, chip, scal, cur_ref, pin_ref, bin_ref, prev_ref, pot_ref, *refs):
-    kz, kx, wy, rcol, out_ref, rows_ref, col_ref = refs
+        (out_ref, 0, nx), None,
+    )
+
+
+def fourth_body(nx, nz, width, chip, scal, cur_ref, prev_ref, pot_ref, *refs):
+    kz, kx, wy, rcol, kx_ref, ky_ref, before_ref = refs[:7]
+    edges, rows1_ref, rows2_ref = refs[7:14], refs[14], refs[15]
+    keep_ref, send_ref, col_ref, out_ref, halo_ref = refs[16:]
+    left_ref, right_ref = edges[:2]
     stride = nz + PAD
+    rests = edge_rests(scal, *edges)
+    for q, near in enumerate((left_ref, right_ref)):
+        moved = transverse(kx_ref, ky_ref, near[0:nx, :])
+        halo_ref[q] = 2.0 * (moved + rests[q]) - before_ref[q]
+    now = (rcol, left_ref, right_ref, 2.0)
 
     def complete(x):
-        u = with_halo(cur_ref[rows_of(x, stride, nz), :], (rcol, pin_ref, bin_ref, 2.0), x)
+        u = with_halo(cur_ref[rows_of(x, stride, nz), :], now, x)
         col_ref[rows_of(x, stride, nz), :] = u
 
     repeat(nx, 16, only(complete), 0)
-    for q in range(chip):
-        rows_ref[q * nz : (q + 1) * nz, :] = col_ref[rows_of(scal[0] + q, stride, nz), :]
     apply_local(
         nx, nz, width, (pot_ref, kz, kx, wy, rcol), (col_ref, stride),
-        lambda x: col_ref[rows_of(x, stride, nz), :], (prev_ref, stride), None, 2.0,
-        (out_ref, scal[0], chip), None,
-    )
+        lambda x: col_ref[rows_of(x, stride, nz), :], (prev_ref, stride),
+        (rcol, halo_ref.at[0], halo_ref.at[1], 2.0), 2.0, (out_ref, scal[0], chip), None,
+    )
+    rows = chip // 2
+    size = rows * nz
+    for ref, where in ((keep_ref, scal[1]), (send_ref, 1 - scal[1])):
+        at = pl.ds(pl.multiple_of(where * size, size), size)
+        ref[0] = rows1_ref[at, :]
+        ref[1] = rows2_ref[at, :]
+        for r in range(rows):
+            x = where * rows + r
+            ref[2, r * nz : (r + 1) * nz, :] = col_ref[rows_of(scal[0] + x, stride, nz), :]
+            ref[3, r * nz : (r + 1) * nz, :] = out_ref[rows_of(x, stride, nz), :]
 
 
 def vm():
@@ -340,22 +394,6 @@
         ),
         name=name,
     )(*ins)
-
-
-def finish_body(nz, rows, scal, last_ref, pin_ref, bin_ref, rcol_ref, *refs):
-    cols = refs[: POWERS - 1]
-    keep_ref, send_ref = refs[POWERS - 1 :]
-    core = scal[1]
-    size = rows * nz
-    halo = (rcol_ref, pin_ref, bin_ref, 2.0)
-    for ref, where in ((keep_ref, core), (send_ref, 1 - core)):
-        at = pl.ds(pl.multiple_of(where * size, size), size)
-        for k in range(POWERS - 1):
-            ref[k] = cols[k][at, :]
-        for r in range(rows):
-            x = where * rows + r
-            u = with_halo(last_ref[rows_of(x, nz + PAD, nz), :], halo, scal[0] + x)
-            ref[POWERS - 1, r * nz : (r + 1) * nz, :] = u
 
 
 def gram_body(scal, packets_ref, keep_ref, recv_ref, cols_ref, gram_ref, acc_ref):
@@ -489,7 +527,8 @@
     me = lax.axis_index("trans")
     core = me % 2
     chip = 2 * rows
-    scal = jnp.stack([(me // 2) * chip, core, lax.axis_index("beam")]).astype(jnp.int32)
+    beam = lax.axis_size("beam")
+    scal = jnp.stack([(me // 2) * chip, core, lax.axis_index("beam"), beam]).astype(jnp.int32)
 
     size = rows * nz
     flat = packets.reshape(npack, size, width)
@@ -519,54 +558,43 @@
         "vectors", vectors_body, [column, column, column, in_vmem(8, width)], ek_late, scal=scal, cost=1
     )
 
-    plane = in_vmem(npack * rows, width)
-    first, bridge, zrest, brest = call(
-        "planes", functools.partial(planes_body, nz), [plane] * 4,
+    count = npack * rows
+    plane, double = in_vmem(count, width), in_vmem(2 * count, width)
+    left, right, first, bridge = call(
+        "planes", functools.partial(planes_body, nz), [double, double, plane, plane],
         flat_late, mine_late, rcol, kvec, mvec, cost=1,
     )
-    pin, bin_ = passed(first, -1), passed(bridge, 1)
-    pnext, bnext = call(
-        "edges", functools.partial(edges_body, 1.0), [plane] * 2, zrest, brest, pin, bin_, coef, cost=1
-    )
-    planes = jnp.stack([pin, bin_, passed(pnext, -1), passed(bnext, 1)])
+    (planes,) = call(
+        "edges", edges_body, [in_vmem(4, count, width)],
+        passed(left, -1), passed(right, 1), passed(first, -2), passed(bridge, 2), first, bridge, coef,
+        scal=scal, cost=1,
+    )
     planes = lax.all_gather(planes, "trans")
 
-    full, edge = in_vmem(nx * (nz + PAD), width), in_vmem(nx, width)
+    full, edge, two_edges = in_vmem(nx * (nz + PAD), width), in_vmem(nx, width), in_vmem(2 * nx, width)
     here = in_vmem(chip * nz, width)
-    col1, col2, first, bridge, rows1, rows2, pot, kz2, kx2, wy2, kx4, rcol, coef = call(
+    got = call(
         "pair", functools.partial(pair_body, nx, nz, width, chip),
-        [full, full, edge, edge, here, here, in_vmem(nx * nz, width),
-         square, across, wide, half_wide(4 * chip, 4 * nx), column, in_vmem(8, width)],
+        [full, full, two_edges, two_edges, edge, edge, here, here, in_vmem(nx * nz, width),
+         square, across, wide, half_wide(4 * chip, 4 * nx), in_vmem(*kinetic_x.shape),
+         in_vmem(width, width), in_vmem(2, nx, width), column, column, column, in_vmem(8, width)],
         cur, planes, pot, kinetic_x, kinetic_y, element_kinetic,
         scal=scal, cost=8, away=(2, 3, 4, 5),
-        scratch=[full, in_vmem(4, nx, width), in_vmem(2, nx, width), pltpu.SemaphoreType.DMA((5,)),
-                 in_vmem(*kinetic_x.shape), in_vmem(*kinetic_y.shape), in_vmem(*element_kinetic.shape),
-                 square, across, wide, in_vmem(width, width)],
-    )
-    pin, bin_ = passed(first, -1), passed(bridge, 1)
-    col3, first, bridge = call(
-        "third", functools.partial(third_body, nx, nz, width), [full, edge, edge],
-        col2, col1, pot, kz2, kx2, wy2, rcol,
-    )
-    first, bridge = call(
-        "edges", functools.partial(edges_body, 2.0), [edge] * 2, first, bridge, pin, bin_, coef, cost=1
-    )
-    plast, blast = passed(first, -1), passed(bridge, 1)
-    local, rows3 = call(
+        scratch=[full, in_vmem(4, nx, width), pltpu.SemaphoreType.DMA((5,)), in_vmem(*kinetic_y.shape),
+                 in_vmem(*element_kinetic.shape), square, across, wide],
+    )
+    col1, col2, left, right, first, bridge, rows1, rows2, pot = got[:9]
+    kz2, kx2, wy2, kx4, kx, ky, before, rcol, _, _, coef = got[9:]
+    edges = [passed(left, -1), passed(right, 1), passed(first, -2), passed(bridge, 2), first, bridge, coef]
+    (col3,) = call(
+        "third", functools.partial(third_body, nx, nz, width), [full], col2, col1, pot, kz2, kx2, wy2, rcol
+    )
+    keep, send = call(
         "fourth", functools.partial(fourth_body, nx, nz, width, chip),
-        [in_vmem(chip * (nz + PAD), width), here],
-        col3, pin, bin_, col2, pot, kz2, kx4, wy2, rcol,
-        scal=scal, scratch=[full], cost=2,
-    )
-    columns = [rows1, rows2, rows3]
-    keep, send = pl.pallas_call(
-        functools.partial(finish_body, nz, rows),
-        out_shape=[in_vmem(POWERS, size, width)] * 2,
-        in_specs=[pl.BlockSpec(memory_space=pltpu.SMEM)] + [vm()] * (4 + POWERS - 1),
-        out_specs=[vm()] * 2,
-        compiler_params=pltpu.CompilerParams(vmem_limit_bytes=LIMIT),
-        name="finish",
-    )(scal, local, plast, blast, rcol, *columns)
+        [in_vmem(POWERS, size, width)] * 2,
+        col3, col2, pot, kz2, kx4, wy2, rcol, kx, ky, before, *edges, rows1, rows2,
+        scal=scal, cost=2, scratch=[full, in_vmem(chip * (nz + PAD), width), in_vmem(2, nx, width)],
+    )
     recv = lax.ppermute(send, "trans", [(i, i ^ 1) for i in range(trans)])
     cols, gram = pl.pallas_call(
         gram_body,
@@ -577,7 +605,6 @@
         compiler_params=pltpu.CompilerParams(vmem_limit_bytes=LIMIT),
         name="gram",
     )(scal, packets.reshape(npack, size, width), keep, recv)
-    beam = lax.axis_size("beam")
     gram = jnp.sum(lax.all_to_all(gram, "trans", 0, 0, tiled=True), axis=0, keepdims=True)
     gram = lax.all_to_all(jnp.broadcast_to(gram, (beam, 1, width)), "beam", 0, 0, tiled=True)
     cells = float(nx * (width // 2) * nz * beam)

time: 151 us -> 152 us (level)
  blocking collectives: 69 us -> 66.2 us
  starting transfers between devices: 35.3 us -> 37.8 us
  Pallas kernels: 24.9 us -> 27.3 us
    pallas_call x7 -> x6, Pallas kernels: 14.5 us -> 17.6 us  [call(): pl.pallas_call(body, out_shape=outs, in_specs=specs, out_specs=[vm()] * l...]
    ppermute x8, starting transfers between devices: 21.7 us -> 24.2 us  [passed(): lax.ppermute(x, 'beam', [(i, i + by) for i in range(peers) if 0 <= i + by...]
    all_to_all x1, blocking collectives: 33.5 us -> 31.5 us  [shards(): lax.all_to_all(jnp.broadcast_to(gram, (beam, 1, width)), 'beam', 0, 0, ti...]
  transfers between devices with their start and end apart: 11 -> 11, of which waited for: 3 -> 2; matrix products, arithmetic and copies ran while one was open for 0% -> 0% of each run, Pallas kernels for 5% -> 4%
where the time goes in v4:
time: 152 us; the launch traced here: 151 us
  blocking collectives  66.2 us (44%)
  starting transfers between devices  37.8 us (25%)
  Pallas kernels  27.3 us (18%)
  between operations  14.2 us (9%)
  waiting for transfers between devices  3.73 us (2%)
  local copies, waits for them, and re-layouts  1.97 us (1%)
    all_to_all x1, blocking collectives, shards(): lax.all_to_all(jnp.broadcast_to(gram, (beam, 1, width)), 'beam', 0, 0, ti...  31.5 us
    all_gather x1, blocking collectives, shards(): planes = lax.all_gather(planes, 'trans')  26.6 us
    ppermute x8, starting transfers between devices, passed(): lax.ppermute(x, 'beam', [(i, i + by) for i in range(peers) if 0 <= i + by...  24.2 us
    pallas_call x6, Pallas kernels, call(): pl.pallas_call(body, out_shape=outs, in_specs=specs, out_specs=[vm()] * l...  17.6 us
    all_to_all x1, starting transfers between devices, shards(): lax.all_to_all(sent, 'trans', 0, 0, tiled=True).reshape(nx * nz, width)  10.4 us
    all_to_all x1, blocking collectives, shards(): lax.all_to_all(gram, 'trans', 0, 0, tiled=True)  8.06 us
    pallas_call x1, Pallas kernels, shards(): pl.pallas_call(functools.partial(basis_body, cells, rows), out_shape=[jax...  5.32 us
    ppermute x1, starting transfers between devices, shards(): recv = lax.ppermute(send, 'trans', [(i, i ^ 1) for i in range(trans)])  3.19 us
  transfers between devices with their start and end apart: 11, of which 2 were waited for; matrix products, arithmetic and copies ran while one was open for 0% of the time, Pallas kernels for 4%

profile of v4, /device:TPU:1, one launch (start us, length us, event | category | flops | bytes accessed | tf_op | source)
XLA Modules:
  0.0 151.3 jit_solution(10173312827120190431)
XLA Ops:
  7.2 0.7 all-gather.3.cloned.1.call-update
  7.9 1.0 copy-done
  8.9 1.3 copies.1
  10.3 10.4 %all-to-all-start = ((f32[8,512,128]{2,1,0:T(8,128)}), f32[8,512,128]{2,1,0:T(8,128)S(1)}, u32[]{:S(2)}, u32[]{:S(2)}) async-start(f32[8,512,128]{2,1,0:T(8,128)} %copies.1), calls=%async_computation | async-start | bytes 4194304 | tf_op jit(solution)/shard_map/all_to_all | solution.py:546
  20.8 0.7 vectors.1
  22.2 1.3 collective-permute-start
  23.5 4.0 %collective-permute-start.1 = (f32[32,128]{1,0:T(8,128)S(1)}, f32[32,128]{1,0:T(8,128)S(1)}, u32[]{:S(2)}, u32[]{:S(2)}) collective-permute-start(f32[32,128]{1,0:T(8,128)S(1)} %get-tuple-element.44), channel_id=1, source_target_pairs={{0,8},{8,16},{16,24},{24,32},{32,40},{40,48},{48,56},{56,64},{64,7... | collective-permute-start | bytes 49160 | tf_op jit(solution)/shard_map/ppermute | solution.py:23
  27.5 1.3 collective-permute-start.2
  28.8 5.5 %collective-permute-start.3 = (f32[16,128]{1,0:T(8,128)S(1)}, f32[16,128]{1,0:T(8,128)S(1)}, u32[]{:S(2)}, u32[]{:S(2)}) collective-permute-start(f32[16,128]{1,0:T(8,128)S(1)} %get-tuple-element.46.bridge_ref), channel_id=1, source_target_pairs={{0,16},{8,24},{16,32},{24,40},{32,48},{40,56},{48,64},{56,72},{64,... | collective-permute-start | bytes 24584 | tf_op jit(solution)/shard_map/ppermute | solution.py:23
  34.3 0.8 collective-permute-done.3.right2_ref
  35.6 26.6 %all-gather = f32[32,16,128]{2,1,0:T(8,128)S(1)} all-gather(f32[4,16,128]{2,1,0:T(8,128)S(1)} %edges.1), channel_id=2, replica_groups=mesh['beam'=64,'trans'=8] {'trans'}, dimensions={0}, use_global_device_ids=true | all-gather | bytes 294912 | tf_op jit(solution)/shard_map/all_gather | solution.py:572
  62.3 10.5 %pair.1 = (f32[4608,128]{1,0:T(8,128)S(1)}, f32[4608,128]{1,0:T(8,128)S(1)}, f32[128,128]{1,0:T(8,128)S(1)}, f32[128,128]{1,0:T(8,128)S(1)}, f32[64,128]{1,0:T(8...) custom-call(s32[4]{0:T(128)S(1)} %pad_add_fusion.scal, ...), custom_call_target="tpu_custom_call" | custom-call | flops 8000000000 | bytes 16000000 | tf_op jit(solution)/shard_map/pair/pallas_call | solution.py:385
  72.8 1.3 collective-permute-start.6
  74.1 5.5 %collective-permute-start.7 = (f32[64,128]{1,0:T(8,128)S(1)}, f32[64,128]{1,0:T(8,128)S(1)}, u32[]{:S(2)}, u32[]{:S(2)}) collective-permute-start(f32[64,128]{1,0:T(8,128)S(1)} %get-tuple-element.62.refs_12_), channel_id=1, source_target_pairs={{0,16},{8,24},{16,32},{24,40},{32,48},{40,56},{48,64},{56,72},{64,... | collective-permute-start | bytes 98312 | tf_op jit(solution)/shard_map/ppermute | solution.py:23
  79.6 1.3 collective-permute-start.4
  80.9 4.0 %collective-permute-start.5 = (f32[128,128]{1,0:T(8,128)S(1)}, f32[128,128]{1,0:T(8,128)S(1)}, u32[]{:S(2)}, u32[]{:S(2)}) collective-permute-start(f32[128,128]{1,0:T(8,128)S(1)} %get-tuple-element.60), channel_id=1, source_target_pairs={{0,8},{8,16},{16,24},{24,32},{32,40},{40,48},{48,56},{56,64},{64,7... | collective-permute-start | bytes 196616 | tf_op jit(solution)/shard_map/ppermute | solution.py:23
  84.9 3.0 %third.1.cur_ref = f32[4608,128]{1,0:T(8,128)S(1)} custom-call(f32[4608,128]{1,0:T(8,128)S(1)} %get-tuple-element.48.cur_ref.prev_ref, f32[4608,128]{1,0:T(8,128)S(1)} %get-tuple-element.49.prev_ref, f32[4096,128]{1,0:T(8,128)S(1)} %get-tuple-element.50.pot_ref, bf16[256,256]{1,0:T(8,128)(2,1)S(1)} %get-tuple-element.51.kz.refs_0_, ...), custom_call_target="tpu_custom_call" | custom-call | flops 4000000000 | bytes 8000000 | tf_op jit(solution)/shard_map/third/pallas_call | solution.py:385
  88.0 2.4 %fourth.1 = (f32[4,512,128]{2,1,0:T(8,128)S(1)}, f32[4,512,128]{2,1,0:T(8,128)S(1)}) custom-call(s32[4]{0:T(128)S(1)} %pad_add_fusion.scal, f32[4608,128]{1,0:T(8,128)S(1)} %third.1.cur_ref, f32[4608,128]{1,0:T(8,128)S(1)} %get-tuple-element.48.cur_ref.prev_ref, f32[4096,128]{1,0:T(8,128)S(1)} %get-tuple-element.50.pot_ref, ...), custom_call_target="tpu_custom_call" | custom-call | flops 2000000000 | bytes 4000000 | tf_op jit(solution)/shard_map/fourth/pallas_call | solution.py:385
  90.4 3.2 %collective-permute-start.8 = (f32[4,512,128]{2,1,0:T(8,128)S(1)}, f32[4,512,128]{2,1,0:T(8,128)S(1)}, u32[]{:S(2)}, u32[]{:S(2)}) collective-permute-start(f32[4,512,128]{2,1,0:T(8,128)S(1)} %get-tuple-element.67), channel_id=1, source_target_pairs={{0,1},{1,0},{2,3},{3,2},{4,5},{5,4},{6,7},{7,6},{8,9},{9,8},{10,11... | collective-permute-start | bytes 3145736 | tf_op jit(solution)/shard_map/ppermute | solution.py:598
  93.6 2.3 %collective-permute-done.8.recv_ref = f32[4,512,128]{2,1,0:T(8,128)S(1)} collective-permute-done((f32[4,512,128]{2,1,0:T(8,128)S(1)}, f32[4,512,128]{2,1,0:T(8,128)S(1)}, u32[]{:S(2)}, u32[]{:S(2)}) %collective-permute-start.8) | collective-permute-done | bytes 1048608 | tf_op jit(solution)/shard_map/ppermute | solution.py:598
  95.9 3.0 %gram.1 = (f32[10,512,128]{2,1,0:T(8,128)S(1)}, f32[8,1,128]{2,1,0:T(1,128)S(1)}) custom-call(s32[4]{0:T(128)S(1)} %pad_add_fusion.scal, f32[2,512,128]{2,1,0:T(8,128)S(1)} %bitcast.12, f32[4,512,128]{2,1,0:T(8,128)S(1)} %get-tuple-element.66.keep_ref, f32[4,512,128]{2,1,0:T(8,128)S(1)} %collective-permute-done.8.recv_ref), custom_call_target="tpu_custom_call" | custom-call | tf_op jit(solution)/shard_map/gram/pallas_call | solution.py:599
  98.9 8.1 %all_to_all.15 = f32[8,1,128]{2,1,0:T(1,128)S(1)} all-to-all(f32[8,1,128]{2,1,0:T(1,128)S(1)} %get-tuple-element.68), channel_id=1, replica_groups=mesh['beam'=64,'trans'=8] {'trans'}, dimensions={0} | all-to-all | bytes 8192 | tf_op jit(solution)/shard_map/all_to_all | solution.py:608
  107.0 31.5 %all_to_all.16.gram_ref = f32[64,1,128]{2,1,0:T(1,128)S(1)} all-to-all(f32[64,1,128]{2,1,0:T(1,128)S(1)} %broadcast_in_dim.2), channel_id=1, replica_groups=mesh['beam'=64,'trans'=8] {'beam'}, dimensions={0} | all-to-all | bytes 65536 | tf_op jit(solution)/shard_map/all_to_all | solution.py:609
  138.5 5.3 %basis.1 = (f32[10,512,128]{2,1,0:T(8,128)}, f32[2,16,128]{2,1,0:T(8,128)S(1)}) custom-call(f32[64,1,128]{2,1,0:T(1,128)S(1)} %all_to_all.16.gram_ref, f32[10,512,128]{2,1,0:T(8,128)S(1)} %get-tuple-element.69.cols_ref), custom_call_target="tpu_custom_call" | custom-call | tf_op jit(solution)/shard_map/basis/pallas_call | solution.py:611
  (23 shorter events, 2.0 us)
Async XLA Ops:
  7.2 55.1 %all-gather.3.cloned.1.call-start = ((), (), s32[]{:S(2)}) async-start(), calls=%async_computation.3 | async-start | bytes 2359296 | tf_op jit(solution)/shard_map/all_gather | solution.py:536
  7.9 1.0 copy-start
  10.3 10.5 %copy-start.3 = (f32[65,65]{1,0:T(8,128)S(1)}, f32[65,65]{1,0:T(8,128)}, u32[]{:S(2)}) copy-start(f32[65,65]{1,0:T(8,128)} %ek_hbm.1) | copy-start | bytes 50704
  10.3 52.0 %all-to-all-start = ((f32[8,512,128]{2,1,0:T(8,128)}), f32[8,512,128]{2,1,0:T(8,128)S(1)}, u32[]{:S(2)}, u32[]{:S(2)}) async-start(f32[8,512,128]{2,1,0:T(8,128)} %copies.1), calls=%async_computation | async-start | bytes 4194304 | tf_op jit(solution)/shard_map/all_to_all | solution.py:546
  20.7 1.0 copy-start.1
  20.7 1.1 copy-start.2
  22.2 12.9 %collective-permute-start = (f32[32,128]{1,0:T(8,128)S(1)}, f32[32,128]{1,0:T(8,128)S(1)}, u32[]{:S(2)}, u32[]{:S(2)}) collective-permute-start(f32[32,128]{1,0:T(8,128)S(1)} %get-tuple-element.43), channel_id=1, source_target_pairs={{8,0},{16,8},{24,16},{32,24},{40,32},{48,40},{56,48},{64,56},{72,6... | collective-permute-start | bytes 49160 | tf_op jit(solution)/shard_map/ppermute | solution.py:23
  23.5 11.6 %collective-permute-start.1 = (f32[32,128]{1,0:T(8,128)S(1)}, f32[32,128]{1,0:T(8,128)S(1)}, u32[]{:S(2)}, u32[]{:S(2)}) collective-permute-start(f32[32,128]{1,0:T(8,128)S(1)} %get-tuple-element.44), channel_id=1, source_target_pairs={{0,8},{8,16},{16,24},{24,32},{32,40},{40,48},{48,56},{56,64},{64,7... | collective-permute-start | bytes 49160 | tf_op jit(solution)/shard_map/ppermute | solution.py:23
  27.5 6.8 %collective-permute-start.2 = (f32[16,128]{1,0:T(8,128)S(1)}, f32[16,128]{1,0:T(8,128)S(1)}, u32[]{:S(2)}, u32[]{:S(2)}) collective-permute-start(f32[16,128]{1,0:T(8,128)S(1)} %get-tuple-element.45.first_ref), channel_id=1, source_target_pairs={{16,0},{24,8},{32,16},{40,24},{48,32},{56,40},{64,48},{72,56},{80,... | collective-permute-start | bytes 24584 | tf_op jit(solution)/shard_map/ppermute | solution.py:23
  28.8 6.3 %collective-permute-start.3 = (f32[16,128]{1,0:T(8,128)S(1)}, f32[16,128]{1,0:T(8,128)S(1)}, u32[]{:S(2)}, u32[]{:S(2)}) collective-permute-start(f32[16,128]{1,0:T(8,128)S(1)} %get-tuple-element.46.bridge_ref), channel_id=1, source_target_pairs={{0,16},{8,24},{16,32},{24,40},{32,48},{40,56},{48,64},{56,72},{64,... | collective-permute-start | bytes 24584 | tf_op jit(solution)/shard_map/ppermute | solution.py:23
  72.8 15.1 %collective-permute-start.6 = (f32[64,128]{1,0:T(8,128)S(1)}, f32[64,128]{1,0:T(8,128)S(1)}, u32[]{:S(2)}, u32[]{:S(2)}) collective-permute-start(f32[64,128]{1,0:T(8,128)S(1)} %get-tuple-element.61.refs_11_), channel_id=1, source_target_pairs={{16,0},{24,8},{32,16},{40,24},{48,32},{56,40},{64,48},{72,56},{80,... | collective-permute-start | bytes 98312 | tf_op jit(solution)/shard_map/ppermute | solution.py:23
  74.1 13.8 %collective-permute-start.7 = (f32[64,128]{1,0:T(8,128)S(1)}, f32[64,128]{1,0:T(8,128)S(1)}, u32[]{:S(2)}, u32[]{:S(2)}) collective-permute-start(f32[64,128]{1,0:T(8,128)S(1)} %get-tuple-element.62.refs_12_), channel_id=1, source_target_pairs={{0,16},{8,24},{16,32},{24,40},{32,48},{40,56},{48,64},{56,72},{64,... | collective-permute-start | bytes 98312 | tf_op jit(solution)/shard_map/ppermute | solution.py:23
  79.6 8.3 %collective-permute-start.4 = (f32[128,128]{1,0:T(8,128)S(1)}, f32[128,128]{1,0:T(8,128)S(1)}, u32[]{:S(2)}, u32[]{:S(2)}) collective-permute-start(f32[128,128]{1,0:T(8,128)S(1)} %get-tuple-element.59), channel_id=1, source_target_pairs={{8,0},{16,8},{24,16},{32,24},{40,32},{48,40},{56,48},{64,56},{72,6... | collective-permute-start | bytes 196616 | tf_op jit(solution)/shard_map/ppermute | solution.py:23
  80.9 7.1 %collective-permute-start.5 = (f32[128,128]{1,0:T(8,128)S(1)}, f32[128,128]{1,0:T(8,128)S(1)}, u32[]{:S(2)}, u32[]{:S(2)}) collective-permute-start(f32[128,128]{1,0:T(8,128)S(1)} %get-tuple-element.60), channel_id=1, source_target_pairs={{0,8},{8,16},{16,24},{24,32},{32,40},{40,48},{48,56},{56,64},{64,7... | collective-permute-start | bytes 196616 | tf_op jit(solution)/shard_map/ppermute | solution.py:23
  90.4 5.5 %collective-permute-start.8 = (f32[4,512,128]{2,1,0:T(8,128)S(1)}, f32[4,512,128]{2,1,0:T(8,128)S(1)}, u32[]{:S(2)}, u32[]{:S(2)}) collective-permute-start(f32[4,512,128]{2,1,0:T(8,128)S(1)} %get-tuple-element.67), channel_id=1, source_target_pairs={{0,1},{1,0},{2,3},{3,2},{4,5},{5,4},{6,7},{7,6},{8,9},{9,8},{10,11... | collective-permute-start | bytes 3145736 | tf_op jit(solution)/shard_map/ppermute | solution.py:598
Sparse Core Ops, SparseCore 0:
  10.1 47.1 all-gather.2

commit v5 on v3

--- a/solution.py
+++ b/solution.py
@@ -225,9 +225,9 @@
 
 
 def pair_body(nx, nz, width, chip, scal, cur_ref, gathered_ref, pot_hbm, kx_hbm, ky_hbm, ek_hbm, *refs):
-    one_ref, two_ref, first_ref, bridge_ref, rows1_ref, rows2_ref, pot_ref = refs[:7]
-    kz2, kx2, wy2, kx4, rcol, coef = refs[7:13]
-    col_ref, planes_ref, halo_ref, sems, kx_ref, ky_raw, ek_ref, kz1, kx1, wy1, ky_ref = refs[13:]
+    one_ref, two_ref, first_ref, bridge_ref, pot_ref = refs[:5]
+    kz2, kx2, wy2, kx4, rcol, coef = refs[5:11]
+    col_ref, planes_ref, halo_ref, sems, kx_ref, ky_raw, ek_ref, kz1, kx1, wy1, ky_ref = refs[11:]
     stride = nz + PAD
     small = [
         pltpu.make_async_copy(src, dst, sems.at[2 + i])
@@ -279,12 +279,17 @@
         (rcol, halo_ref.at[0], halo_ref.at[1], 2.0), 2.0, (two_ref, 0, nx), bridge_ref,
     )
     first_ref[...] = two_ref[pl.ds(0, nx, stride=stride), :]
-    for ref, rows_ref in ((one_ref, rows1_ref), (two_ref, rows2_ref)):
-        for q in range(chip):
-            rows_ref[q * nz : (q + 1) * nz, :] = ref[rows_of(scal[0] + q, stride, nz), :]
-
-
-def third_body(nx, nz, width, cur_ref, prev_ref, pot_ref, kz, kx, wy, rcol, out_ref, first_ref, bridge_ref):
+
+
+def part_rows(scal, chip, nz, ref, stride, base, keep_ref, send_ref, k):
+    rows = chip // 2
+    for to_ref, core in ((keep_ref, scal[1]), (send_ref, 1 - scal[1])):
+        for r in range(rows):
+            to_ref[k, r * nz : (r + 1) * nz, :] = ref[rows_of(base + core * rows + r, stride, nz), :]
+
+
+def third_body(nx, nz, width, chip, scal, cur_ref, prev_ref, pot_ref, kz, kx, wy, rcol, *outs):
+    out_ref, first_ref, bridge_ref, keep_ref, send_ref = outs
     stride = nz + PAD
     apply_local(
         nx, nz, width, (pot_ref, kz, kx, wy, rcol), (cur_ref, stride),
@@ -292,10 +297,12 @@
         (out_ref, 0, nx), bridge_ref,
     )
     first_ref[...] = out_ref[pl.ds(0, nx, stride=stride), :]
+    for k, ref in enumerate((prev_ref, cur_ref)):
+        part_rows(scal, chip, nz, ref, stride, scal[0], keep_ref, send_ref, k)
 
 
 def fourth_body(nx, nz, width, chip, scal, cur_ref, pin_ref, bin_ref, prev_ref, pot_ref, *refs):
-    kz, kx, wy, rcol, out_ref, rows_ref, col_ref = refs
+    kz, kx, wy, rcol, out_ref, keep_ref, send_ref, col_ref = refs
     stride = nz + PAD
 
     def complete(x):
@@ -303,8 +310,7 @@
         col_ref[rows_of(x, stride, nz), :] = u
 
     repeat(nx, 16, only(complete), 0)
-    for q in range(chip):
-        rows_ref[q * nz : (q + 1) * nz, :] = col_ref[rows_of(scal[0] + q, stride, nz), :]
+    part_rows(scal, chip, nz, col_ref, stride, scal[0], keep_ref, send_ref, 0)
     apply_local(
         nx, nz, width, (pot_ref, kz, kx, wy, rcol), (col_ref, stride),
         lambda x: col_ref[rows_of(x, stride, nz), :], (prev_ref, stride), None, 2.0,
@@ -342,42 +348,31 @@
     )(*ins)
 
 
-def finish_body(nz, rows, scal, last_ref, pin_ref, bin_ref, rcol_ref, *refs):
-    cols = refs[: POWERS - 1]
-    keep_ref, send_ref = refs[POWERS - 1 :]
-    core = scal[1]
-    size = rows * nz
+def finish_body(nz, rows, scal, last_ref, pin_ref, bin_ref, rcol_ref, keep_ref, send_ref):
     halo = (rcol_ref, pin_ref, bin_ref, 2.0)
-    for ref, where in ((keep_ref, core), (send_ref, 1 - core)):
-        at = pl.ds(pl.multiple_of(where * size, size), size)
-        for k in range(POWERS - 1):
-            ref[k] = cols[k][at, :]
+    for ref, where in ((keep_ref, scal[1]), (send_ref, 1 - scal[1])):
         for r in range(rows):
             x = where * rows + r
             u = with_halo(last_ref[rows_of(x, nz + PAD, nz), :], halo, scal[0] + x)
-            ref[POWERS - 1, r * nz : (r + 1) * nz, :] = u
-
-
-def gram_body(scal, packets_ref, keep_ref, recv_ref, cols_ref, gram_ref, acc_ref):
-    core = scal[1]
-    ncol, size, width = cols_ref.shape
-    npow = ncol // 2
+            ref[0, r * nz : (r + 1) * nz, :] = u
+
+
+EARLY = 3
+
+
+def at_column(cols, c):
+    p, k = divmod(c, POWERS + 1)
+    if k < EARLY:
+        return cols[0], p * EARLY + k
+    return cols[1], p * (POWERS + 1 - EARLY) + k - EARLY
+
+
+def add_products(cols, groups, acc_ref):
+    ncol = 2 * (POWERS + 1)
+    _, size, width = cols[0].shape
     half = width // 2
-    cols_ref[0] = packets_ref[0]
-    cols_ref[npow] = packets_ref[1]
-    for k in range(npow - 1):
-        cols_ref[core * npow + 1 + k] = keep_ref[k]
-        cols_ref[(1 - core) * npow + 1 + k] = recv_ref[k]
-    acc_ref[...] = jnp.zeros_like(acc_ref)
     sign = jnp.where(lax.broadcasted_iota(jnp.int32, (8, width), 1) < half, 1.0, -1.0)
-    first, second = list(range(npow)), list(range(npow, ncol))
-    groups = [
-        [(a, b) for a in first for b in first if a <= b],
-        [(a, b) for a in second for b in second if a <= b],
-        [(a, b) for a in first for b in second[:3]],
-        [(a, b) for a in first for b in second[3:]],
-    ]
-    unroll = 16
+    unroll = 32
     for pairs in groups:
         used = sorted({c for pair in pairs for c in pair})
         turned = sorted({b for a, b in pairs if a != b})
@@ -386,7 +381,10 @@
             sums = list(sums)
             for q in range(unroll):
                 at = pl.ds(pl.multiple_of((i * unroll + q) * 8, 8), 8)
-                v = {c: cols_ref[c, at, :] for c in used}
+                v = {}
+                for c in used:
+                    ref, n = at_column(cols, c)
+                    v[c] = ref[n, at, :]
                 t = {c: pltpu.roll(v[c], half, 1) for c in turned}
                 n = 0
                 for a, b in pairs:
@@ -410,12 +408,48 @@
                     sums[n] * sign, axis=0, keepdims=True
                 )
                 n += 1
+
+
+def column_sets():
+    first = list(range(POWERS + 1))
+    second = [POWERS + 1 + k for k in first]
+    old = lambda c: c % (POWERS + 1) < EARLY
+    inside = [[(a, b) for a in cols for b in cols if a <= b] for cols in (first, second)]
+    across = [(a, b) for a in first for b in second]
+    early = [[p for p in inside[0] + inside[1] if old(p[0]) and old(p[1])]]
+    early.append([p for p in across if old(p[0]) and old(p[1])])
+    late = [[p for p in pairs if not (old(p[0]) and old(p[1]))] for pairs in inside]
+    late.append([p for p in across if old(p[0]) and not old(p[1])])
+    late.append([p for p in across if not old(p[0])])
+    return early, late
+
+
+def early_body(scal, packets_ref, keep_ref, recv_ref, cols_ref, acc_ref):
+    core = scal[1]
+    for p in range(2):
+        cols_ref[p * EARLY] = packets_ref[p]
+    for k in range(EARLY - 1):
+        cols_ref[core * EARLY + 1 + k] = keep_ref[k]
+        cols_ref[(1 - core) * EARLY + 1 + k] = recv_ref[k]
+    acc_ref[...] = jnp.zeros_like(acc_ref)
+    add_products((cols_ref, None), column_sets()[0], acc_ref)
+
+
+def gram_body(scal, early_ref, part_ref, keep3, recv3, keep4, recv4, cols_ref, gram_ref, acc_ref):
+    core = scal[1]
+    later = POWERS + 1 - EARLY
+    for k, (mine, other) in enumerate(((keep3, recv3), (keep4, recv4))):
+        cols_ref[core * later + k] = mine[0]
+        cols_ref[(1 - core) * later + k] = other[0]
+    acc_ref[...] = part_ref[...]
+    add_products((early_ref, cols_ref), column_sets()[1], acc_ref)
     row = jnp.sum(acc_ref[...].T, axis=0, keepdims=True)
     gram_ref[...] = jnp.broadcast_to(row[None], gram_ref.shape)
 
 
-def basis_body(cells, rows, gram_ref, cols_ref, basis_ref, factor_ref, coef_ref, out_ref, sems):
-    ncol, size, width = cols_ref.shape
+def basis_body(cells, rows, gram_ref, early_ref, late_ref, basis_ref, factor_ref, coef_ref, out_ref, sems):
+    ncol, size, width = out_ref.shape
+    cols = (early_ref, late_ref)
     half = width // 2
     row = jnp.sum(gram_ref[...], axis=0) * (1.0 / cells)
     r = lax.broadcasted_iota(jnp.int32, (16, width), 0)
@@ -443,9 +477,9 @@
         below = r > j
         re = re - jnp.where(below, col_re * row_re - col_im * row_im, 0.0)
         im = im - jnp.where(below, col_re * row_im + col_im * row_re, 0.0)
-    keep = (c >= r) & (c < ncol)
-    factor_ref[0] = jnp.where(keep, up_re, 0.0)
-    factor_ref[1] = jnp.where(keep & (c > r), up_im, 0.0)
+    for q, up in ((0, jnp.where(c >= r, up_re, 0.0)), (1, jnp.where(c > r, up_im, 0.0))):
+        for k in range(ncol):
+            factor_ref[k, q : q + 1, :] = up[k : k + 1, :ncol]
     sign = jnp.where(lax.broadcasted_iota(jnp.int32, (8, width), 1) < half, 1.0, -1.0)
     for k in range(ncol):
         for i in range(k + 1):
@@ -455,11 +489,14 @@
             )
     group = 4
     each = size // rows
-    copies = []
-    for r in range(rows):
-        for start in range(r * each, (r + 1) * each, 8 * group):
-            slots = [slice(start + 8 * g, start + 8 * g + 8) for g in range(group)]
-            v = [[cols_ref[i, s, :] for s in slots] for i in range(ncol)]
+
+    def row(r, carry):
+        for start in range(0, each, 8 * group):
+            slots = [pl.ds(pl.multiple_of(r * each + start + 8 * g, 8), 8) for g in range(group)]
+            v = []
+            for i in range(ncol):
+                ref, n = at_column(cols, i)
+                v.append([ref[n, s, :] for s in slots])
             t = [[pltpu.roll(x, half, 1) for x in xs] for xs in v]
             for k in range(ncol):
                 total = [None] * group
@@ -473,12 +510,16 @@
                         total[g] = term if total[g] is None else total[g] + term
                 for g in range(group):
                     out_ref[k, slots[g], :] = total[g]
-        part = pl.ds(r * each, each)
-        copy = pltpu.make_async_copy(out_ref.at[:, part, :], basis_ref.at[:, part, :], sems.at[r])
-        copy.start()
-        copies.append(copy)
-    for copy in copies:
-        copy.wait()
+        copy(r).start()
+        return carry
+
+    def copy(r):
+        part = pl.ds(pl.multiple_of(r * each, 8), each)
+        return pltpu.make_async_copy(out_ref.at[:, part, :], basis_ref.at[:, part, :], sems.at[r])
+
+    lax.fori_loop(0, rows, row, 0)
+    for r in range(rows):
+        copy(r).wait()
 
 
 def shards(packets, kinetic_x, kinetic_y, element_kinetic, potential):
@@ -487,6 +528,7 @@
     nx = rows * trans
     ncol = npack * (POWERS + 1)
     me = lax.axis_index("trans")
+    beam = lax.axis_size("beam")
     core = me % 2
     chip = 2 * rows
     scal = jnp.stack([(me // 2) * chip, core, lax.axis_index("beam")]).astype(jnp.int32)
@@ -532,10 +574,9 @@
     planes = lax.all_gather(planes, "trans")
 
     full, edge = in_vmem(nx * (nz + PAD), width), in_vmem(nx, width)
-    here = in_vmem(chip * nz, width)
-    col1, col2, first, bridge, rows1, rows2, pot, kz2, kx2, wy2, kx4, rcol, coef = call(
+    col1, col2, first, bridge, pot, kz2, kx2, wy2, kx4, rcol, coef = call(
         "pair", functools.partial(pair_body, nx, nz, width, chip),
-        [full, full, edge, edge, here, here, in_vmem(nx * nz, width),
+        [full, full, edge, edge, in_vmem(nx * nz, width),
          square, across, wide, half_wide(4 * chip, 4 * nx), column, in_vmem(8, width)],
         cur, planes, pot, kinetic_x, kinetic_y, element_kinetic,
         scal=scal, cost=8, away=(2, 3, 4, 5),
@@ -544,40 +585,41 @@
                  square, across, wide, in_vmem(width, width)],
     )
     pin, bin_ = passed(first, -1), passed(bridge, 1)
-    col3, first, bridge = call(
-        "third", functools.partial(third_body, nx, nz, width), [full, edge, edge],
-        col2, col1, pot, kz2, kx2, wy2, rcol,
-    )
+    col3, first, bridge, keep, send = call(
+        "third", functools.partial(third_body, nx, nz, width, chip),
+        [full, edge, edge, in_vmem(2, size, width), in_vmem(2, size, width)],
+        col2, col1, pot, kz2, kx2, wy2, rcol, scal=scal,
+    )
+
+    def other_core(x):
+        return lax.ppermute(x, "trans", [(i, i ^ 1) for i in range(trans)])
+
+    recv = other_core(send)
     first, bridge = call(
         "edges", functools.partial(edges_body, 2.0), [edge] * 2, first, bridge, pin, bin_, coef, cost=1
     )
     plast, blast = passed(first, -1), passed(bridge, 1)
-    local, rows3 = call(
+    one = in_vmem(1, size, width)
+    local, keep3, send3 = call(
         "fourth", functools.partial(fourth_body, nx, nz, width, chip),
-        [in_vmem(chip * (nz + PAD), width), here],
+        [in_vmem(chip * (nz + PAD), width), one, one],
         col3, pin, bin_, col2, pot, kz2, kx4, wy2, rcol,
         scal=scal, scratch=[full], cost=2,
     )
-    columns = [rows1, rows2, rows3]
-    keep, send = pl.pallas_call(
-        functools.partial(finish_body, nz, rows),
-        out_shape=[in_vmem(POWERS, size, width)] * 2,
-        in_specs=[pl.BlockSpec(memory_space=pltpu.SMEM)] + [vm()] * (4 + POWERS - 1),
-        out_specs=[vm()] * 2,
-        compiler_params=pltpu.CompilerParams(vmem_limit_bytes=LIMIT),
-        name="finish",
-    )(scal, local, plast, blast, rcol, *columns)
-    recv = lax.ppermute(send, "trans", [(i, i ^ 1) for i in range(trans)])
-    cols, gram = pl.pallas_call(
-        gram_body,
-        out_shape=[in_vmem(ncol, size, width), in_vmem(trans, 1, width)],
-        in_specs=[pl.BlockSpec(memory_space=pltpu.SMEM)] + [vm()] * 3,
-        out_specs=[vm()] * 2,
-        scratch_shapes=[pltpu.VMEM((128, width), F32)],
-        compiler_params=pltpu.CompilerParams(vmem_limit_bytes=LIMIT),
-        name="gram",
-    )(scal, packets.reshape(npack, size, width), keep, recv)
-    beam = lax.axis_size("beam")
+    recv3 = other_core(send3)
+    early, part = call(
+        "early", early_body, [in_vmem(npack * EARLY, size, width), in_vmem(128, width)],
+        flat, keep, recv, scal=scal, cost=1,
+    )
+    keep4, send4 = call(
+        "finish", functools.partial(finish_body, nz, rows), [one, one],
+        local, plast, blast, rcol, scal=scal, cost=1,
+    )
+    recv4 = other_core(send4)
+    late, gram = call(
+        "gram", gram_body, [in_vmem(ncol - npack * EARLY, size, width), in_vmem(trans, 1, width)],
+        early, part, keep3, recv3, keep4, recv4, scal=scal, scratch=[in_vmem(128, width)], cost=1,
+    )
     gram = jnp.sum(lax.all_to_all(gram, "trans", 0, 0, tiled=True), axis=0, keepdims=True)
     gram = lax.all_to_all(jnp.broadcast_to(gram, (beam, 1, width)), "beam", 0, 0, tiled=True)
     cells = float(nx * (width // 2) * nz * beam)
@@ -585,9 +627,9 @@
         functools.partial(basis_body, cells, rows),
         out_shape=[
             jax.ShapeDtypeStruct((ncol, size, width), F32),
-            jax.ShapeDtypeStruct((2, 16, width), F32),
+            jax.ShapeDtypeStruct((ncol, 2, ncol), F32),
         ],
-        in_specs=[vm(), vm()],
+        in_specs=[vm(), vm(), vm()],
         out_specs=[pl.BlockSpec(memory_space=pl.ANY), vm()],
         scratch_shapes=[
             pltpu.VMEM((2, ncol * ncol, 8, width), F32),
@@ -596,8 +638,8 @@
         ],
         compiler_params=pltpu.CompilerParams(vmem_limit_bytes=LIMIT),
         name="basis",
-    )(gram, cols)
-    return basis.reshape(ncol, rows, nz, width), factor[:, :ncol, :ncol]
+    )(gram, early, late)
+    return basis.reshape(ncol, rows, nz, width), factor.transpose(1, 0, 2)
 
 
 def solution(mesh):

time: 151 us -> 151 us (level)
  starting transfers between devices: 35.3 us -> 39.2 us
  waiting for transfers between devices: 4.5 us -> 2.26 us
    pallas_call x7 -> x10, Pallas kernels: 14.5 us -> 19.2 us  [call(): pl.pallas_call(body, out_shape=outs, in_specs=specs, out_specs=[vm()] * l...]
    ppermute x1 -> x3, starting transfers between devices: 3.18 us -> 7.04 us  [other_core(): return lax.ppermute(x, 'trans', [(i, i ^ 1) for i in range(trans)])]
    pallas_call x2 -> x0, Pallas kernels: 3.73 us -> none  [the longest x1 3.03 us: shards(): pl.pallas_call(gram_body, out_shape=[in_vmem(ncol, size, width), in_vmem(...]
    ppermute x1 -> x3, waiting for transfers between devices: 2.26 us -> 0.03 us  [other_core(): return lax.ppermute(x, 'trans', [(i, i ^ 1) for i in range(trans)])]
  transfers between devices with their start and end apart: 11 -> 13, of which waited for: 3 -> 2; matrix products, arithmetic and copies ran while one was open for 0% -> 0% of each run, Pallas kernels for 5% -> 7%
where the time goes in v5:
time: 151 us; the launch traced here: 150 us
  blocking collectives  67.7 us (45%)
  starting transfers between devices  39.2 us (26%)
  Pallas kernels  25.4 us (17%)
  between operations  14.3 us (9%)
  waiting for transfers between devices  2.26 us (1%)
    all_to_all x1, blocking collectives, shards(): lax.all_to_all(jnp.broadcast_to(gram, (beam, 1, width)), 'beam', 0, 0, ti...  32.1 us
    all_gather x1, blocking collectives, shards(): planes = lax.all_gather(planes, 'trans')  27.4 us
    ppermute x8, starting transfers between devices, passed(): lax.ppermute(x, 'beam', [(i, i + by) for i in range(peers) if 0 <= i + by...  21.7 us
    pallas_call x10, Pallas kernels, call(): pl.pallas_call(body, out_shape=outs, in_specs=specs, out_specs=[vm()] * l...  19.2 us
    all_to_all x1, starting transfers between devices, shards(): lax.all_to_all(sent, 'trans', 0, 0, tiled=True).reshape(nx * nz, width)  10.4 us
    all_to_all x1, blocking collectives, shards(): lax.all_to_all(gram, 'trans', 0, 0, tiled=True)  8.17 us
    ppermute x3, starting transfers between devices, other_core(): return lax.ppermute(x, 'trans', [(i, i ^ 1) for i in range(trans)])  7.04 us
    pallas_call x1, Pallas kernels, shards(): pl.pallas_call(functools.partial(basis_body, cells, rows), out_shape=[jax...  4.9 us
  transfers between devices with their start and end apart: 13, of which 2 were waited for; matrix products, arithmetic and copies ran while one was open for 0% of the time, Pallas kernels for 7%

profile of v5, /device:TPU:1, one launch (start us, length us, event | category | flops | bytes accessed | tf_op | source)
XLA Modules:
  0.0 150.3 jit_solution(5985084844483618355)
XLA Ops:
  7.9 1.0 copy-done
  8.9 1.3 copies.1
  10.3 10.4 %all-to-all-start = ((f32[8,512,128]{2,1,0:T(8,128)}), f32[8,512,128]{2,1,0:T(8,128)S(1)}, u32[]{:S(2)}, u32[]{:S(2)}) async-start(f32[8,512,128]{2,1,0:T(8,128)} %copies.1), calls=%async_computation | async-start | bytes 4194304 | tf_op jit(solution)/shard_map/all_to_all | solution.py:549
  22.2 1.3 collective-permute-start
  23.5 4.0 %collective-permute-start.1 = (f32[16,128]{1,0:T(8,128)S(1)}, f32[16,128]{1,0:T(8,128)S(1)}, u32[]{:S(2)}, u32[]{:S(2)}) collective-permute-start(f32[16,128]{1,0:T(8,128)S(1)} %get-tuple-element.51), channel_id=1, source_target_pairs={{0,8},{8,16},{16,24},{24,32},{32,40},{40,48},{48,56},{56,64},{64,7... | collective-permute-start | bytes 24584 | tf_op jit(solution)/shard_map/ppermute | solution.py:23
  27.5 0.8 collective-permute-done.1.bin_ref
  28.3 1.3 collective-permute-start.2
  29.6 4.5 %collective-permute-start.3 = (f32[16,128]{1,0:T(8,128)S(1)}, f32[16,128]{1,0:T(8,128)S(1)}, u32[]{:S(2)}, u32[]{:S(2)}) collective-permute-start(f32[16,128]{1,0:T(8,128)S(1)} %get-tuple-element.56), channel_id=1, source_target_pairs={{0,8},{8,16},{16,24},{24,32},{32,40},{40,48},{48,56},{56,64},{64,7... | collective-permute-start | bytes 24584 | tf_op jit(solution)/shard_map/ppermute | solution.py:23
  34.9 27.4 %all-gather = f32[32,16,128]{2,1,0:T(8,128)S(1)} all-gather(f32[4,16,128]{2,1,0:T(8,128)S(1)} %pad_maximum_fusion), channel_id=2, replica_groups=mesh['beam'=64,'trans'=8] {'trans'}, dimensions={0}, use_global_device_ids=true | all-gather | bytes 294912 | tf_op jit(solution)/shard_map/all_gather | solution.py:574
  62.3 8.3 %pair.1 = (f32[4608,128]{1,0:T(8,128)S(1)}, f32[4608,128]{1,0:T(8,128)S(1)}, f32[64,128]{1,0:T(8,128)S(1)}, f32[64,128]{1,0:T(8,128)S(1)}, f32[4096,128]{1,0:T(8...) custom-call(s32[3]{0:T(128)S(1)} %pad_add_fusion.scal, ...), custom_call_target="tpu_custom_call" | custom-call | flops 8000000000 | bytes 16000000 | tf_op jit(solution)/shard_map/pair/pallas_call | solution.py:337
  70.6 1.3 collective-permute-start.5
  71.9 4.0 %collective-permute-start.6 = (f32[64,128]{1,0:T(8,128)S(1)}, f32[64,128]{1,0:T(8,128)S(1)}, u32[]{:S(2)}, u32[]{:S(2)}) collective-permute-start(f32[64,128]{1,0:T(8,128)S(1)} %get-tuple-element.70), channel_id=1, source_target_pairs={{0,8},{8,16},{16,24},{24,32},{32,40},{40,48},{48,56},{56,64},{64,7... | collective-permute-start | bytes 98312 | tf_op jit(solution)/shard_map/ppermute | solution.py:23
  75.9 3.7 %third.1 = (f32[4608,128]{1,0:T(8,128)S(1)}, f32[64,128]{1,0:T(8,128)S(1)}, f32[64,128]{1,0:T(8,128)S(1)}, f32[2,512,128]{2,1,0:T(8,128)S(1)}, f32[2,512,128]{2,1,0:T(8,128)S(1)}) custom-call(s32[3]{0:T(128)S(1)} %pad_add_fusion.scal, f32[4608,128]{1,0:T(8,128)S(1)} %get-tuple-element.57.cur_ref.prev_ref, f32[4608,128]{1,0:T(8,128)S(1)} %get-tuple-element.58.prev_ref, ...), custom_call_target="tpu_custom_call" | custom-call | flops 4000000000 | bytes 8000000 | tf_op jit(solution)/shard_map/third/pallas_call | solution.py:337
  79.6 2.6 %collective-permute-start.4 = (f32[2,512,128]{2,1,0:T(8,128)S(1)}, f32[2,512,128]{2,1,0:T(8,128)S(1)}, u32[]{:S(2)}, u32[]{:S(2)}) collective-permute-start(f32[2,512,128]{2,1,0:T(8,128)S(1)} %get-tuple-element.65), channel_id=1, source_target_pairs={{0,1},{1,0},{2,3},{3,2},{4,5},{5,4},{6,7},{7,6},{8,9},{9,8},{10,11... | collective-permute-start | bytes 1572872 | tf_op jit(solution)/shard_map/ppermute | solution.py:595
  82.3 1.3 collective-permute-start.8
  83.6 4.0 %collective-permute-start.9 = (f32[64,128]{1,0:T(8,128)S(1)}, f32[64,128]{1,0:T(8,128)S(1)}, u32[]{:S(2)}, u32[]{:S(2)}) collective-permute-start(f32[64,128]{1,0:T(8,128)S(1)} %get-tuple-element.79), channel_id=1, source_target_pairs={{0,8},{8,16},{16,24},{24,32},{32,40},{40,48},{48,56},{56,64},{64,7... | collective-permute-start | bytes 98312 | tf_op jit(solution)/shard_map/ppermute | solution.py:23
  87.6 1.9 %fourth.1 = (f32[1152,128]{1,0:T(8,128)S(1)}, f32[1,512,128]{2,1,0:T(8,128)S(1)}, f32[1,512,128]{2,1,0:T(8,128)S(1)}) custom-call(s32[3]{0:T(128)S(1)} %pad_add_fusion.scal, f32[4608,128]{1,0:T(8,128)S(1)} %get-tuple-element.68.cur_ref, f32[64,128]{1,0:T(8,128)S(1)} %collective-permute-done.5.pin_ref, f32[64,128]{1,0:T(8,128)S(1)} %collective-permute-done.6.bin_ref, ...), custom_call_target="tpu_custom_call" | custom-call | flops 2000000000 | bytes 4000000 | tf_op jit(solution)/shard_map/fourth/pallas_call | solution.py:337
  89.5 2.5 %collective-permute-start.7 = (f32[1,512,128]{2,1,0:T(8,128)S(1)}, f32[1,512,128]{2,1,0:T(8,128)S(1)}, u32[]{:S(2)}, u32[]{:S(2)}) collective-permute-start(f32[1,512,128]{2,1,0:T(8,128)S(1)} %get-tuple-element.73), channel_id=1, source_target_pairs={{0,1},{1,0},{2,3},{3,2},{4,5},{5,4},{6,7},{7,6},{8,9},{9,8},{10,11... | collective-permute-start | bytes 786440 | tf_op jit(solution)/shard_map/ppermute | solution.py:595
  92.6 1.9 %collective-permute-start.10 = (f32[1,512,128]{2,1,0:T(8,128)S(1)}, f32[1,512,128]{2,1,0:T(8,128)S(1)}, u32[]{:S(2)}, u32[]{:S(2)}) collective-permute-start(f32[1,512,128]{2,1,0:T(8,128)S(1)} %get-tuple-element.81), channel_id=1, source_target_pairs={{0,1},{1,0},{2,3},{3,2},{4,5},{5,4},{6,7},{7,6},{8,9},{9,8},{10,11... | collective-permute-start | bytes 786440 | tf_op jit(solution)/shard_map/ppermute | solution.py:595
  94.5 1.4 early.1
  96.0 2.1 %gram.1 = (f32[4,512,128]{2,1,0:T(8,128)S(1)}, f32[8,1,128]{2,1,0:T(1,128)S(1)}) custom-call(s32[3]{0:T(128)S(1)} %pad_add_fusion.scal, f32[6,512,128]{2,1,0:T(8,128)S(1)} %get-tuple-element.66.early_ref, f32[128,128]{1,0:T(8,128)S(1)} %get-tuple-element.67.part_ref, f32[1,512,128]{2,1,0:T(8,128)S(1)} %get-tuple-element.72.keep3, ...), custom_call_target="tpu_custom_call" | custom-call | flops 1000000000 | bytes 2000000 | tf_op jit(solution)/shard_map/gram/pallas_call | solution.py:337
  98.2 8.2 %all_to_all.15 = f32[8,1,128]{2,1,0:T(1,128)S(1)} all-to-all(f32[8,1,128]{2,1,0:T(1,128)S(1)} %get-tuple-element.82), channel_id=1, replica_groups=mesh['beam'=64,'trans'=8] {'trans'}, dimensions={0} | all-to-all | bytes 8192 | tf_op jit(solution)/shard_map/all_to_all | solution.py:623
  106.4 32.1 %all_to_all.16.gram_ref = f32[64,1,128]{2,1,0:T(1,128)S(1)} all-to-all(f32[64,1,128]{2,1,0:T(1,128)S(1)} %broadcast_in_dim.2), channel_id=1, replica_groups=mesh['beam'=64,'trans'=8] {'beam'}, dimensions={0} | all-to-all | bytes 65536 | tf_op jit(solution)/shard_map/all_to_all | solution.py:624
  138.5 4.9 %basis.1 = (f32[10,512,128]{2,1,0:T(8,128)}, f32[10,2,10]{2,1,0:T(2,128)}) custom-call(f32[64,1,128]{2,1,0:T(1,128)S(1)} %all_to_all.16.gram_ref, f32[6,512,128]{2,1,0:T(8,128)S(1)} %get-tuple-element.66.early_ref, f32[4,512,128]{2,1,0:T(8,128)S(1)} %get-tuple-element.83.late_ref), custom_call_target="tpu_custom_call" | custom-call | tf_op jit(solution)/shard_map/basis/pallas_call | solution.py:626
  (30 shorter events, 3.7 us)
Async XLA Ops:
  7.2 55.1 %all-gather.3.cloned.1.call-start = ((), (), s32[]{:S(2)}) async-start(), calls=%async_computation.3 | async-start | bytes 2359296 | tf_op jit(solution)/shard_map/all_gather | solution.py:539
  7.9 1.0 copy-start
  10.3 10.5 %copy-start.3 = (f32[65,65]{1,0:T(8,128)S(1)}, f32[65,65]{1,0:T(8,128)}, u32[]{:S(2)}) copy-start(f32[65,65]{1,0:T(8,128)} %ek_hbm.1) | copy-start | bytes 50704
  10.3 52.0 %all-to-all-start = ((f32[8,512,128]{2,1,0:T(8,128)}), f32[8,512,128]{2,1,0:T(8,128)S(1)}, u32[]{:S(2)}, u32[]{:S(2)}) async-start(f32[8,512,128]{2,1,0:T(8,128)} %copies.1), calls=%async_computation | async-start | bytes 4194304 | tf_op jit(solution)/shard_map/all_to_all | solution.py:549
  20.7 1.0 copy-start.1
  20.7 1.1 copy-start.2
  22.2 5.3 %collective-permute-start = (f32[16,128]{1,0:T(8,128)S(1)}, f32[16,128]{1,0:T(8,128)S(1)}, u32[]{:S(2)}, u32[]{:S(2)}) collective-permute-start(f32[16,128]{1,0:T(8,128)S(1)} %get-tuple-element.50), channel_id=1, source_target_pairs={{8,0},{16,8},{24,16},{32,24},{40,32},{48,40},{56,48},{64,56},{72,6... | collective-permute-start | bytes 24584 | tf_op jit(solution)/shard_map/ppermute | solution.py:23
  23.5 4.8 %collective-permute-start.1 = (f32[16,128]{1,0:T(8,128)S(1)}, f32[16,128]{1,0:T(8,128)S(1)}, u32[]{:S(2)}, u32[]{:S(2)}) collective-permute-start(f32[16,128]{1,0:T(8,128)S(1)} %get-tuple-element.51), channel_id=1, source_target_pairs={{0,8},{8,16},{16,24},{24,32},{32,40},{40,48},{48,56},{56,64},{64,7... | collective-permute-start | bytes 24584 | tf_op jit(solution)/shard_map/ppermute | solution.py:23
  28.3 5.8 %collective-permute-start.2 = (f32[16,128]{1,0:T(8,128)S(1)}, f32[16,128]{1,0:T(8,128)S(1)}, u32[]{:S(2)}, u32[]{:S(2)}) collective-permute-start(f32[16,128]{1,0:T(8,128)S(1)} %get-tuple-element.55), channel_id=1, source_target_pairs={{8,0},{16,8},{24,16},{32,24},{40,32},{48,40},{56,48},{64,56},{72,6... | collective-permute-start | bytes 24584 | tf_op jit(solution)/shard_map/ppermute | solution.py:23
  29.6 5.3 %collective-permute-start.3 = (f32[16,128]{1,0:T(8,128)S(1)}, f32[16,128]{1,0:T(8,128)S(1)}, u32[]{:S(2)}, u32[]{:S(2)}) collective-permute-start(f32[16,128]{1,0:T(8,128)S(1)} %get-tuple-element.56), channel_id=1, source_target_pairs={{0,8},{8,16},{16,24},{24,32},{32,40},{40,48},{48,56},{56,64},{64,7... | collective-permute-start | bytes 24584 | tf_op jit(solution)/shard_map/ppermute | solution.py:23
  70.6 11.6 %collective-permute-start.5 = (f32[64,128]{1,0:T(8,128)S(1)}, f32[64,128]{1,0:T(8,128)S(1)}, u32[]{:S(2)}, u32[]{:S(2)}) collective-permute-start(f32[64,128]{1,0:T(8,128)S(1)} %get-tuple-element.69), channel_id=1, source_target_pairs={{8,0},{16,8},{24,16},{32,24},{40,32},{48,40},{56,48},{64,56},{72,6... | collective-permute-start | bytes 98312 | tf_op jit(solution)/shard_map/ppermute | solution.py:23
  71.9 10.4 %collective-permute-start.6 = (f32[64,128]{1,0:T(8,128)S(1)}, f32[64,128]{1,0:T(8,128)S(1)}, u32[]{:S(2)}, u32[]{:S(2)}) collective-permute-start(f32[64,128]{1,0:T(8,128)S(1)} %get-tuple-element.70), channel_id=1, source_target_pairs={{0,8},{8,16},{16,24},{24,32},{32,40},{40,48},{48,56},{56,64},{64,7... | collective-permute-start | bytes 98312 | tf_op jit(solution)/shard_map/ppermute | solution.py:23
  79.6 15.0 %collective-permute-start.4 = (f32[2,512,128]{2,1,0:T(8,128)S(1)}, f32[2,512,128]{2,1,0:T(8,128)S(1)}, u32[]{:S(2)}, u32[]{:S(2)}) collective-permute-start(f32[2,512,128]{2,1,0:T(8,128)S(1)} %get-tuple-element.65), channel_id=1, source_target_pairs={{0,1},{1,0},{2,3},{3,2},{4,5},{5,4},{6,7},{7,6},{8,9},{9,8},{10,11... | collective-permute-start | bytes 1572872 | tf_op jit(solution)/shard_map/ppermute | solution.py:595
  82.3 9.7 %collective-permute-start.8 = (f32[64,128]{1,0:T(8,128)S(1)}, f32[64,128]{1,0:T(8,128)S(1)}, u32[]{:S(2)}, u32[]{:S(2)}) collective-permute-start(f32[64,128]{1,0:T(8,128)S(1)} %get-tuple-element.78), channel_id=1, source_target_pairs={{8,0},{16,8},{24,16},{32,24},{40,32},{48,40},{56,48},{64,56},{72,6... | collective-permute-start | bytes 98312 | tf_op jit(solution)/shard_map/ppermute | solution.py:23
  83.6 8.4 %collective-permute-start.9 = (f32[64,128]{1,0:T(8,128)S(1)}, f32[64,128]{1,0:T(8,128)S(1)}, u32[]{:S(2)}, u32[]{:S(2)}) collective-permute-start(f32[64,128]{1,0:T(8,128)S(1)} %get-tuple-element.79), channel_id=1, source_target_pairs={{0,8},{8,16},{16,24},{24,32},{32,40},{40,48},{48,56},{56,64},{64,7... | collective-permute-start | bytes 98312 | tf_op jit(solution)/shard_map/ppermute | solution.py:23
  89.5 6.5 %collective-permute-start.7 = (f32[1,512,128]{2,1,0:T(8,128)S(1)}, f32[1,512,128]{2,1,0:T(8,128)S(1)}, u32[]{:S(2)}, u32[]{:S(2)}) collective-permute-start(f32[1,512,128]{2,1,0:T(8,128)S(1)} %get-tuple-element.73), channel_id=1, source_target_pairs={{0,1},{1,0},{2,3},{3,2},{4,5},{5,4},{6,7},{7,6},{8,9},{9,8},{10,11... | collective-permute-start | bytes 786440 | tf_op jit(solution)/shard_map/ppermute | solution.py:595
  92.6 3.4 %collective-permute-start.10 = (f32[1,512,128]{2,1,0:T(8,128)S(1)}, f32[1,512,128]{2,1,0:T(8,128)S(1)}, u32[]{:S(2)}, u32[]{:S(2)}) collective-permute-start(f32[1,512,128]{2,1,0:T(8,128)S(1)} %get-tuple-element.81), channel_id=1, source_target_pairs={{0,1},{1,0},{2,3},{3,2},{4,5},{5,4},{6,7},{7,6},{8,9},{9,8},{10,11... | collective-permute-start | bytes 786440 | tf_op jit(solution)/shard_map/ppermute | solution.py:595
Sparse Core Ops, SparseCore 0:
  10.1 47.1 all-gather.2

commit v6 on v3

--- a/solution.py
+++ b/solution.py
@@ -377,7 +377,7 @@
         [(a, b) for a in first for b in second[:3]],
         [(a, b) for a in first for b in second[3:]],
     ]
-    unroll = 16
+    unroll = 32
     for pairs in groups:
         used = sorted({c for pair in pairs for c in pair})
         turned = sorted({b for a, b in pairs if a != b})
@@ -443,9 +443,9 @@
         below = r > j
         re = re - jnp.where(below, col_re * row_re - col_im * row_im, 0.0)
         im = im - jnp.where(below, col_re * row_im + col_im * row_re, 0.0)
-    keep = (c >= r) & (c < ncol)
-    factor_ref[0] = jnp.where(keep, up_re, 0.0)
-    factor_ref[1] = jnp.where(keep & (c > r), up_im, 0.0)
+    for q, up in ((0, jnp.where(c >= r, up_re, 0.0)), (1, jnp.where(c > r, up_im, 0.0))):
+        for k in range(ncol):
+            factor_ref[k, q : q + 1, :] = up[k : k + 1, :ncol]
     sign = jnp.where(lax.broadcasted_iota(jnp.int32, (8, width), 1) < half, 1.0, -1.0)
     for k in range(ncol):
         for i in range(k + 1):
@@ -455,10 +455,10 @@
             )
     group = 4
     each = size // rows
-    copies = []
-    for r in range(rows):
-        for start in range(r * each, (r + 1) * each, 8 * group):
-            slots = [slice(start + 8 * g, start + 8 * g + 8) for g in range(group)]
+
+    def row(r, carry):
+        for start in range(0, each, 8 * group):
+            slots = [pl.ds(pl.multiple_of(r * each + start + 8 * g, 8), 8) for g in range(group)]
             v = [[cols_ref[i, s, :] for s in slots] for i in range(ncol)]
             t = [[pltpu.roll(x, half, 1) for x in xs] for xs in v]
             for k in range(ncol):
@@ -473,12 +473,16 @@
                         total[g] = term if total[g] is None else total[g] + term
                 for g in range(group):
                     out_ref[k, slots[g], :] = total[g]
-        part = pl.ds(r * each, each)
-        copy = pltpu.make_async_copy(out_ref.at[:, part, :], basis_ref.at[:, part, :], sems.at[r])
-        copy.start()
-        copies.append(copy)
-    for copy in copies:
-        copy.wait()
+        copy(r).start()
+        return carry
+
+    def copy(r):
+        part = pl.ds(pl.multiple_of(r * each, 8), each)
+        return pltpu.make_async_copy(out_ref.at[:, part, :], basis_ref.at[:, part, :], sems.at[r])
+
+    lax.fori_loop(0, rows, row, 0)
+    for r in range(rows):
+        copy(r).wait()
 
 
 def shards(packets, kinetic_x, kinetic_y, element_kinetic, potential):
@@ -585,7 +589,7 @@
         functools.partial(basis_body, cells, rows),
         out_shape=[
             jax.ShapeDtypeStruct((ncol, size, width), F32),
-            jax.ShapeDtypeStruct((2, 16, width), F32),
+            jax.ShapeDtypeStruct((ncol, 2, ncol), F32),
         ],
         in_specs=[vm(), vm()],
         out_specs=[pl.BlockSpec(memory_space=pl.ANY), vm()],
@@ -597,7 +601,7 @@
         compiler_params=pltpu.CompilerParams(vmem_limit_bytes=LIMIT),
         name="basis",
     )(gram, cols)
-    return basis.reshape(ncol, rows, nz, width), factor[:, :ncol, :ncol]
+    return basis.reshape(ncol, rows, nz, width), factor.transpose(1, 0, 2)
 
 
 def solution(mesh):

time: 151 us -> 149 us (0.987)
  no operation moved by 1% of the time
where the time goes in v6:
time: 149 us
  blocking collectives  68.9 us (46%)
  starting transfers between devices  35.3 us (24%)
  Pallas kernels  24.1 us (16%)
  between operations  14.2 us (10%)
  waiting for transfers between devices  4.5 us (3%)
    all_to_all x1, blocking collectives, shards(): lax.all_to_all(jnp.broadcast_to(gram, (beam, 1, width)), 'beam', 0, 0, ti...  33.5 us
    all_gather x1, blocking collectives, shards(): planes = lax.all_gather(planes, 'trans')  27.4 us
    ppermute x8, starting transfers between devices, passed(): lax.ppermute(x, 'beam', [(i, i + by) for i in range(peers) if 0 <= i + by...  21.7 us
    pallas_call x7, Pallas kernels, call(): pl.pallas_call(body, out_shape=outs, in_specs=specs, out_specs=[vm()] * l...  14.5 us
    all_to_all x1, starting transfers between devices, shards(): lax.all_to_all(sent, 'trans', 0, 0, tiled=True).reshape(nx * nz, width)  10.4 us
    all_to_all x1, blocking collectives, shards(): lax.all_to_all(gram, 'trans', 0, 0, tiled=True)  8.08 us
    pallas_call x1, Pallas kernels, shards(): pl.pallas_call(functools.partial(basis_body, cells, rows), out_shape=[jax...  4.9 us
    ppermute x1, starting transfers between devices, shards(): recv = lax.ppermute(send, 'trans', [(i, i ^ 1) for i in range(trans)])  3.2 us
  transfers between devices with their start and end apart: 11, of which 3 were waited for; matrix products, arithmetic and copies ran while one was open for 0% of the time, Pallas kernels for 5%

profile of v6, /device:TPU:1, one launch (start us, length us, event | category | flops | bytes accessed | tf_op | source)
XLA Modules:
  0.0 148.6 jit_solution(11047688777782266497)
XLA Ops:
  7.9 1.0 copy-done
  8.9 1.3 copies.1
  10.3 10.4 %all-to-all-start = ((f32[8,512,128]{2,1,0:T(8,128)}), f32[8,512,128]{2,1,0:T(8,128)S(1)}, u32[]{:S(2)}, u32[]{:S(2)}) async-start(f32[8,512,128]{2,1,0:T(8,128)} %copies.1), calls=%async_computation | async-start | bytes 4194304 | tf_op jit(solution)/shard_map/all_to_all | solution.py:511
  20.8 0.7 vectors.1
  22.2 1.3 collective-permute-start
  23.5 4.0 %collective-permute-start.1 = (f32[16,128]{1,0:T(8,128)S(1)}, f32[16,128]{1,0:T(8,128)S(1)}, u32[]{:S(2)}, u32[]{:S(2)}) collective-permute-start(f32[16,128]{1,0:T(8,128)S(1)} %get-tuple-element.48), channel_id=1, source_target_pairs={{0,8},{8,16},{16,24},{24,32},{32,40},{40,48},{48,56},{56,64},{64,7... | collective-permute-start | bytes 24584 | tf_op jit(solution)/shard_map/ppermute | solution.py:23
  27.5 0.8 collective-permute-done.1.bin_ref
  28.3 1.3 collective-permute-start.2
  29.6 4.5 %collective-permute-start.3 = (f32[16,128]{1,0:T(8,128)S(1)}, f32[16,128]{1,0:T(8,128)S(1)}, u32[]{:S(2)}, u32[]{:S(2)}) collective-permute-start(f32[16,128]{1,0:T(8,128)S(1)} %get-tuple-element.53), channel_id=1, source_target_pairs={{0,8},{8,16},{16,24},{24,32},{32,40},{40,48},{48,56},{56,64},{64,7... | collective-permute-start | bytes 24584 | tf_op jit(solution)/shard_map/ppermute | solution.py:23
  34.2 0.8 collective-permute-done.3
  34.9 27.4 %all-gather = f32[32,16,128]{2,1,0:T(8,128)S(1)} all-gather(f32[4,16,128]{2,1,0:T(8,128)S(1)} %pad_maximum_fusion), channel_id=2, replica_groups=mesh['beam'=64,'trans'=8] {'trans'}, dimensions={0}, use_global_device_ids=true | all-gather | bytes 294912 | tf_op jit(solution)/shard_map/all_gather | solution.py:536
  62.3 8.3 %pair.1 = (f32[4608,128]{1,0:T(8,128)S(1)}, f32[4608,128]{1,0:T(8,128)S(1)}, f32[64,128]{1,0:T(8,128)S(1)}, f32[64,128]{1,0:T(8,128)S(1)}, f32[1024,128]{1,0:T(8...) custom-call(s32[3]{0:T(128)S(1)} %pad_add_fusion.scal, ...), custom_call_target="tpu_custom_call" | custom-call | flops 8000000000 | bytes 16000000 | tf_op jit(solution)/shard_map/pair/pallas_call | solution.py:331
  70.6 1.3 collective-permute-start.4
  71.9 4.0 %collective-permute-start.5 = (f32[64,128]{1,0:T(8,128)S(1)}, f32[64,128]{1,0:T(8,128)S(1)}, u32[]{:S(2)}, u32[]{:S(2)}) collective-permute-start(f32[64,128]{1,0:T(8,128)S(1)} %get-tuple-element.63), channel_id=1, source_target_pairs={{0,8},{8,16},{16,24},{24,32},{32,40},{40,48},{48,56},{56,64},{64,7... | collective-permute-start | bytes 98312 | tf_op jit(solution)/shard_map/ppermute | solution.py:23
  75.9 3.1 %third.1 = (f32[4608,128]{1,0:T(8,128)S(1)}, f32[64,128]{1,0:T(8,128)S(1)}, f32[64,128]{1,0:T(8,128)S(1)}) custom-call(f32[4608,128]{1,0:T(8,128)S(1)} %get-tuple-element.54.cur_ref.prev_ref, f32[4608,128]{1,0:T(8,128)S(1)} %get-tuple-element.55.prev_ref, f32[4096,128]{1,0:T(8,128)S(1)} %get-tuple-element.56.pot_ref, ...), custom_call_target="tpu_custom_call" | custom-call | flops 4000000000 | bytes 8000000 | tf_op jit(solution)/shard_map/third/pallas_call | solution.py:331
  79.0 1.3 collective-permute-start.6
  80.3 4.0 %collective-permute-start.7 = (f32[64,128]{1,0:T(8,128)S(1)}, f32[64,128]{1,0:T(8,128)S(1)}, u32[]{:S(2)}, u32[]{:S(2)}) collective-permute-start(f32[64,128]{1,0:T(8,128)S(1)} %get-tuple-element.70), channel_id=1, source_target_pairs={{0,8},{8,16},{16,24},{24,32},{32,40},{40,48},{48,56},{56,64},{64,7... | collective-permute-start | bytes 98312 | tf_op jit(solution)/shard_map/ppermute | solution.py:23
  84.3 2.0 %fourth.1 = (f32[1152,128]{1,0:T(8,128)S(1)}, f32[1024,128]{1,0:T(8,128)S(1)}) custom-call(s32[3]{0:T(128)S(1)} %pad_add_fusion.scal, f32[4608,128]{1,0:T(8,128)S(1)} %get-tuple-element.61.cur_ref, f32[64,128]{1,0:T(8,128)S(1)} %collective-permute-done.4.pin_ref, f32[64,128]{1,0:T(8,128)S(1)} %collective-permute-done.5.bin_ref, ...), custom_call_target="tpu_custom_call" | custom-call | flops 2000000000 | bytes 4000000 | tf_op jit(solution)/shard_map/fourth/pallas_call | solution.py:331
  87.0 3.2 %collective-permute-start.8 = (f32[4,512,128]{2,1,0:T(8,128)S(1)}, f32[4,512,128]{2,1,0:T(8,128)S(1)}, u32[]{:S(2)}, u32[]{:S(2)}) collective-permute-start(f32[4,512,128]{2,1,0:T(8,128)S(1)} %get-tuple-element.75), channel_id=1, source_target_pairs={{0,1},{1,0},{2,3},{3,2},{4,5},{5,4},{6,7},{7,6},{8,9},{9,8},{10,11... | collective-permute-start | bytes 3145736 | tf_op jit(solution)/shard_map/ppermute | solution.py:574
  90.2 2.3 %collective-permute-done.8.recv_ref = f32[4,512,128]{2,1,0:T(8,128)S(1)} collective-permute-done((f32[4,512,128]{2,1,0:T(8,128)S(1)}, f32[4,512,128]{2,1,0:T(8,128)S(1)}, u32[]{:S(2)}, u32[]{:S(2)}) %collective-permute-start.8) | collective-permute-done | bytes 1048608 | tf_op jit(solution)/shard_map/ppermute | solution.py:574
  92.5 2.7 %gram.1 = (f32[10,512,128]{2,1,0:T(8,128)S(1)}, f32[8,1,128]{2,1,0:T(1,128)S(1)}) custom-call(s32[3]{0:T(128)S(1)} %pad_add_fusion.scal, f32[2,512,128]{2,1,0:T(8,128)S(1)} %bitcast.16, f32[4,512,128]{2,1,0:T(8,128)S(1)} %get-tuple-element.74.keep_ref, f32[4,512,128]{2,1,0:T(8,128)S(1)} %collective-permute-done.8.recv_ref), custom_call_target="tpu_custom_call" | custom-call | tf_op jit(solution)/shard_map/gram/pallas_call | solution.py:575
  95.2 8.1 %all_to_all.15 = f32[8,1,128]{2,1,0:T(1,128)S(1)} all-to-all(f32[8,1,128]{2,1,0:T(1,128)S(1)} %get-tuple-element.76), channel_id=1, replica_groups=mesh['beam'=64,'trans'=8] {'trans'}, dimensions={0} | all-to-all | bytes 8192 | tf_op jit(solution)/shard_map/all_to_all | solution.py:585
  103.4 33.5 %all_to_all.16.gram_ref = f32[64,1,128]{2,1,0:T(1,128)S(1)} all-to-all(f32[64,1,128]{2,1,0:T(1,128)S(1)} %broadcast_in_dim.2), channel_id=1, replica_groups=mesh['beam'=64,'trans'=8] {'beam'}, dimensions={0} | all-to-all | bytes 65536 | tf_op jit(solution)/shard_map/all_to_all | solution.py:586
  136.8 4.9 %basis.1 = (f32[10,512,128]{2,1,0:T(8,128)}, f32[10,2,10]{2,1,0:T(2,128)}) custom-call(f32[64,1,128]{2,1,0:T(1,128)S(1)} %all_to_all.16.gram_ref, f32[10,512,128]{2,1,0:T(8,128)S(1)} %get-tuple-element.77.cols_ref), custom_call_target="tpu_custom_call" | custom-call | tf_op jit(solution)/shard_map/basis/pallas_call | solution.py:588
  (25 shorter events, 2.3 us)
Async XLA Ops:
  7.2 55.1 %all-gather.3.cloned.1.call-start = ((), (), s32[]{:S(2)}) async-start(), calls=%async_computation.3 | async-start | bytes 2359296 | tf_op jit(solution)/shard_map/all_gather | solution.py:501
  7.9 1.0 copy-start
  10.3 10.5 %copy-start.3 = (f32[65,65]{1,0:T(8,128)S(1)}, f32[65,65]{1,0:T(8,128)}, u32[]{:S(2)}) copy-start(f32[65,65]{1,0:T(8,128)} %ek_hbm.1) | copy-start | bytes 50704
  10.3 52.0 %all-to-all-start = ((f32[8,512,128]{2,1,0:T(8,128)}), f32[8,512,128]{2,1,0:T(8,128)S(1)}, u32[]{:S(2)}, u32[]{:S(2)}) async-start(f32[8,512,128]{2,1,0:T(8,128)} %copies.1), calls=%async_computation | async-start | bytes 4194304 | tf_op jit(solution)/shard_map/all_to_all | solution.py:511
  20.7 1.0 copy-start.1
  20.7 1.1 copy-start.2
  22.2 5.3 %collective-permute-start = (f32[16,128]{1,0:T(8,128)S(1)}, f32[16,128]{1,0:T(8,128)S(1)}, u32[]{:S(2)}, u32[]{:S(2)}) collective-permute-start(f32[16,128]{1,0:T(8,128)S(1)} %get-tuple-element.47), channel_id=1, source_target_pairs={{8,0},{16,8},{24,16},{32,24},{40,32},{48,40},{56,48},{64,56},{72,6... | collective-permute-start | bytes 24584 | tf_op jit(solution)/shard_map/ppermute | solution.py:23
  23.5 4.8 %collective-permute-start.1 = (f32[16,128]{1,0:T(8,128)S(1)}, f32[16,128]{1,0:T(8,128)S(1)}, u32[]{:S(2)}, u32[]{:S(2)}) collective-permute-start(f32[16,128]{1,0:T(8,128)S(1)} %get-tuple-element.48), channel_id=1, source_target_pairs={{0,8},{8,16},{16,24},{24,32},{32,40},{40,48},{48,56},{56,64},{64,7... | collective-permute-start | bytes 24584 | tf_op jit(solution)/shard_map/ppermute | solution.py:23
  28.3 5.8 %collective-permute-start.2 = (f32[16,128]{1,0:T(8,128)S(1)}, f32[16,128]{1,0:T(8,128)S(1)}, u32[]{:S(2)}, u32[]{:S(2)}) collective-permute-start(f32[16,128]{1,0:T(8,128)S(1)} %get-tuple-element.52), channel_id=1, source_target_pairs={{8,0},{16,8},{24,16},{32,24},{40,32},{48,40},{56,48},{64,56},{72,6... | collective-permute-start | bytes 24584 | tf_op jit(solution)/shard_map/ppermute | solution.py:23
  29.6 5.3 %collective-permute-start.3 = (f32[16,128]{1,0:T(8,128)S(1)}, f32[16,128]{1,0:T(8,128)S(1)}, u32[]{:S(2)}, u32[]{:S(2)}) collective-permute-start(f32[16,128]{1,0:T(8,128)S(1)} %get-tuple-element.53), channel_id=1, source_target_pairs={{0,8},{8,16},{16,24},{24,32},{32,40},{40,48},{48,56},{56,64},{64,7... | collective-permute-start | bytes 24584 | tf_op jit(solution)/shard_map/ppermute | solution.py:23
  70.6 8.4 %collective-permute-start.4 = (f32[64,128]{1,0:T(8,128)S(1)}, f32[64,128]{1,0:T(8,128)S(1)}, u32[]{:S(2)}, u32[]{:S(2)}) collective-permute-start(f32[64,128]{1,0:T(8,128)S(1)} %get-tuple-element.62), channel_id=1, source_target_pairs={{8,0},{16,8},{24,16},{32,24},{40,32},{48,40},{56,48},{64,56},{72,6... | collective-permute-start | bytes 98312 | tf_op jit(solution)/shard_map/ppermute | solution.py:23
  71.9 7.1 %collective-permute-start.5 = (f32[64,128]{1,0:T(8,128)S(1)}, f32[64,128]{1,0:T(8,128)S(1)}, u32[]{:S(2)}, u32[]{:S(2)}) collective-permute-start(f32[64,128]{1,0:T(8,128)S(1)} %get-tuple-element.63), channel_id=1, source_target_pairs={{0,8},{8,16},{16,24},{24,32},{32,40},{40,48},{48,56},{56,64},{64,7... | collective-permute-start | bytes 98312 | tf_op jit(solution)/shard_map/ppermute | solution.py:23
  79.0 7.3 %collective-permute-start.6 = (f32[64,128]{1,0:T(8,128)S(1)}, f32[64,128]{1,0:T(8,128)S(1)}, u32[]{:S(2)}, u32[]{:S(2)}) collective-permute-start(f32[64,128]{1,0:T(8,128)S(1)} %get-tuple-element.69), channel_id=1, source_target_pairs={{8,0},{16,8},{24,16},{32,24},{40,32},{48,40},{56,48},{64,56},{72,6... | collective-permute-start | bytes 98312 | tf_op jit(solution)/shard_map/ppermute | solution.py:23
  80.3 6.0 %collective-permute-start.7 = (f32[64,128]{1,0:T(8,128)S(1)}, f32[64,128]{1,0:T(8,128)S(1)}, u32[]{:S(2)}, u32[]{:S(2)}) collective-permute-start(f32[64,128]{1,0:T(8,128)S(1)} %get-tuple-element.70), channel_id=1, source_target_pairs={{0,8},{8,16},{16,24},{24,32},{32,40},{40,48},{48,56},{56,64},{64,7... | collective-permute-start | bytes 98312 | tf_op jit(solution)/shard_map/ppermute | solution.py:23
  87.0 5.5 %collective-permute-start.8 = (f32[4,512,128]{2,1,0:T(8,128)S(1)}, f32[4,512,128]{2,1,0:T(8,128)S(1)}, u32[]{:S(2)}, u32[]{:S(2)}) collective-permute-start(f32[4,512,128]{2,1,0:T(8,128)S(1)} %get-tuple-element.75), channel_id=1, source_target_pairs={{0,1},{1,0},{2,3},{3,2},{4,5},{5,4},{6,7},{7,6},{8,9},{9,8},{10,11... | collective-permute-start | bytes 3145736 | tf_op jit(solution)/shard_map/ppermute | solution.py:574
Sparse Core Ops, SparseCore 0:
  10.1 47.1 all-gather.2

commit v7 on v6

--- a/solution.py
+++ b/solution.py
@@ -358,58 +358,78 @@
             ref[POWERS - 1, r * nz : (r + 1) * nz, :] = u
 
 
-def gram_body(scal, packets_ref, keep_ref, recv_ref, cols_ref, gram_ref, acc_ref):
+def product_sums(load, chunks, pairs, unroll, sums):
+    used = sorted({c for pair in pairs for c in pair})
+    turned = sorted({b for a, b in pairs if a != b})
+
+    def chunk(i, sums):
+        sums = list(sums)
+        for q in range(unroll):
+            v = {c: load(c, (i * unroll + q) * 8) for c in used}
+            t = {c: pltpu.roll(v[c], v[c].shape[-1] // 2, 1) for c in turned}
+            n = 0
+            for a, b in pairs:
+                sums[n] = sums[n] + v[a] * v[b]
+                n += 1
+                if a != b:
+                    sums[n] = sums[n] + v[a] * t[b]
+                    n += 1
+        return tuple(sums)
+
+    if sums is None:
+        count = sum(1 if a == b else 2 for a, b in pairs)
+        width = load(used[0], 0).shape[-1]
+        sums = tuple(jnp.zeros((8, width), F32) for _ in range(count))
+    return lax.fori_loop(0, chunks // unroll, chunk, sums)
+
+
+def store_sums(acc_ref, pairs, sums, base):
+    ncol = 2 * (POWERS + 1)
+    width = acc_ref.shape[1]
+    sign = jnp.where(lax.broadcasted_iota(jnp.int32, (8, width), 1) < width // 2, 1.0, -1.0)
+    n = 0
+    for a, b in pairs:
+        acc_ref[pl.ds(base + a * ncol + b, 1), :] = jnp.sum(sums[n], axis=0, keepdims=True)
+        n += 1
+        if a != b:
+            acc_ref[pl.ds(base + b * ncol + a, 1), :] = jnp.sum(sums[n] * sign, axis=0, keepdims=True)
+            n += 1
+
+
+def inside_body(nz, scal, first_ref, keep_ref, send_ref, acc_ref):
+    npow = keep_ref.shape[0] + 1
+    size = keep_ref.shape[1]
+    pairs = [(a, b) for a in range(npow) for b in range(npow) if a <= b]
+    sums = None
+    for ref, where in ((keep_ref, scal[1]), (send_ref, 1 - scal[1])):
+
+        def load(c, at, ref=ref, where=where):
+            if c == 0:
+                return first_ref[pl.ds(pl.multiple_of(scal[0] * nz + where * size + at, 8), 8), :]
+            return ref[c - 1, pl.ds(pl.multiple_of(at, 8), 8), :]
+
+        sums = product_sums(load, size // 8, pairs, 32, sums)
+    acc_ref[...] = jnp.zeros_like(acc_ref)
+    store_sums(acc_ref, pairs, sums, scal[1] * (npow * (2 * npow + 1)))
+
+
+def gram_body(scal, packets_ref, keep_ref, recv_ref, part_ref, cols_ref, gram_ref, acc_ref):
     core = scal[1]
     ncol, size, width = cols_ref.shape
     npow = ncol // 2
-    half = width // 2
     cols_ref[0] = packets_ref[0]
     cols_ref[npow] = packets_ref[1]
     for k in range(npow - 1):
         cols_ref[core * npow + 1 + k] = keep_ref[k]
         cols_ref[(1 - core) * npow + 1 + k] = recv_ref[k]
-    acc_ref[...] = jnp.zeros_like(acc_ref)
-    sign = jnp.where(lax.broadcasted_iota(jnp.int32, (8, width), 1) < half, 1.0, -1.0)
+    acc_ref[...] = part_ref[...]
     first, second = list(range(npow)), list(range(npow, ncol))
-    groups = [
-        [(a, b) for a in first for b in first if a <= b],
-        [(a, b) for a in second for b in second if a <= b],
-        [(a, b) for a in first for b in second[:3]],
-        [(a, b) for a in first for b in second[3:]],
-    ]
-    unroll = 32
-    for pairs in groups:
-        used = sorted({c for pair in pairs for c in pair})
-        turned = sorted({b for a, b in pairs if a != b})
-
-        def chunk(i, sums, pairs=pairs, used=used, turned=turned):
-            sums = list(sums)
-            for q in range(unroll):
-                at = pl.ds(pl.multiple_of((i * unroll + q) * 8, 8), 8)
-                v = {c: cols_ref[c, at, :] for c in used}
-                t = {c: pltpu.roll(v[c], half, 1) for c in turned}
-                n = 0
-                for a, b in pairs:
-                    sums[n] = sums[n] + v[a] * v[b]
-                    n += 1
-                    if a != b:
-                        sums[n] = sums[n] + v[a] * t[b]
-                        n += 1
-            return tuple(sums)
-
-        count = sum(1 if a == b else 2 for a, b in pairs)
-        sums = lax.fori_loop(
-            0, size // (8 * unroll), chunk, tuple(jnp.zeros((8, width), F32) for _ in range(count))
+    for some in (second[:3], second[3:]):
+        pairs = [(a, b) for a in first for b in some]
+        sums = product_sums(
+            lambda c, at: cols_ref[c, pl.ds(pl.multiple_of(at, 8), 8), :], size // 8, pairs, 32, None
         )
-        n = 0
-        for a, b in pairs:
-            acc_ref[a * ncol + b : a * ncol + b + 1, :] = jnp.sum(sums[n], axis=0, keepdims=True)
-            n += 1
-            if a != b:
-                acc_ref[b * ncol + a : b * ncol + a + 1, :] = jnp.sum(
-                    sums[n] * sign, axis=0, keepdims=True
-                )
-                n += 1
+        store_sums(acc_ref, pairs, sums, 0)
     row = jnp.sum(acc_ref[...].T, axis=0, keepdims=True)
     gram_ref[...] = jnp.broadcast_to(row[None], gram_ref.shape)
 
@@ -572,15 +592,14 @@
         name="finish",
     )(scal, local, plast, blast, rcol, *columns)
     recv = lax.ppermute(send, "trans", [(i, i ^ 1) for i in range(trans)])
-    cols, gram = pl.pallas_call(
-        gram_body,
-        out_shape=[in_vmem(ncol, size, width), in_vmem(trans, 1, width)],
-        in_specs=[pl.BlockSpec(memory_space=pltpu.SMEM)] + [vm()] * 3,
-        out_specs=[vm()] * 2,
-        scratch_shapes=[pltpu.VMEM((128, width), F32)],
-        compiler_params=pltpu.CompilerParams(vmem_limit_bytes=LIMIT),
-        name="gram",
-    )(scal, packets.reshape(npack, size, width), keep, recv)
+    (part,) = call(
+        "inside", functools.partial(inside_body, nz), [in_vmem(128, width)], cur, keep, send,
+        scal=scal, cost=1,
+    )
+    cols, gram = call(
+        "gram", gram_body, [in_vmem(ncol, size, width), in_vmem(trans, 1, width)],
+        flat, keep, recv, part, scal=scal, scratch=[in_vmem(128, width)], cost=1,
+    )
     beam = lax.axis_size("beam")
     gram = jnp.sum(lax.all_to_all(gram, "trans", 0, 0, tiled=True), axis=0, keepdims=True)
     gram = lax.all_to_all(jnp.broadcast_to(gram, (beam, 1, width)), "beam", 0, 0, tiled=True)

time: 149 us -> 148 us (level)
  waiting for transfers between devices: 4.5 us -> 2.99 us
    pallas_call x7 -> x9, Pallas kernels: 14.5 us -> 17.8 us  [call(): pl.pallas_call(body, out_shape=outs, in_specs=specs, out_specs=[vm()] * l...]
    pallas_call x1 -> x0, Pallas kernels: 2.71 us -> none  [shards(): pl.pallas_call(gram_body, out_shape=[in_vmem(ncol, size, width), in_vmem(...]
    ppermute x1, waiting for transfers between devices: 2.26 us -> 0.76 us  [shards(): recv = lax.ppermute(send, 'trans', [(i, i ^ 1) for i in range(trans)])]
  transfers between devices with their start and end apart: 11 -> 11, of which waited for: 3 -> 3; matrix products, arithmetic and copies ran while one was open for 0% -> 0% of each run, Pallas kernels for 5% -> 6%
where the time goes in v7:
time: 148 us
  blocking collectives  68.9 us (47%)
  starting transfers between devices  35.3 us (24%)
  Pallas kernels  24.7 us (17%)
  between operations  14.2 us (10%)
  waiting for transfers between devices  2.99 us (2%)
    all_to_all x1, blocking collectives, shards(): lax.all_to_all(jnp.broadcast_to(gram, (beam, 1, width)), 'beam', 0, 0, ti...  33.5 us
    all_gather x1, blocking collectives, shards(): planes = lax.all_gather(planes, 'trans')  27.4 us
    ppermute x8, starting transfers between devices, passed(): lax.ppermute(x, 'beam', [(i, i + by) for i in range(peers) if 0 <= i + by...  21.7 us
    pallas_call x9, Pallas kernels, call(): pl.pallas_call(body, out_shape=outs, in_specs=specs, out_specs=[vm()] * l...  17.8 us
    all_to_all x1, starting transfers between devices, shards(): lax.all_to_all(sent, 'trans', 0, 0, tiled=True).reshape(nx * nz, width)  10.4 us
    all_to_all x1, blocking collectives, shards(): lax.all_to_all(gram, 'trans', 0, 0, tiled=True)  8.08 us
    pallas_call x1, Pallas kernels, shards(): pl.pallas_call(functools.partial(basis_body, cells, rows), out_shape=[jax...  4.9 us
    ppermute x1, starting transfers between devices, shards(): recv = lax.ppermute(send, 'trans', [(i, i ^ 1) for i in range(trans)])  3.2 us
  transfers between devices with their start and end apart: 11, of which 3 were waited for; matrix products, arithmetic and copies ran while one was open for 0% of the time, Pallas kernels for 6%

profile of v7, /device:TPU:1, one launch (start us, length us, event | category | flops | bytes accessed | tf_op | source)
XLA Modules:
  0.0 147.7 jit_solution(14679903921908432154)
XLA Ops:
  7.9 1.0 copy-done
  8.9 1.3 copies.1
  10.3 10.4 %all-to-all-start = ((f32[8,512,128]{2,1,0:T(8,128)}), f32[8,512,128]{2,1,0:T(8,128)S(1)}, u32[]{:S(2)}, u32[]{:S(2)}) async-start(f32[8,512,128]{2,1,0:T(8,128)} %copies.1), calls=%async_computation | async-start | bytes 4194304 | tf_op jit(solution)/shard_map/all_to_all | solution.py:531
  22.2 1.3 collective-permute-start
  23.5 4.0 %collective-permute-start.1 = (f32[16,128]{1,0:T(8,128)S(1)}, f32[16,128]{1,0:T(8,128)S(1)}, u32[]{:S(2)}, u32[]{:S(2)}) collective-permute-start(f32[16,128]{1,0:T(8,128)S(1)} %get-tuple-element.48), channel_id=1, source_target_pairs={{0,8},{8,16},{16,24},{24,32},{32,40},{40,48},{48,56},{56,64},{64,7... | collective-permute-start | bytes 24584 | tf_op jit(solution)/shard_map/ppermute | solution.py:23
  27.5 0.8 collective-permute-done.1.bin_ref
  28.3 1.3 collective-permute-start.2
  29.6 4.5 %collective-permute-start.3 = (f32[16,128]{1,0:T(8,128)S(1)}, f32[16,128]{1,0:T(8,128)S(1)}, u32[]{:S(2)}, u32[]{:S(2)}) collective-permute-start(f32[16,128]{1,0:T(8,128)S(1)} %get-tuple-element.53), channel_id=1, source_target_pairs={{0,8},{8,16},{16,24},{24,32},{32,40},{40,48},{48,56},{56,64},{64,7... | collective-permute-start | bytes 24584 | tf_op jit(solution)/shard_map/ppermute | solution.py:23
  34.2 0.8 collective-permute-done.3
  34.9 27.4 %all-gather = f32[32,16,128]{2,1,0:T(8,128)S(1)} all-gather(f32[4,16,128]{2,1,0:T(8,128)S(1)} %pad_maximum_fusion), channel_id=2, replica_groups=mesh['beam'=64,'trans'=8] {'trans'}, dimensions={0}, use_global_device_ids=true | all-gather | bytes 294912 | tf_op jit(solution)/shard_map/all_gather | solution.py:556
  62.3 8.3 %pair.1 = (f32[4608,128]{1,0:T(8,128)S(1)}, f32[4608,128]{1,0:T(8,128)S(1)}, f32[64,128]{1,0:T(8,128)S(1)}, f32[64,128]{1,0:T(8,128)S(1)}, f32[1024,128]{1,0:T(8...) custom-call(s32[3]{0:T(128)S(1)} %pad_add_fusion.scal, ...), custom_call_target="tpu_custom_call" | custom-call | flops 8000000000 | bytes 16000000 | tf_op jit(solution)/shard_map/pair/pallas_call | solution.py:331
  70.6 1.3 collective-permute-start.4
  71.9 4.0 %collective-permute-start.5 = (f32[64,128]{1,0:T(8,128)S(1)}, f32[64,128]{1,0:T(8,128)S(1)}, u32[]{:S(2)}, u32[]{:S(2)}) collective-permute-start(f32[64,128]{1,0:T(8,128)S(1)} %get-tuple-element.63), channel_id=1, source_target_pairs={{0,8},{8,16},{16,24},{24,32},{32,40},{40,48},{48,56},{56,64},{64,7... | collective-permute-start | bytes 98312 | tf_op jit(solution)/shard_map/ppermute | solution.py:23
  75.9 3.1 %third.1 = (f32[4608,128]{1,0:T(8,128)S(1)}, f32[64,128]{1,0:T(8,128)S(1)}, f32[64,128]{1,0:T(8,128)S(1)}) custom-call(f32[4608,128]{1,0:T(8,128)S(1)} %get-tuple-element.54.cur_ref.prev_ref, f32[4608,128]{1,0:T(8,128)S(1)} %get-tuple-element.55.prev_ref, f32[4096,128]{1,0:T(8,128)S(1)} %get-tuple-element.56.pot_ref, ...), custom_call_target="tpu_custom_call" | custom-call | flops 4000000000 | bytes 8000000 | tf_op jit(solution)/shard_map/third/pallas_call | solution.py:331
  79.0 1.3 collective-permute-start.6
  80.3 4.0 %collective-permute-start.7 = (f32[64,128]{1,0:T(8,128)S(1)}, f32[64,128]{1,0:T(8,128)S(1)}, u32[]{:S(2)}, u32[]{:S(2)}) collective-permute-start(f32[64,128]{1,0:T(8,128)S(1)} %get-tuple-element.70), channel_id=1, source_target_pairs={{0,8},{8,16},{16,24},{24,32},{32,40},{40,48},{48,56},{56,64},{64,7... | collective-permute-start | bytes 98312 | tf_op jit(solution)/shard_map/ppermute | solution.py:23
  84.3 2.0 %fourth.1 = (f32[1152,128]{1,0:T(8,128)S(1)}, f32[1024,128]{1,0:T(8,128)S(1)}) custom-call(s32[3]{0:T(128)S(1)} %pad_add_fusion.scal, f32[4608,128]{1,0:T(8,128)S(1)} %get-tuple-element.61.cur_ref, f32[64,128]{1,0:T(8,128)S(1)} %collective-permute-done.4.pin_ref, f32[64,128]{1,0:T(8,128)S(1)} %collective-permute-done.5.bin_ref, ...), custom_call_target="tpu_custom_call" | custom-call | flops 2000000000 | bytes 4000000 | tf_op jit(solution)/shard_map/fourth/pallas_call | solution.py:331
  87.0 3.2 %collective-permute-start.8 = (f32[4,512,128]{2,1,0:T(8,128)S(1)}, f32[4,512,128]{2,1,0:T(8,128)S(1)}, u32[]{:S(2)}, u32[]{:S(2)}) collective-permute-start(f32[4,512,128]{2,1,0:T(8,128)S(1)} %get-tuple-element.75.send_ref), channel_id=1, source_target_pairs={{0,1},{1,0},{2,3},{3,2},{4,5},{5,4},{6,7},{7,6},{8,9},{9,8},{10,11... | collective-permute-start | bytes 3145736 | tf_op jit(solution)/shard_map/ppermute | solution.py:594
  90.2 1.5 %inside.1.part_ref = f32[128,128]{1,0:T(8,128)S(1)} custom-call(s32[3]{0:T(128)S(1)} %pad_add_fusion.scal, f32[4096,128]{1,0:T(8,128)S(1)} %bitcast.14, f32[4,512,128]{2,1,0:T(8,128)S(1)} %get-tuple-element.74.keep_ref, f32[4,512,128]{2,1,0:T(8,128)S(1)} %get-tuple-element.75.send_ref), custom_call_target="tpu_custom_call" | custom-call | flops 1000000000 | bytes 2000000 | tf_op jit(solution)/shard_map/inside/pallas_call | solution.py:331
  91.7 0.8 collective-permute-done.8.recv_ref
  92.5 1.8 %gram.1 = (f32[10,512,128]{2,1,0:T(8,128)S(1)}, f32[8,1,128]{2,1,0:T(1,128)S(1)}) custom-call(s32[3]{0:T(128)S(1)} %pad_add_fusion.scal, f32[2,512,128]{2,1,0:T(8,128)S(1)} %bitcast.17, f32[4,512,128]{2,1,0:T(8,128)S(1)} %get-tuple-element.74.keep_ref, f32[4,512,128]{2,1,0:T(8,128)S(1)} %collective-permute-done.8.recv_ref, f32[128,128]{1,0:T(8,128)S(1)} %inside.1.part_ref), custom_call_target="tpu_custom_call" | custom-call | flops 1000000000 | bytes 2000000 | tf_op jit(solution)/shard_map/gram/pallas_call | solution.py:331
  94.3 8.1 %all_to_all.15 = f32[8,1,128]{2,1,0:T(1,128)S(1)} all-to-all(f32[8,1,128]{2,1,0:T(1,128)S(1)} %get-tuple-element.76), channel_id=1, replica_groups=mesh['beam'=64,'trans'=8] {'trans'}, dimensions={0} | all-to-all | bytes 8192 | tf_op jit(solution)/shard_map/all_to_all | solution.py:604
  102.4 33.5 %all_to_all.16.gram_ref = f32[64,1,128]{2,1,0:T(1,128)S(1)} all-to-all(f32[64,1,128]{2,1,0:T(1,128)S(1)} %broadcast_in_dim.2), channel_id=1, replica_groups=mesh['beam'=64,'trans'=8] {'beam'}, dimensions={0} | all-to-all | bytes 65536 | tf_op jit(solution)/shard_map/all_to_all | solution.py:605
  135.9 4.9 %basis.1 = (f32[10,512,128]{2,1,0:T(8,128)}, f32[10,2,10]{2,1,0:T(2,128)}) custom-call(f32[64,1,128]{2,1,0:T(1,128)S(1)} %all_to_all.16.gram_ref, f32[10,512,128]{2,1,0:T(8,128)S(1)} %get-tuple-element.77.cols_ref), custom_call_target="tpu_custom_call" | custom-call | tf_op jit(solution)/shard_map/basis/pallas_call | solution.py:607
  (26 shorter events, 3.0 us)
Async XLA Ops:
  7.2 55.1 %all-gather.3.cloned.1.call-start = ((), (), s32[]{:S(2)}) async-start(), calls=%async_computation.3 | async-start | bytes 2359296 | tf_op jit(solution)/shard_map/all_gather | solution.py:521
  7.9 1.0 copy-start
  10.3 10.5 %copy-start.3 = (f32[65,65]{1,0:T(8,128)S(1)}, f32[65,65]{1,0:T(8,128)}, u32[]{:S(2)}) copy-start(f32[65,65]{1,0:T(8,128)} %ek_hbm.1) | copy-start | bytes 50704
  10.3 52.0 %all-to-all-start = ((f32[8,512,128]{2,1,0:T(8,128)}), f32[8,512,128]{2,1,0:T(8,128)S(1)}, u32[]{:S(2)}, u32[]{:S(2)}) async-start(f32[8,512,128]{2,1,0:T(8,128)} %copies.1), calls=%async_computation | async-start | bytes 4194304 | tf_op jit(solution)/shard_map/all_to_all | solution.py:531
  20.7 1.0 copy-start.1
  20.7 1.1 copy-start.2
  22.2 5.3 %collective-permute-start = (f32[16,128]{1,0:T(8,128)S(1)}, f32[16,128]{1,0:T(8,128)S(1)}, u32[]{:S(2)}, u32[]{:S(2)}) collective-permute-start(f32[16,128]{1,0:T(8,128)S(1)} %get-tuple-element.47), channel_id=1, source_target_pairs={{8,0},{16,8},{24,16},{32,24},{40,32},{48,40},{56,48},{64,56},{72,6... | collective-permute-start | bytes 24584 | tf_op jit(solution)/shard_map/ppermute | solution.py:23
  23.5 4.8 %collective-permute-start.1 = (f32[16,128]{1,0:T(8,128)S(1)}, f32[16,128]{1,0:T(8,128)S(1)}, u32[]{:S(2)}, u32[]{:S(2)}) collective-permute-start(f32[16,128]{1,0:T(8,128)S(1)} %get-tuple-element.48), channel_id=1, source_target_pairs={{0,8},{8,16},{16,24},{24,32},{32,40},{40,48},{48,56},{56,64},{64,7... | collective-permute-start | bytes 24584 | tf_op jit(solution)/shard_map/ppermute | solution.py:23
  28.3 5.8 %collective-permute-start.2 = (f32[16,128]{1,0:T(8,128)S(1)}, f32[16,128]{1,0:T(8,128)S(1)}, u32[]{:S(2)}, u32[]{:S(2)}) collective-permute-start(f32[16,128]{1,0:T(8,128)S(1)} %get-tuple-element.52), channel_id=1, source_target_pairs={{8,0},{16,8},{24,16},{32,24},{40,32},{48,40},{56,48},{64,56},{72,6... | collective-permute-start | bytes 24584 | tf_op jit(solution)/shard_map/ppermute | solution.py:23
  29.6 5.3 %collective-permute-start.3 = (f32[16,128]{1,0:T(8,128)S(1)}, f32[16,128]{1,0:T(8,128)S(1)}, u32[]{:S(2)}, u32[]{:S(2)}) collective-permute-start(f32[16,128]{1,0:T(8,128)S(1)} %get-tuple-element.53), channel_id=1, source_target_pairs={{0,8},{8,16},{16,24},{24,32},{32,40},{40,48},{48,56},{56,64},{64,7... | collective-permute-start | bytes 24584 | tf_op jit(solution)/shard_map/ppermute | solution.py:23
  70.6 8.4 %collective-permute-start.4 = (f32[64,128]{1,0:T(8,128)S(1)}, f32[64,128]{1,0:T(8,128)S(1)}, u32[]{:S(2)}, u32[]{:S(2)}) collective-permute-start(f32[64,128]{1,0:T(8,128)S(1)} %get-tuple-element.62), channel_id=1, source_target_pairs={{8,0},{16,8},{24,16},{32,24},{40,32},{48,40},{56,48},{64,56},{72,6... | collective-permute-start | bytes 98312 | tf_op jit(solution)/shard_map/ppermute | solution.py:23
  71.9 7.1 %collective-permute-start.5 = (f32[64,128]{1,0:T(8,128)S(1)}, f32[64,128]{1,0:T(8,128)S(1)}, u32[]{:S(2)}, u32[]{:S(2)}) collective-permute-start(f32[64,128]{1,0:T(8,128)S(1)} %get-tuple-element.63), channel_id=1, source_target_pairs={{0,8},{8,16},{16,24},{24,32},{32,40},{40,48},{48,56},{56,64},{64,7... | collective-permute-start | bytes 98312 | tf_op jit(solution)/shard_map/ppermute | solution.py:23
  79.0 7.3 %collective-permute-start.6 = (f32[64,128]{1,0:T(8,128)S(1)}, f32[64,128]{1,0:T(8,128)S(1)}, u32[]{:S(2)}, u32[]{:S(2)}) collective-permute-start(f32[64,128]{1,0:T(8,128)S(1)} %get-tuple-element.69), channel_id=1, source_target_pairs={{8,0},{16,8},{24,16},{32,24},{40,32},{48,40},{56,48},{64,56},{72,6... | collective-permute-start | bytes 98312 | tf_op jit(solution)/shard_map/ppermute | solution.py:23
  80.3 6.0 %collective-permute-start.7 = (f32[64,128]{1,0:T(8,128)S(1)}, f32[64,128]{1,0:T(8,128)S(1)}, u32[]{:S(2)}, u32[]{:S(2)}) collective-permute-start(f32[64,128]{1,0:T(8,128)S(1)} %get-tuple-element.70), channel_id=1, source_target_pairs={{0,8},{8,16},{16,24},{24,32},{32,40},{40,48},{48,56},{56,64},{64,7... | collective-permute-start | bytes 98312 | tf_op jit(solution)/shard_map/ppermute | solution.py:23
  87.0 5.5 %collective-permute-start.8 = (f32[4,512,128]{2,1,0:T(8,128)S(1)}, f32[4,512,128]{2,1,0:T(8,128)S(1)}, u32[]{:S(2)}, u32[]{:S(2)}) collective-permute-start(f32[4,512,128]{2,1,0:T(8,128)S(1)} %get-tuple-element.75.send_ref), channel_id=1, source_target_pairs={{0,1},{1,0},{2,3},{3,2},{4,5},{5,4},{6,7},{7,6},{8,9},{9,8},{10,11... | collective-permute-start | bytes 3145736 | tf_op jit(solution)/shard_map/ppermute | solution.py:594
Sparse Core Ops, SparseCore 0:
  10.1 47.1 all-gather.2

commit v8 on v7

--- a/solution.py
+++ b/solution.py
@@ -597,12 +597,12 @@
         scal=scal, cost=1,
     )
     cols, gram = call(
-        "gram", gram_body, [in_vmem(ncol, size, width), in_vmem(trans, 1, width)],
+        "gram", gram_body, [in_vmem(ncol, size, width), in_vmem(lax.axis_size("beam"), 1, width)],
         flat, keep, recv, part, scal=scal, scratch=[in_vmem(128, width)], cost=1,
     )
     beam = lax.axis_size("beam")
-    gram = jnp.sum(lax.all_to_all(gram, "trans", 0, 0, tiled=True), axis=0, keepdims=True)
-    gram = lax.all_to_all(jnp.broadcast_to(gram, (beam, 1, width)), "beam", 0, 0, tiled=True)
+    gram = jnp.sum(lax.all_to_all(gram, "beam", 0, 0, tiled=True), axis=0, keepdims=True)
+    gram = lax.all_to_all(jnp.broadcast_to(gram, (trans, 1, width)), "trans", 0, 0, tiled=True)
     cells = float(nx * (width // 2) * nz * beam)
     basis, factor = pl.pallas_call(
         functools.partial(basis_body, cells, rows),

time: 148 us -> 150 us (1.014)
  blocking collectives: 68.9 us -> 70.4 us
where the time goes in v8:
time: 150 us; the launch traced here: 149 us
  blocking collectives  70.4 us (47%)
  starting transfers between devices  35.3 us (24%)
  Pallas kernels  24.7 us (16%)
  between operations  14.2 us (9%)
  waiting for transfers between devices  2.99 us (2%)
    all_to_all x1, blocking collectives, shards(): lax.all_to_all(gram, 'beam', 0, 0, tiled=True)  33.5 us
    all_gather x1, blocking collectives, shards(): planes = lax.all_gather(planes, 'trans')  27.4 us
    ppermute x8, starting transfers between devices, passed(): lax.ppermute(x, 'beam', [(i, i + by) for i in range(peers) if 0 <= i + by...  21.7 us
    pallas_call x9, Pallas kernels, call(): pl.pallas_call(body, out_shape=outs, in_specs=specs, out_specs=[vm()] * l...  17.8 us
    all_to_all x1, starting transfers between devices, shards(): lax.all_to_all(sent, 'trans', 0, 0, tiled=True).reshape(nx * nz, width)  10.4 us
    all_to_all x1, blocking collectives, shards(): lax.all_to_all(jnp.broadcast_to(gram, (trans, 1, width)), 'trans', 0, 0,...  9.5 us
    pallas_call x1, Pallas kernels, shards(): pl.pallas_call(functools.partial(basis_body, cells, rows), out_shape=[jax...  4.84 us
    ppermute x1, starting transfers between devices, shards(): recv = lax.ppermute(send, 'trans', [(i, i ^ 1) for i in range(trans)])  3.2 us
  transfers between devices with their start and end apart: 11, of which 3 were waited for; matrix products, arithmetic and copies ran while one was open for 0% of the time, Pallas kernels for 6%

profile of v8, /device:TPU:1, one launch (start us, length us, event | category | flops | bytes accessed | tf_op | source)
XLA Modules:
  0.0 149.1 jit_solution(2824646879202302429)
XLA Ops:
  7.9 1.0 copy-done
  8.9 1.3 copies.1
  10.3 10.4 %all-to-all-start = ((f32[8,512,128]{2,1,0:T(8,128)}), f32[8,512,128]{2,1,0:T(8,128)S(1)}, u32[]{:S(2)}, u32[]{:S(2)}) async-start(f32[8,512,128]{2,1,0:T(8,128)} %copies.1), calls=%async_computation | async-start | bytes 4194304 | tf_op jit(solution)/shard_map/all_to_all | solution.py:531
  22.2 1.3 collective-permute-start
  23.5 4.0 %collective-permute-start.1 = (f32[16,128]{1,0:T(8,128)S(1)}, f32[16,128]{1,0:T(8,128)S(1)}, u32[]{:S(2)}, u32[]{:S(2)}) collective-permute-start(f32[16,128]{1,0:T(8,128)S(1)} %get-tuple-element.48), channel_id=1, source_target_pairs={{0,8},{8,16},{16,24},{24,32},{32,40},{40,48},{48,56},{56,64},{64,7... | collective-permute-start | bytes 24584 | tf_op jit(solution)/shard_map/ppermute | solution.py:23
  27.5 0.8 collective-permute-done.1.bin_ref
  28.3 1.3 collective-permute-start.2
  29.6 4.5 %collective-permute-start.3 = (f32[16,128]{1,0:T(8,128)S(1)}, f32[16,128]{1,0:T(8,128)S(1)}, u32[]{:S(2)}, u32[]{:S(2)}) collective-permute-start(f32[16,128]{1,0:T(8,128)S(1)} %get-tuple-element.53), channel_id=1, source_target_pairs={{0,8},{8,16},{16,24},{24,32},{32,40},{40,48},{48,56},{56,64},{64,7... | collective-permute-start | bytes 24584 | tf_op jit(solution)/shard_map/ppermute | solution.py:23
  34.2 0.8 collective-permute-done.3
  34.9 27.4 %all-gather = f32[32,16,128]{2,1,0:T(8,128)S(1)} all-gather(f32[4,16,128]{2,1,0:T(8,128)S(1)} %pad_maximum_fusion), channel_id=2, replica_groups=mesh['beam'=64,'trans'=8] {'trans'}, dimensions={0}, use_global_device_ids=true | all-gather | bytes 294912 | tf_op jit(solution)/shard_map/all_gather | solution.py:556
  62.3 8.3 %pair.1 = (f32[4608,128]{1,0:T(8,128)S(1)}, f32[4608,128]{1,0:T(8,128)S(1)}, f32[64,128]{1,0:T(8,128)S(1)}, f32[64,128]{1,0:T(8,128)S(1)}, f32[1024,128]{1,0:T(8...) custom-call(s32[3]{0:T(128)S(1)} %pad_add_fusion.scal, ...), custom_call_target="tpu_custom_call" | custom-call | flops 8000000000 | bytes 16000000 | tf_op jit(solution)/shard_map/pair/pallas_call | solution.py:331
  70.6 1.3 collective-permute-start.4
  71.9 4.0 %collective-permute-start.5 = (f32[64,128]{1,0:T(8,128)S(1)}, f32[64,128]{1,0:T(8,128)S(1)}, u32[]{:S(2)}, u32[]{:S(2)}) collective-permute-start(f32[64,128]{1,0:T(8,128)S(1)} %get-tuple-element.63), channel_id=1, source_target_pairs={{0,8},{8,16},{16,24},{24,32},{32,40},{40,48},{48,56},{56,64},{64,7... | collective-permute-start | bytes 98312 | tf_op jit(solution)/shard_map/ppermute | solution.py:23
  75.9 3.1 %third.1 = (f32[4608,128]{1,0:T(8,128)S(1)}, f32[64,128]{1,0:T(8,128)S(1)}, f32[64,128]{1,0:T(8,128)S(1)}) custom-call(f32[4608,128]{1,0:T(8,128)S(1)} %get-tuple-element.54.cur_ref.prev_ref, f32[4608,128]{1,0:T(8,128)S(1)} %get-tuple-element.55.prev_ref, f32[4096,128]{1,0:T(8,128)S(1)} %get-tuple-element.56.pot_ref, ...), custom_call_target="tpu_custom_call" | custom-call | flops 4000000000 | bytes 8000000 | tf_op jit(solution)/shard_map/third/pallas_call | solution.py:331
  79.0 1.3 collective-permute-start.6
  80.3 4.0 %collective-permute-start.7 = (f32[64,128]{1,0:T(8,128)S(1)}, f32[64,128]{1,0:T(8,128)S(1)}, u32[]{:S(2)}, u32[]{:S(2)}) collective-permute-start(f32[64,128]{1,0:T(8,128)S(1)} %get-tuple-element.70), channel_id=1, source_target_pairs={{0,8},{8,16},{16,24},{24,32},{32,40},{40,48},{48,56},{56,64},{64,7... | collective-permute-start | bytes 98312 | tf_op jit(solution)/shard_map/ppermute | solution.py:23
  84.3 2.0 %fourth.1 = (f32[1152,128]{1,0:T(8,128)S(1)}, f32[1024,128]{1,0:T(8,128)S(1)}) custom-call(s32[3]{0:T(128)S(1)} %pad_add_fusion.scal, f32[4608,128]{1,0:T(8,128)S(1)} %get-tuple-element.61.cur_ref, f32[64,128]{1,0:T(8,128)S(1)} %collective-permute-done.4.pin_ref, f32[64,128]{1,0:T(8,128)S(1)} %collective-permute-done.5.bin_ref, ...), custom_call_target="tpu_custom_call" | custom-call | flops 2000000000 | bytes 4000000 | tf_op jit(solution)/shard_map/fourth/pallas_call | solution.py:331
  87.0 3.2 %collective-permute-start.8 = (f32[4,512,128]{2,1,0:T(8,128)S(1)}, f32[4,512,128]{2,1,0:T(8,128)S(1)}, u32[]{:S(2)}, u32[]{:S(2)}) collective-permute-start(f32[4,512,128]{2,1,0:T(8,128)S(1)} %get-tuple-element.75.send_ref), channel_id=1, source_target_pairs={{0,1},{1,0},{2,3},{3,2},{4,5},{5,4},{6,7},{7,6},{8,9},{9,8},{10,11... | collective-permute-start | bytes 3145736 | tf_op jit(solution)/shard_map/ppermute | solution.py:594
  90.2 1.5 %inside.1.part_ref = f32[128,128]{1,0:T(8,128)S(1)} custom-call(s32[3]{0:T(128)S(1)} %pad_add_fusion.scal, f32[4096,128]{1,0:T(8,128)S(1)} %bitcast.14, f32[4,512,128]{2,1,0:T(8,128)S(1)} %get-tuple-element.74.keep_ref, f32[4,512,128]{2,1,0:T(8,128)S(1)} %get-tuple-element.75.send_ref), custom_call_target="tpu_custom_call" | custom-call | flops 1000000000 | bytes 2000000 | tf_op jit(solution)/shard_map/inside/pallas_call | solution.py:331
  91.7 0.8 collective-permute-done.8.recv_ref
  92.5 1.8 %gram.1 = (f32[10,512,128]{2,1,0:T(8,128)S(1)}, f32[64,1,128]{2,1,0:T(1,128)S(1)}) custom-call(s32[3]{0:T(128)S(1)} %pad_add_fusion.scal, f32[2,512,128]{2,1,0:T(8,128)S(1)} %bitcast.17, f32[4,512,128]{2,1,0:T(8,128)S(1)} %get-tuple-element.74.keep_ref, f32[4,512,128]{2,1,0:T(8,128)S(1)} %collective-permute-done.8.recv_ref, f32[128,128]{1,0:T(8,128)S(1)} %inside.1.part_ref), custom_call_target="tpu_custom_call" | custom-call | flops 1000000000 | bytes 2000000 | tf_op jit(solution)/shard_map/gram/pallas_call | solution.py:331
  94.3 33.5 %all_to_all.15 = f32[64,1,128]{2,1,0:T(1,128)S(1)} all-to-all(f32[64,1,128]{2,1,0:T(1,128)S(1)} %get-tuple-element.76), channel_id=1, replica_groups=mesh['beam'=64,'trans'=8] {'beam'}, dimensions={0} | all-to-all | bytes 65536 | tf_op jit(solution)/shard_map/all_to_all | solution.py:604
  127.9 9.5 %all_to_all.16.gram_ref = f32[8,1,128]{2,1,0:T(1,128)S(1)} all-to-all(f32[8,1,128]{2,1,0:T(1,128)S(1)} %broadcast_in_dim.2), channel_id=1, replica_groups=mesh['beam'=64,'trans'=8] {'trans'}, dimensions={0} | all-to-all | bytes 8192 | tf_op jit(solution)/shard_map/all_to_all | solution.py:605
  137.4 4.8 %basis.1 = (f32[10,512,128]{2,1,0:T(8,128)}, f32[10,2,10]{2,1,0:T(2,128)}) custom-call(f32[8,1,128]{2,1,0:T(1,128)S(1)} %all_to_all.16.gram_ref, f32[10,512,128]{2,1,0:T(8,128)S(1)} %get-tuple-element.77.cols_ref), custom_call_target="tpu_custom_call" | custom-call | tf_op jit(solution)/shard_map/basis/pallas_call | solution.py:607
  (26 shorter events, 3.1 us)
Async XLA Ops:
  7.2 55.1 %all-gather.3.cloned.1.call-start = ((), (), s32[]{:S(2)}) async-start(), calls=%async_computation.3 | async-start | bytes 2359296 | tf_op jit(solution)/shard_map/all_gather | solution.py:521
  7.9 1.0 copy-start
  10.3 10.5 %copy-start.3 = (f32[65,65]{1,0:T(8,128)S(1)}, f32[65,65]{1,0:T(8,128)}, u32[]{:S(2)}) copy-start(f32[65,65]{1,0:T(8,128)} %ek_hbm.1) | copy-start | bytes 50704
  10.3 52.0 %all-to-all-start = ((f32[8,512,128]{2,1,0:T(8,128)}), f32[8,512,128]{2,1,0:T(8,128)S(1)}, u32[]{:S(2)}, u32[]{:S(2)}) async-start(f32[8,512,128]{2,1,0:T(8,128)} %copies.1), calls=%async_computation | async-start | bytes 4194304 | tf_op jit(solution)/shard_map/all_to_all | solution.py:531
  20.7 1.0 copy-start.1
  20.7 1.1 copy-start.2
  22.2 5.3 %collective-permute-start = (f32[16,128]{1,0:T(8,128)S(1)}, f32[16,128]{1,0:T(8,128)S(1)}, u32[]{:S(2)}, u32[]{:S(2)}) collective-permute-start(f32[16,128]{1,0:T(8,128)S(1)} %get-tuple-element.47), channel_id=1, source_target_pairs={{8,0},{16,8},{24,16},{32,24},{40,32},{48,40},{56,48},{64,56},{72,6... | collective-permute-start | bytes 24584 | tf_op jit(solution)/shard_map/ppermute | solution.py:23
  23.5 4.8 %collective-permute-start.1 = (f32[16,128]{1,0:T(8,128)S(1)}, f32[16,128]{1,0:T(8,128)S(1)}, u32[]{:S(2)}, u32[]{:S(2)}) collective-permute-start(f32[16,128]{1,0:T(8,128)S(1)} %get-tuple-element.48), channel_id=1, source_target_pairs={{0,8},{8,16},{16,24},{24,32},{32,40},{40,48},{48,56},{56,64},{64,7... | collective-permute-start | bytes 24584 | tf_op jit(solution)/shard_map/ppermute | solution.py:23
  28.3 5.8 %collective-permute-start.2 = (f32[16,128]{1,0:T(8,128)S(1)}, f32[16,128]{1,0:T(8,128)S(1)}, u32[]{:S(2)}, u32[]{:S(2)}) collective-permute-start(f32[16,128]{1,0:T(8,128)S(1)} %get-tuple-element.52), channel_id=1, source_target_pairs={{8,0},{16,8},{24,16},{32,24},{40,32},{48,40},{56,48},{64,56},{72,6... | collective-permute-start | bytes 24584 | tf_op jit(solution)/shard_map/ppermute | solution.py:23
  29.6 5.3 %collective-permute-start.3 = (f32[16,128]{1,0:T(8,128)S(1)}, f32[16,128]{1,0:T(8,128)S(1)}, u32[]{:S(2)}, u32[]{:S(2)}) collective-permute-start(f32[16,128]{1,0:T(8,128)S(1)} %get-tuple-element.53), channel_id=1, source_target_pairs={{0,8},{8,16},{16,24},{24,32},{32,40},{40,48},{48,56},{56,64},{64,7... | collective-permute-start | bytes 24584 | tf_op jit(solution)/shard_map/ppermute | solution.py:23
  70.6 8.4 %collective-permute-start.4 = (f32[64,128]{1,0:T(8,128)S(1)}, f32[64,128]{1,0:T(8,128)S(1)}, u32[]{:S(2)}, u32[]{:S(2)}) collective-permute-start(f32[64,128]{1,0:T(8,128)S(1)} %get-tuple-element.62), channel_id=1, source_target_pairs={{8,0},{16,8},{24,16},{32,24},{40,32},{48,40},{56,48},{64,56},{72,6... | collective-permute-start | bytes 98312 | tf_op jit(solution)/shard_map/ppermute | solution.py:23
  71.9 7.1 %collective-permute-start.5 = (f32[64,128]{1,0:T(8,128)S(1)}, f32[64,128]{1,0:T(8,128)S(1)}, u32[]{:S(2)}, u32[]{:S(2)}) collective-permute-start(f32[64,128]{1,0:T(8,128)S(1)} %get-tuple-element.63), channel_id=1, source_target_pairs={{0,8},{8,16},{16,24},{24,32},{32,40},{40,48},{48,56},{56,64},{64,7... | collective-permute-start | bytes 98312 | tf_op jit(solution)/shard_map/ppermute | solution.py:23
  79.0 7.3 %collective-permute-start.6 = (f32[64,128]{1,0:T(8,128)S(1)}, f32[64,128]{1,0:T(8,128)S(1)}, u32[]{:S(2)}, u32[]{:S(2)}) collective-permute-start(f32[64,128]{1,0:T(8,128)S(1)} %get-tuple-element.69), channel_id=1, source_target_pairs={{8,0},{16,8},{24,16},{32,24},{40,32},{48,40},{56,48},{64,56},{72,6... | collective-permute-start | bytes 98312 | tf_op jit(solution)/shard_map/ppermute | solution.py:23
  80.3 6.0 %collective-permute-start.7 = (f32[64,128]{1,0:T(8,128)S(1)}, f32[64,128]{1,0:T(8,128)S(1)}, u32[]{:S(2)}, u32[]{:S(2)}) collective-permute-start(f32[64,128]{1,0:T(8,128)S(1)} %get-tuple-element.70), channel_id=1, source_target_pairs={{0,8},{8,16},{16,24},{24,32},{32,40},{40,48},{48,56},{56,64},{64,7... | collective-permute-start | bytes 98312 | tf_op jit(solution)/shard_map/ppermute | solution.py:23
  87.0 5.5 %collective-permute-start.8 = (f32[4,512,128]{2,1,0:T(8,128)S(1)}, f32[4,512,128]{2,1,0:T(8,128)S(1)}, u32[]{:S(2)}, u32[]{:S(2)}) collective-permute-start(f32[4,512,128]{2,1,0:T(8,128)S(1)} %get-tuple-element.75.send_ref), channel_id=1, source_target_pairs={{0,1},{1,0},{2,3},{3,2},{4,5},{5,4},{6,7},{7,6},{8,9},{9,8},{10,11... | collective-permute-start | bytes 3145736 | tf_op jit(solution)/shard_map/ppermute | solution.py:594
Sparse Core Ops, SparseCore 0:
  10.1 47.1 all-gather.2
